TPU v7x, 256 devices: a whole 4x4x8 slice. The times are simulated.
256 devices in a mesh: dp: 32 (over x, z), expert: 8 (over y, core).
Axes of the slice: x: 4, y: 4, z: 8, core: 2. Of those that a mesh axis runs over, the one named last changes fastest.
Arguments:
- teacher_in: bfloat16 [256, 6144], P('dp'), may hold values from -6 to 6
- route_ids: int32 [256, 2], replicated, may hold values from 0 to 7, all different within a row; in each aligned block of 8 rows (0 to 7, 8 to 15, ...) at most 4 rows name the same one
- router: bfloat16 [6144, 8], replicated, may hold values from -0.078125 to 0.078125
- w_gate: bfloat16 [8, 6144, 8192], P('expert', None, 'dp'), may hold values from -0.078125 to 0.078125
- w_up: bfloat16 [8, 6144, 8192], P('expert', None, 'dp'), may hold values from -0.078125 to 0.078125
- w_down: bfloat16 [8, 8192, 6144], P('expert', 'dp'), may hold values from -0.125 to 0.125
- projection: bfloat16 [6144, 4096], P('dp'), may hold values from -0.078125 to 0.078125
- student_in: bfloat16 [256, 4096], P('dp', 'expert'), may hold values from -6 to 6
- s_gate: bfloat16 [4096, 7168], P('expert', 'dp'), may hold values from -0.09375 to 0.09375
- s_up: bfloat16 [4096, 7168], P('expert', 'dp'), may hold values from -0.09375 to 0.09375
- s_down: bfloat16 [7168, 4096], P('dp', 'expert'), may hold values from -0.0625 to 0.0625
Outputs:
- grad_gate: bfloat16 [4096, 7168], P('expert', 'dp')
- grad_up: bfloat16 [4096, 7168], P('expert', 'dp')
- grad_down: bfloat16 [7168, 4096], P('dp', 'expert')
- mismatch: float32 [256, 4096], P('dp', 'expert')
Inputs may be any that keep to these rules, and one draw needn't show every extreme that they name: `route_ids`: each row names two different experts. In every block of 8 rows (rows b * 8 to b * 8 + 7) no expert is named by more than 4 rows, and in some block an expert is named by exactly 4 rows.
All inputs are finite; a program needn't handle non-finite values.
Results may differ from a plain program's by a relative error of at most 0.011.
Values may be sent and summed in bfloat16 or wider, within the bound.
No kernel may reach another device: no remote copies, remote signals or barrier semaphores. Data moves between devices by JAX's collectives and lax.ppermute only.
A program may use at most 64 MiB of HBM per device.

v0:
```python
import math

import jax
import jax.numpy as jnp
from jax import lax
from jax.sharding import PartitionSpec as P


def slot_numbers(block_ids, experts):
    count = block_ids.shape[0]
    onehot = (block_ids[:, :, None] == jnp.arange(experts, dtype=jnp.int32)[None, None, :]).astype(
        jnp.int32
    )
    flat = onehot.reshape(count * 2, experts)
    before = jnp.cumsum(flat, axis=0) - flat
    return jnp.sum(before * flat, axis=1).reshape(count, 2)


def slot_matrix(block_ids, block_slots, expert_index, capacity):
    slot_range = jnp.arange(capacity, dtype=jnp.int32)
    match = (block_ids == expert_index)[None, :, :] & (
        block_slots[None, :, :] == slot_range[:, None, None]
    )
    return jnp.sum(match.astype(jnp.int32), axis=2).astype(jnp.bfloat16)


def expert_hidden(expert_rows, gate_matrix, up_matrix):
    gate_part = jnp.dot(expert_rows, gate_matrix, preferred_element_type=jnp.float32)
    up_part = jnp.dot(expert_rows, up_matrix, preferred_element_type=jnp.float32)
    return (gate_part * jax.nn.sigmoid(gate_part) * up_part).astype(jnp.bfloat16)


def dp_rows(values):
    return lax.all_gather(values, "dp", axis=0, tiled=True)


def dp_sums(term_fn, share):
    return lax.psum_scatter(
        term_fn(jnp.int32(0), share * lax.axis_size("dp")), "dp", scatter_dimension=0, tiled=True
    )


def expert_totals(values):
    return lax.psum(values, "expert")


def pair_backward(d_hidden, pair_sums, width):
    gate_s = pair_sums[:, :width]
    up_s = pair_sums[:, width:]
    sigma = jax.nn.sigmoid(gate_s)
    active = gate_s * sigma
    d_gate = (d_hidden * up_s * sigma * (1.0 + gate_s * (1.0 - sigma))).astype(jnp.bfloat16)
    d_up = (d_hidden * active).astype(jnp.bfloat16)
    return jnp.concatenate([d_gate, d_up], axis=1)


def pair_forward(pair_sums, width):
    gate_s = pair_sums[:, :width]
    up_s = pair_sums[:, width:]
    return (gate_s * jax.nn.sigmoid(gate_s) * up_s).astype(jnp.bfloat16)


def body(
    teacher_in,
    route_ids,
    router,
    w_gate,
    w_up,
    w_down,
    projection,
    student_in,
    s_gate,
    s_up,
    s_down,
):
    blocks = lax.axis_size("dp")
    experts = router.shape[1]
    tok_dp = teacher_in.shape[0]
    capacity = 4 * tok_dp // experts
    expert_index = lax.axis_index("expert")
    block_index = lax.axis_index("dp")
    gate_matrix = w_gate[0]
    up_matrix = w_up[0]
    down_matrix = w_down[0]
    sd_dev = student_in.shape[1]
    sff_dev = s_gate.shape[1]
    own_ids = lax.dynamic_slice_in_dim(route_ids, block_index * tok_dp, tok_dp, 0)
    own_slots = slot_numbers(own_ids, experts)
    logits = jnp.dot(teacher_in, router, preferred_element_type=jnp.float32)
    picked = jnp.take_along_axis(logits, own_ids, axis=1)
    gates = jax.nn.sigmoid(picked - picked[:, ::-1])
    every_token = lax.all_gather(teacher_in, "dp", axis=0, tiled=True)
    id_blocks = route_ids.reshape(blocks, tok_dp, 2)
    slot_blocks = jax.vmap(lambda block_ids: slot_numbers(block_ids, experts))(id_blocks)
    chosen_all = jax.vmap(
        lambda block_ids, block_slots: slot_matrix(block_ids, block_slots, expert_index, capacity)
    )(id_blocks, slot_blocks)
    gathered = jnp.einsum(
        "bct,btd->bcd",
        chosen_all,
        every_token.reshape(blocks, tok_dp, -1),
        preferred_element_type=jnp.float32,
    )
    hidden = expert_hidden(
        gathered.astype(jnp.bfloat16).reshape(blocks * capacity, -1), gate_matrix, up_matrix
    )

    def feature_term(start, count):
        return lax.dot_general(
            down_matrix, hidden, (((0,), (1,)), ((), ())), preferred_element_type=jnp.float32
        )

    summed = dp_sums(feature_term, projection.shape[0]).astype(jnp.bfloat16)

    def slot_term(start, count):
        return lax.dot_general(
            summed, projection, (((0,), (0,)), ((), ())), preferred_element_type=jnp.float32
        )

    projected = dp_sums(slot_term, capacity).astype(jnp.bfloat16)
    returned = lax.all_to_all(
        projected.reshape(capacity, experts, sd_dev),
        "expert",
        split_axis=1,
        concat_axis=1,
        tiled=True,
    )
    slot_hit = (
        own_slots[:, :, None] == jnp.arange(capacity, dtype=jnp.int32)[None, None, :]
    ).astype(jnp.float32)
    expert_hit = (
        own_ids[:, :, None] == jnp.arange(experts, dtype=jnp.int32)[None, None, :]
    ).astype(jnp.float32)
    weights = jnp.einsum(
        "tk,tkc,tkx->tcx", gates, slot_hit, expert_hit, precision=lax.Precision.HIGHEST
    )
    target = jnp.dot(
        weights.reshape(tok_dp, capacity * experts),
        returned.reshape(capacity * experts, sd_dev).astype(jnp.float32),
        precision=lax.Precision.HIGHEST,
    )
    student_all = dp_rows(student_in)
    tokens = student_all.shape[0]
    both_weights = jnp.concatenate([s_gate, s_up], axis=1)
    pair_sums = expert_totals(
        jnp.dot(student_all, both_weights, preferred_element_type=jnp.float32)
    )
    hidden_s = pair_forward(pair_sums, sff_dev)

    def out_term(start, count):
        return jnp.dot(hidden_s, s_down, preferred_element_type=jnp.float32)

    student_out = dp_sums(out_term, tok_dp)
    mismatch = student_in.astype(jnp.float32) + student_out - target
    cotangent = (mismatch * (1.0 / math.sqrt(tokens))).astype(jnp.bfloat16)
    cotangent_all = dp_rows(cotangent)
    grad_down = lax.dot_general(
        hidden_s, cotangent_all, (((0,), (0,)), ((), ())), preferred_element_type=jnp.float32
    ).astype(jnp.bfloat16)
    d_hidden = expert_totals(
        lax.dot_general(
            cotangent_all, s_down, (((1,), (1,)), ((), ())), preferred_element_type=jnp.float32
        )
    )
    d_pair = pair_backward(d_hidden, pair_sums, sff_dev)
    grads = lax.dot_general(
        student_all, d_pair, (((0,), (0,)), ((), ())), preferred_element_type=jnp.float32
    )
    grad_gate = grads[:, :sff_dev].astype(jnp.bfloat16)
    grad_up = grads[:, sff_dev:].astype(jnp.bfloat16)
    return (grad_gate, grad_up, grad_down, mismatch)


def solution(mesh):
    return jax.shard_map(
        body,
        mesh=mesh,
        in_specs=(
            P("dp", None),
            P(),
            P(),
            P("expert", None, "dp"),
            P("expert", None, "dp"),
            P("expert", "dp", None),
            P("dp", None),
            P("dp", "expert"),
            P("expert", "dp"),
            P("expert", "dp"),
            P("dp", "expert"),
        ),
        out_specs=(P("expert", "dp"), P("expert", "dp"), P("dp", "expert"), P("dp", "expert")),
        check_vma=False,
    )
```

profile of v0, /device:TPU:1, one launch (start us, length us, event | category | flops | bytes accessed | tf_op | source)
XLA Modules:
  0.0 669.1 jit_solution(17760271130415425715)
XLA Ops:
  8.0 0.0 copy-start
  8.0 0.0 all-gather.2.cloned.1.call-start
  8.1 0.7 all-gather.2.cloned.1.call-update
  8.7 0.0 all-reduce.5.cloned.1.call-start
  8.8 41.7 %all_gather.9 = bf16[256,512]{1,0:T(8,128)(2,1)S(1)} all-gather(bf16[8,512]{1,0:T(8,128)(2,1)} %param.18), channel_id=1, replica_groups=mesh['dp'=32,'expert'=8] {'dp'}, dimensions={0}, use_global_device_ids=true | all-gather | bytes 270336 | tf_op jit(solution)/shard_map/all_gather | solution.py:34
  50.5 0.7 copy-done.1
  51.3 2.1 convolution_bitcast_fusion.1
  53.4 0.0 all-reduce.5.cloned.1.call-update
  53.4 0.0 reduce-scatter.7.cloned.1.call-start
  53.5 0.8 copy.36
  54.3 0.1 eq.102
  54.4 0.1 copy.41
  54.5 0.6 fusion.49
  55.1 0.7 broadcast_compare_fusion
  55.7 0.1 eq.101
  55.8 0.1 copy.39
  56.0 0.1 copy.43
  56.1 36.1 %all-gather.2.cloned.1.call-done = bf16[256,6144]{1,0:T(8,128)(2,1)} async-done(((bf16[8,6144]{1,0:T(8,128)(2,1)}), bf16[256,6144]{1,0:T(8,128)(2,1)}) %all-gather.2.cloned.1.call-update) | async-done | bytes 3145744 | tf_op jit(solution)/shard_map/all_gather | solution.py:92
  92.1 4.0 convolution_convert_fusion
  96.1 3.7 reshape.49
  99.8 2.9 fusion.3
  102.8 0.0 copy-done
  102.8 5.9 convolution_bitcast_fusion
  108.7 3.5 copy.46
  112.2 0.0 reduce-scatter.7.cloned.1.call-update
  112.3 0.0 copy-start.2
  112.3 0.0 reduce-scatter.5.cloned.1.call-start
  112.4 0.1 copy.37
  112.5 0.1 copy.38
  112.5 0.1 reshape.51
  112.6 1.1 fusion.51
  113.7 0.7 gather_fusion
  114.4 0.1 reshape.54
  114.5 0.1 eq.88
  114.6 0.1 rev.3
  114.6 0.1 fusion.39
  114.7 0.2 select_reduce_fusion
  114.9 0.1 eq.92
  115.0 0.6 dynamic-slice
  116.3 10.5 %all-reduce.5.cloned.1.call-done = f32[256,448]{0,1:T(8,128)} async-done(((f32[256,448]{0,1:T(8,128)}), f32[256,448]{0,1:T(8,128)}) %all-reduce.5.cloned.1.call-update) | async-done | bytes 458768 | tf_op jit(solution)/shard_map/psum | solution.py:44
  126.8 1.1 multiply_convert_fusion.2
  127.9 1.0 fusion.50
  129.0 0.0 reduce-scatter.5.cloned.1.call-update
  129.0 196.8 %reduce-scatter.7.cloned.1.call-done = f32[192,128]{1,0:T(8,128)} async-done(((f32[6144,128]{1,0:T(8,128)}), f32[192,128]{1,0:T(8,128)}) %reduce-scatter.7.cloned.1.call-update) | async-done | bytes 98320
  325.8 1.0 copy.47
  326.8 0.0 copy-start.3
  326.8 3.2 fusion.53
  330.0 141.1 %all-reduce.8 = bf16[128,4096]{1,0:T(8,128)(2,1)} all-reduce(f32[128,4096]{1,0:T(8,128)} %fusion.53), channel_id=4, replica_groups=mesh['dp'=32,'expert'=8] {'dp'}, use_global_device_ids=true, to_apply=%region_8.9.clone | all-reduce | flops 524288 | bytes 3145728
  471.1 1.5 dynamic-slice_convert_fusion
  472.6 35.8 %all-to-all-start = ((bf16[4,8,512]{2,0,1:T(4,128)(2,1)}), bf16[4,8,512]{2,0,1:T(4,128)(2,1)S(1)}, u32[]{:S(2)}, u32[]{:S(2)}) async-start(bf16[4,8,512]{2,0,1:T(4,128)(2,1)} %bitcast.8), calls=%async_computation.1 | async-start | bytes 65536 | tf_op jit(solution)/shard_map/all_to_all | solution.py:121
  508.4 0.0 all-reduce.7.cloned.1.call-start
  508.4 0.3 fusion.35
  508.7 0.1 copy.45
  508.8 32.2 %reduce-scatter.5.cloned.1.call-done = f32[8,512]{1,0:T(8,128)} async-done(((f32[256,512]{1,0:T(8,128)}), f32[8,512]{1,0:T(8,128)}) %reduce-scatter.5.cloned.1.call-update) | async-done | bytes 16400 | tf_op jit(solution)/shard_map/reduce_scatter | solution.py:38
  540.9 0.0 all-to-all-done
  540.9 1.5 multiply_convert_fusion.3
  542.5 35.5 %all_gather.11 = bf16[256,512]{1,0:T(8,128)(2,1)S(1)} all-gather(bf16[8,512]{1,0:T(8,128)(2,1)S(1)} %get-tuple-element.10), channel_id=1, replica_groups=mesh['dp'=32,'expert'=8] {'dp'}, dimensions={0}, use_global_device_ids=true | all-gather | bytes 270336 | tf_op jit(solution)/shard_map/all_gather | solution.py:34
  578.0 1.9 fusion.52
  579.9 0.0 all-reduce.7.cloned.1.call-update
  579.9 0.9 convolution_convert_fusion.2
  580.8 77.8 %all-reduce.7.cloned.1.call-done = f32[256,224]{0,1:T(8,128)} async-done(((f32[256,224]{0,1:T(8,128)}), f32[256,224]{0,1:T(8,128)}) %all-reduce.7.cloned.1.call-update) | async-done | bytes 229392 | tf_op jit(solution)/shard_map/psum | solution.py:44
  658.7 1.3 multiply_convert_fusion.1
  660.0 1.2 fusion.6
  661.2 0.8 fusion.48
  (13 shorter events, 0.1 us)
Async XLA Ops:
  8.0 94.8 %copy-start = (bf16[1,256,6144]{2,1,0:T(8,128)(2,1)S(1)}, bf16[1,256,6144]{2,1,0:T(8,128)(2,1)}, u32[]{:S(2)}) copy-start(bf16[1,256,6144]{2,1,0:T(8,128)(2,1)} %param.16) | copy-start | bytes 9437188
  8.0 84.1 %all-gather.2.cloned.1.call-start = ((), (), s32[]{:S(2)}) async-start(), calls=%async_computation.5 | async-start | bytes 3244032 | tf_op jit(solution)/shard_map/all_gather | solution.py:92
  8.7 118.0 %all-reduce.5.cloned.1.call-start = ((), (), s32[]{:S(2)}) async-start(), calls=%async_computation.3 | async-start | bytes 917504 | tf_op jit(solution)/shard_map/psum | solution.py:44
  50.5 0.7 copy-start.1
  53.4 272.4 %reduce-scatter.7.cloned.1.call-start = ((), (), s32[]{:S(2)}) async-start(), calls=%async_computation.7 | async-start | bytes 3244032
  112.2 2.8 copy-start.4
  112.3 15.6 %copy-start.2 = (bf16[224,512]{1,0:T(8,128)(2,1)S(1)}, bf16[224,512]{1,0:T(8,128)(2,1)}, u32[]{:S(2)}) copy-start(bf16[224,512]{1,0:T(8,128)(2,1)} %param.21) | copy-start | bytes 688132
  112.3 428.7 %reduce-scatter.5.cloned.1.call-start = ((), (), s32[]{:S(2)}) async-start(), calls=%async_computation.4 | async-start | bytes 540672 | tf_op jit(solution)/shard_map/reduce_scatter | solution.py:38
  326.8 214.2 %copy-start.3 = (bf16[8,512]{1,0:T(8,128)(2,1)S(1)}, bf16[8,512]{1,0:T(8,128)(2,1)}, u32[]{:S(2)}) copy-start(bf16[8,512]{1,0:T(8,128)(2,1)} %param.18) | copy-start | bytes 24580
  472.6 68.4 %all-to-all-start = ((bf16[4,8,512]{2,0,1:T(4,128)(2,1)}), bf16[4,8,512]{2,0,1:T(4,128)(2,1)S(1)}, u32[]{:S(2)}, u32[]{:S(2)}) async-start(bf16[4,8,512]{2,0,1:T(4,128)(2,1)} %bitcast.8), calls=%async_computation.1 | async-start | bytes 65536 | tf_op jit(solution)/shard_map/all_to_all | solution.py:121
  508.4 150.3 %all-reduce.7.cloned.1.call-start = ((), (), s32[]{:S(2)}) async-start(), calls=%async_computation.6 | async-start | bytes 458752 | tf_op jit(solution)/shard_map/psum | solution.py:44
Sparse Core Ops, SparseCore 0:
  11.8 80.3 all-gather.1
  112.4 213.3 reduce-scatter.6
  329.6 211.2 reduce-scatter.4
Sparse Core Ops, SparseCore 1:
  53.5 73.2 all-reduce.4
  580.0 78.6 all-reduce.6
where the time goes:
time: 670 us; the launch traced here: 669 us
  waiting for transfers between devices  354 us (53%)
  blocking collectives  218 us (33%)
  starting transfers between devices  35.9 us (5%)
  matrix products  26.2 us (4%)
  between operations  16 us (2%)
  local copies, waits for them, and re-layouts  14.4 us (2%)
    unnamed x6, waiting for transfers between devices  198 us
    unnamed x1, blocking collectives  141 us
    psum x2, waiting for transfers between devices, expert_totals(): return lax.psum(values, 'expert')  88.3 us
    all_gather x2, blocking collectives, dp_rows(): return lax.all_gather(values, 'dp', axis=0, tiled=True)  77.3 us
    all_gather x1, waiting for transfers between devices, body(): every_token = lax.all_gather(teacher_in, 'dp', axis=0, tiled=True)  36.1 us
    all_to_all x1, starting transfers between devices, body(): lax.all_to_all(projected.reshape(capacity, experts, sd_dev), 'expert', sp...  35.8 us
    reduce_scatter x1, waiting for transfers between devices, dp_sums(): lax.psum_scatter(term_fn(jnp.int32(0), share * lax.axis_size('dp')), 'dp'...  32.2 us
  transfers between devices with their start and end apart: 6, of which 5 were waited for; matrix products, arithmetic and copies ran while one was open for 6% of the time, Pallas kernels for 0%

commit v1 on v0

v1 whole, which is shorter than its diff:
```python
import math

import jax
import jax.numpy as jnp
from jax import lax
from jax.sharding import Mesh
from jax.sharding import PartitionSpec as P

NX, NZ, NY, NC = 4, 8, 4, 2
DP = ("x", "z")
EX = ("y", "c")
BF = jnp.bfloat16
F32 = jnp.float32


def exchange(values, axes):
    return lax.all_to_all(values, axes, 0, 0, tiled=False)


def spread(values, axes, count):
    return exchange(jnp.broadcast_to(values[None], (count,) + values.shape), axes)


def swap_cores(values):
    return lax.ppermute(values, "c", [(0, 1), (1, 0)])


def both_cores(values, core):
    other = swap_cores(values)
    first = jnp.where(core == 0, values, other)
    second = jnp.where(core == 0, other, values)
    return first, second


def expert_sum(values):
    rows, width = values.shape
    terms = exchange(values.astype(BF).reshape(NY * NC, rows // (NY * NC), width), EX)
    mine = jnp.sum(terms.astype(F32), axis=0)
    return spread(mine.astype(BF), EX, NY * NC).reshape(rows, width).astype(F32)


def body(
    teacher_in,
    route_ids,
    router,
    w_gate,
    w_up,
    w_down,
    projection,
    student_in,
    s_gate,
    s_up,
    s_down,
):
    core = lax.axis_index("c")
    row = lax.axis_index("y")
    expert = row * NC + core
    tok_dp, width = teacher_in.shape
    tokens = route_ids.shape[0]
    experts = router.shape[1]
    sff_dev = s_gate.shape[1]
    sd_dev = student_in.shape[1]
    chunk = width // (NY * NC)

    part = lax.dynamic_slice_in_dim(teacher_in, expert * chunk, chunk, 1)
    column = spread(part, "z", NZ).reshape(NZ * tok_dp, chunk)
    plane = spread(column, ("x", "y"), NX * NY).reshape(NX, NY, NZ * tok_dp, chunk)
    even, odd = both_cores(plane, core)
    every = jnp.stack([even, odd], axis=0)
    every = every.transpose(1, 3, 2, 0, 4).reshape(tokens, width)

    logits = jnp.dot(every, router, preferred_element_type=F32)
    lane = lax.broadcasted_iota(jnp.int32, (tokens, experts), 1)
    first = route_ids[:, 0:1]
    second = route_ids[:, 1:2]
    l0 = jnp.sum(jnp.where(lane == first, logits, 0.0), axis=1, keepdims=True)
    l1 = jnp.sum(jnp.where(lane == second, logits, 0.0), axis=1, keepdims=True)
    gate = jnp.where(first == expert, jax.nn.sigmoid(l0 - l1), 0.0) + jnp.where(
        second == expert, jax.nn.sigmoid(l1 - l0), 0.0
    )
    named = (first == expert) | (second == expert)

    gate_part = jnp.dot(every, w_gate[0], preferred_element_type=F32)
    up_part = jnp.dot(every, w_up[0], preferred_element_type=F32)
    active = gate_part * jax.nn.sigmoid(gate_part) * up_part
    hidden = jnp.where(named, active * gate, 0.0).astype(BF)

    partial = lax.dot_general(
        w_down[0], hidden, (((0,), (1,)), ((), ())), preferred_element_type=F32
    )
    half = tokens // NC
    low = partial[:, :half]
    high = partial[:, half:]
    keep = jnp.where(core == 0, low, high)
    give = jnp.where(core == 0, high, low).astype(BF)
    pair = (keep + swap_cores(give).astype(F32)).astype(BF)
    group = width // (NX * NZ * NY)
    terms = pair.reshape(NX, NZ, NY, group, half).transpose(0, 2, 1, 3, 4)
    terms = exchange(terms.reshape(NX * NY, NZ, group, half), ("x", "y"))
    summed = jnp.sum(terms.astype(F32), axis=0).astype(BF)
    terms = exchange(summed, "z")
    summed = jnp.sum(terms.astype(F32), axis=0).astype(BF)
    mine = spread(summed, EX, NY * NC)
    mine = mine.reshape(NY, NC, group, half).transpose(0, 2, 1, 3)
    mine = mine.reshape(NY * group, tokens)
    return_cols = lax.dynamic_slice_in_dim(projection, expert * sd_dev, sd_dev, 1)
    target = lax.dot_general(
        mine, return_cols, (((0,), (0,)), ((), ())), preferred_element_type=F32
    )

    student_all = spread(student_in, DP, NX * NZ).reshape(tokens, sd_dev)
    gate_s = jnp.dot(student_all, s_gate, preferred_element_type=F32)
    up_s = jnp.dot(student_all, s_up, preferred_element_type=F32)
    pair_sums = expert_sum(jnp.concatenate([gate_s, up_s], axis=1))
    gate_s = pair_sums[:, :sff_dev]
    up_s = pair_sums[:, sff_dev:]
    sigma = jax.nn.sigmoid(gate_s)
    active_s = gate_s * sigma
    hidden_s = (active_s * up_s).astype(BF)
    out_part = jnp.dot(hidden_s, s_down, preferred_element_type=F32) - target
    terms = exchange(out_part.astype(BF).reshape(NX * NZ, tok_dp, sd_dev), DP)
    mismatch = student_in.astype(F32) + jnp.sum(terms.astype(F32), axis=0)
    cotangent = (mismatch * (1.0 / math.sqrt(tokens))).astype(BF)
    cotangent_all = spread(cotangent, DP, NX * NZ).reshape(tokens, sd_dev)
    grad_down = lax.dot_general(
        hidden_s, cotangent_all, (((0,), (0,)), ((), ())), preferred_element_type=F32
    ).astype(BF)
    d_hidden = expert_sum(
        lax.dot_general(
            cotangent_all, s_down, (((1,), (1,)), ((), ())), preferred_element_type=F32
        )
    )
    d_gate = (d_hidden * up_s * sigma * (1.0 + gate_s * (1.0 - sigma))).astype(BF)
    d_up = (d_hidden * active_s).astype(BF)
    grad_gate = lax.dot_general(
        student_all, d_gate, (((0,), (0,)), ((), ())), preferred_element_type=F32
    ).astype(BF)
    grad_up = lax.dot_general(
        student_all, d_up, (((0,), (0,)), ((), ())), preferred_element_type=F32
    ).astype(BF)
    return (grad_gate, grad_up, grad_down, mismatch)


def solution(mesh):
    fine = Mesh(mesh.devices.reshape(NX, NZ, NY, NC), ("x", "z", "y", "c"))
    return jax.shard_map(
        body,
        mesh=fine,
        in_specs=(
            P(DP, None),
            P(),
            P(),
            P(EX, None, DP),
            P(EX, None, DP),
            P(EX, DP, None),
            P(DP, None),
            P(DP, EX),
            P(EX, DP),
            P(EX, DP),
            P(DP, EX),
        ),
        out_specs=(P(EX, DP), P(EX, DP), P(DP, EX), P(DP, EX)),
        check_vma=False,
    )
```

time: 670 us -> 251 us (0.37)
  waiting for transfers between devices: 354 us -> 36.9 us
  blocking collectives: 218 us -> 110 us
  other arithmetic: 4.01 us -> 22 us
  between operations: 16 us -> 0.85 us
  local copies, waits for them, and re-layouts: 14.4 us -> 24.5 us
    unnamed x6 -> x0, waiting for transfers between devices: 198 us -> none
    unnamed x1 -> x0, blocking collectives: 141 us -> none
    all_to_all x0 -> x7, blocking collectives: none -> 110 us  [exchange(): return lax.all_to_all(values, axes, 0, 0, tiled=False)]
    psum x2 -> x0, waiting for transfers between devices: 88.3 us -> none  [expert_totals(): return lax.psum(values, 'expert')]
    all_gather x2 -> x0, blocking collectives: 77.3 us -> none  [dp_rows(): return lax.all_gather(values, 'dp', axis=0, tiled=True)]
    all_gather x1 -> x0, waiting for transfers between devices: 36.1 us -> none  [body(): every_token = lax.all_gather(teacher_in, 'dp', axis=0, tiled=True)]
    all_to_all x1 -> x5, waiting for transfers between devices: 0.01 us -> 33.6 us  [exchange(): return lax.all_to_all(values, axes, 0, 0, tiled=False)]
    reduce_scatter x1 -> x0, waiting for transfers between devices: 32.2 us -> none  [dp_sums(): lax.psum_scatter(term_fn(jnp.int32(0), share * lax.axis_size('dp')), 'dp'...]
  transfers between devices with their start and end apart: 6 -> 7, of which waited for: 5 -> 5; matrix products, arithmetic and copies ran while one was open for 6% -> 8% of each run, Pallas kernels for 0% -> 0%
where the time goes in v1:
time: 251 us; the launch traced here: 250 us
  blocking collectives  110 us (44%)
  waiting for transfers between devices  36.9 us (15%)
  starting transfers between devices  31.1 us (12%)
  local copies, waits for them, and re-layouts  24.5 us (10%)
  matrix products  24.4 us (10%)
  other arithmetic  22 us (9%)
    all_to_all x7, blocking collectives, exchange(): return lax.all_to_all(values, axes, 0, 0, tiled=False)  110 us
    all_to_all x5, waiting for transfers between devices, exchange(): return lax.all_to_all(values, axes, 0, 0, tiled=False)  33.6 us
    all_to_all x5, starting transfers between devices, exchange(): return lax.all_to_all(values, axes, 0, 0, tiled=False)  27.7 us
    dot_general x1, matrix products, body(): lax.dot_general(w_down[0], hidden, (((0,), (1,)), ((), ())), preferred_el...  8.95 us
    reshape x1, local copies, waits for them, and re-layouts, body(): every = every.transpose(1, 3, 2, 0, 4).reshape(tokens, width)  7.77 us
    convert_element_type x1, other arithmetic, body(): pair = (keep + swap_cores(give).astype(F32)).astype(BF)  5.03 us
  transfers between devices with their start and end apart: 7, of which 5 were waited for; matrix products, arithmetic and copies ran while one was open for 8% of the time, Pallas kernels for 0%

profile of v1, /device:TPU:1, one launch (start us, length us, event | category | flops | bytes accessed | tf_op | source)
XLA Modules:
  0.0 249.9 jit_solution(13316427733083084950)
XLA Ops:
  0.6 0.0 copy-start
  0.6 0.0 copy-start.8
  0.7 0.9 constant_dynamic-slice_fusion
  1.5 16.6 %all_to_all.60 = bf16[8,8,768]{2,1,0:T(8,128)(2,1)S(1)} all-to-all(bf16[8,8,768]{2,1,0:T(8,128)(2,1)S(1)} %broadcast_in_dim.73), channel_id=1, replica_groups=mesh['x'=4,'z'=8,'y'=4,'c'=2] {'z'}, dimensions={0} | all-to-all | bytes 196608 | tf_op jit(solution)/shard_map/all_to_all | solution.py:17
  18.1 0.1 broadcast_in_dim.75
  18.3 27.1 %all_to_all.61 = bf16[16,64,768]{2,1,0:T(8,128)(2,1)} all-to-all(bf16[16,64,768]{2,1,0:T(8,128)(2,1)S(1)} %broadcast_in_dim.75), channel_id=1, replica_groups=mesh['x'=4,'z'=8,'y'=4,'c'=2] {'x','y'}, dimensions={0} | all-to-all | bytes 3145728 | tf_op jit(solution)/shard_map/all_to_all | solution.py:17
  45.4 3.0 %collective-permute-start = (bf16[4,4,64,768]{3,2,1,0:T(8,128)(2,1)}, bf16[4,4,64,768]{3,2,1,0:T(8,128)(2,1)}, u32[]{:S(2)}, u32[]{:S(2)}) collective-permute-start(bf16[4,4,64,768]{3,2,1,0:T(8,128)(2,1)} %bitcast.6), channel_id=1, source_target_pairs={{0,1},{1,0},{2,3},{3,2},{4,5},{5,4},{6,7},{7,6},{8,9},{9,8},{10,11... | collective-permute-start | bytes 4718600 | tf_op jit(solution)/shard_map/ppermute | solution.py:25
  48.4 0.0 copy-done.8
  48.4 3.3 %collective-permute-done = bf16[4,4,64,768]{3,2,1,0:T(8,128)(2,1)} collective-permute-done((bf16[4,4,64,768]{3,2,1,0:T(8,128)(2,1)}, bf16[4,4,64,768]{3,2,1,0:T(8,128)(2,1)}, u32[]{:S(2)}, u32[]{:S(2)}) %collective-permute-start) | collective-permute-done | bytes 1572896 | tf_op jit(solution)/shard_map/ppermute | solution.py:25
  51.8 2.1 select_bitcast_fusion.1
  53.9 0.3 maximum_bitcast_fusion
  54.1 4.9 %copy.24 = bf16[4,64,4,2,768]{4,3,2,1,0:T(2,128)(2,1)} copy(bf16[4,64,4,2,768]{4,1,2,0,3:T(8,128)(2,1)S(1)} %maximum_bitcast_fusion) | data formatting | bytes 6291456 | tf_op jit(solution)/shard_map/transpose | solution.py:70
  59.0 7.8 %reshape.125 = bf16[256,6144]{1,0:T(8,128)(2,1)} reshape(bf16[4,64,4,2,768]{4,3,2,1,0:T(2,128)(2,1)} %copy.24) | data formatting | bytes 6291456 | tf_op jit(solution)/shard_map/reshape | solution.py:70
  66.8 4.0 %fusion.3 = f32[256,256]{1,0:T(8,128)S(1)} fusion(bf16[256,6144]{1,0:T(8,128)(2,1)} %reshape.125, bf16[1,6144,256]{2,1,0:T(8,128)(2,1)} %param.14), kind=kOutput, calls=%fused_computation.5 | convolution fusion | flops 805306368 | bytes 6553600 | tf_op jit(solution)/shard_map/dot_general | solution.py:83
  70.8 0.0 copy-done.1
  70.8 0.0 copy-done.5
  70.8 0.9 select_reduce_fusion
  71.8 0.0 copy-done
  71.8 9.0 %convolution_bitcast_fusion = f32[6144,256]{0,1:T(8,128)} fusion(bf16[1,256,6144]{2,1,0:T(8,128)(2,1)S(1)} %copy-done, bf16[256,6144]{1,0:T(8,128)(2,1)} %reshape.125, bf16[1,6144,256]{2,1,0:T(8,128)(2,1)} %param.15, f32[256,256]{1,0:T(8,128)S(1)} %fusion.3, f32[256]{0:T(256)S(1)} %bitcast.96, pred[256]{0:T(512)(128)(4,1)S(1)} %or_reduce_fusion), kind=kOutput, calls=%fused_computation | convolution fusion | flops 1611137024 | bytes 15992064 | tf_op jit(solution)/shard_map/dot_general | solution.py:88
  80.7 4.4 %select_convert_fusion = bf16[6144,128]{0,1:T(8,128)(2,1)} fusion(f32[6144,256]{0,1:T(8,128)} %convolution_bitcast_fusion, pred[]{:T(512)S(6)} %eq.40), kind=kLoop, calls=%fused_computation.8 | loop fusion | flops 786432 | bytes 4718593 | tf_op jit(solution)/shard_map/convert_element_type | solution.py:95
  85.1 0.4 collective-permute-start.1
  85.5 0.0 copy-done.6
  85.5 13.7 %all_to_all.62 = bf16[32,8,512]{2,1,0:T(8,128)(2,1)S(1)} all-to-all(bf16[32,8,512]{2,1,0:T(8,128)(2,1)S(1)} %broadcast_in_dim.40), channel_id=1, replica_groups=mesh['x'=4,'z'=8,'y'=4,'c'=2] {'x','z'}, dimensions={0} | all-to-all | bytes 524288 | tf_op jit(solution)/shard_map/all_to_all | solution.py:17
  99.2 0.3 convolution_convert_fusion.3
  99.5 0.3 convolution_convert_fusion.4
  99.7 0.1 pad_maximum_fusion
  99.9 11.5 %all_to_all.63 = bf16[8,32,448]{2,1,0:T(8,128)(2,1)} all-to-all(bf16[8,32,448]{2,1,0:T(8,128)(2,1)S(1)} %pad_maximum_fusion), channel_id=1, replica_groups=mesh['x'=4,'z'=8,'y'=4,'c'=2] {'y','c'}, dimensions={0} | all-to-all | bytes 458752 | tf_op jit(solution)/shard_map/all_to_all | solution.py:17
  111.4 1.0 reduce_sum.75
  112.4 0.7 broadcast_in_dim.70
  113.1 5.0 %all-to-all-start.2 = ((bf16[8,32,448]{2,1,0:T(8,128)(2,1)}), bf16[8,32,448]{2,1,0:T(8,128)(2,1)}, u32[]{:S(2)}, u32[]{:S(2)}) async-start(bf16[8,32,448]{2,1,0:T(8,128)(2,1)} %broadcast_in_dim.70), calls=%async_computation.2 | async-start | bytes 524288 | tf_op jit(solution)/shard_map/all_to_all | solution.py:17
  118.1 0.0 collective-permute-done.1
  118.1 5.0 %add_convert_fusion = bf16[6144,128]{0,1:T(8,128)(2,1)} fusion(bf16[6144,128]{0,1:T(8,128)(2,1)} %collective-permute-done.1, f32[6144,256]{0,1:T(8,128)} %convolution_bitcast_fusion, pred[]{:T(512)S(6)} %eq.40), kind=kLoop, calls=%fused_computation.7 | loop fusion | flops 3145728 | bytes 9437185 | tf_op jit(solution)/shard_map/convert_element_type | solution.py:96
  123.1 2.6 %copy.25 = bf16[6144,128]{1,0:T(8,128)(2,1)} copy(bf16[6144,128]{0,1:T(8,128)(2,1)} %add_convert_fusion) | data formatting | bytes 3145728 | tf_op jit(solution)/shard_map/convert_element_type | solution.py:96
  125.7 2.8 %copy.26 = bf16[4,4,8,48,128]{4,3,2,1,0:T(8,128)(2,1)} copy(bf16[4,4,8,48,128]{4,3,1,2,0:T(8,128)(2,1)} %bitcast.88) | data formatting | bytes 3145728 | tf_op jit(solution)/shard_map/transpose | solution.py:98
  128.5 0.0 all-to-all-done.2
  128.5 6.2 %all-to-all-start.5 = ((bf16[16,8,48,128]{3,2,1,0:T(8,128)(2,1)}), bf16[16,8,48,128]{3,2,1,0:T(8,128)(2,1)}, u32[]{:S(2)}, u32[]{:S(2)}) async-start(bf16[16,8,48,128]{3,2,1,0:T(8,128)(2,1)} %bitcast.87), calls=%async_computation.5 | async-start | bytes 3145728 | tf_op jit(solution)/shard_map/all_to_all | solution.py:17
  134.6 1.8 bitcast_convert_fusion
  136.5 20.6 %all-to-all-done.5 = bf16[16,8,48,128]{3,2,1,0:T(8,128)(2,1)} async-done(((bf16[16,8,48,128]{3,2,1,0:T(8,128)(2,1)}), bf16[16,8,48,128]{3,2,1,0:T(8,128)(2,1)}, u32[]{:S(2)}, u32[]{:S(2)}) %all-to-all-start.5) | async-done | bytes 1572896 | tf_op jit(solution)/shard_map/all_to_all | solution.py:17
  157.0 2.3 reduce_sum.78
  159.3 4.0 %all-to-all-start.6 = ((bf16[8,48,128]{2,1,0:T(8,128)(2,1)}), bf16[8,48,128]{2,1,0:T(8,128)(2,1)}, u32[]{:S(2)}, u32[]{:S(2)}) async-start(bf16[8,48,128]{2,1,0:T(8,128)(2,1)} %reduce_sum.78), calls=%async_computation.6 | async-start | bytes 196608 | tf_op jit(solution)/shard_map/all_to_all | solution.py:17
  163.3 1.2 multiply_convert_fusion
  164.5 6.3 %all-to-all-done.6 = bf16[8,48,128]{2,1,0:T(8,128)(2,1)} async-done(((bf16[8,48,128]{2,1,0:T(8,128)(2,1)}), bf16[8,48,128]{2,1,0:T(8,128)(2,1)}, u32[]{:S(2)}, u32[]{:S(2)}) %all-to-all-start.6) | async-done | bytes 98336 | tf_op jit(solution)/shard_map/all_to_all | solution.py:17
  170.9 0.9 reduce_sum.79
  171.8 0.7 broadcast_in_dim.79
  172.4 7.9 %all-to-all-start.7 = ((bf16[8,48,128]{2,1,0:T(8,128)(2,1)}), bf16[8,48,128]{2,1,0:T(8,128)(2,1)}, u32[]{:S(2)}, u32[]{:S(2)}) async-start(bf16[8,48,128]{2,1,0:T(8,128)(2,1)} %broadcast_in_dim.79), calls=%async_computation.7 | async-start | bytes 196608 | tf_op jit(solution)/shard_map/all_to_all | solution.py:17
  180.3 2.0 fusion.54
  182.3 3.2 %all-to-all-done.7 = bf16[8,48,128]{2,1,0:T(8,128)(2,1)} async-done(((bf16[8,48,128]{2,1,0:T(8,128)(2,1)}), bf16[8,48,128]{2,1,0:T(8,128)(2,1)}, u32[]{:S(2)}, u32[]{:S(2)}) %all-to-all-start.7) | async-done | bytes 98336 | tf_op jit(solution)/shard_map/all_to_all | solution.py:17
  185.4 1.0 copy.27
  186.4 1.4 fusion.6
  187.8 12.7 %all_to_all.64 = bf16[32,8,512]{2,1,0:T(8,128)(2,1)S(1)} all-to-all(bf16[32,8,512]{2,1,0:T(8,128)(2,1)S(1)} %fusion.6), channel_id=1, replica_groups=mesh['x'=4,'z'=8,'y'=4,'c'=2] {'x','z'}, dimensions={0} | all-to-all | bytes 524288 | tf_op jit(solution)/shard_map/all_to_all | solution.py:17
  200.5 0.6 multiply_convert_fusion.1
  201.1 15.8 %all_to_all.65 = bf16[32,8,512]{2,1,0:T(8,128)(2,1)S(1)} all-to-all(bf16[32,8,512]{2,1,0:T(8,128)(2,1)S(1)} %broadcast_in_dim.80), channel_id=1, replica_groups=mesh['x'=4,'z'=8,'y'=4,'c'=2] {'x','z'}, dimensions={0} | all-to-all | bytes 524288 | tf_op jit(solution)/shard_map/all_to_all | solution.py:17
  216.9 0.7 copy-done.2
  217.6 1.8 convolution_convert_fusion.5
  219.5 1.7 copy.28
  221.1 12.8 %all_to_all.66 = bf16[8,32,224]{2,1,0:T(8,128)(2,1)} all-to-all(bf16[8,32,224]{2,1,0:T(8,128)(2,1)} %bitcast.91), channel_id=1, replica_groups=mesh['x'=4,'z'=8,'y'=4,'c'=2] {'y','c'}, dimensions={0} | all-to-all | bytes 229376 | tf_op jit(solution)/shard_map/all_to_all | solution.py:17
  234.0 0.9 reduce_sum.81
  234.9 0.7 broadcast_in_dim.81
  235.6 4.7 %all-to-all-start.11 = ((bf16[8,32,224]{2,1,0:T(8,128)(2,1)}), bf16[8,32,224]{2,1,0:T(8,128)(2,1)}, u32[]{:S(2)}, u32[]{:S(2)}) async-start(bf16[8,32,224]{2,1,0:T(8,128)(2,1)} %broadcast_in_dim.81), calls=%async_computation.11 | async-start | bytes 262144 | tf_op jit(solution)/shard_map/all_to_all | solution.py:17
  240.3 1.9 convolution_convert_fusion
  242.2 3.5 %all-to-all-done.11 = bf16[8,32,224]{2,1,0:T(8,128)(2,1)} async-done(((bf16[8,32,224]{2,1,0:T(8,128)(2,1)}), bf16[8,32,224]{2,1,0:T(8,128)(2,1)}, u32[]{:S(2)}, u32[]{:S(2)}) %all-to-all-start.11) | async-done | bytes 114720 | tf_op jit(solution)/shard_map/all_to_all | solution.py:17
  245.7 1.3 fusion.25
  247.0 2.0 fusion.14
  249.0 0.9 fusion.13
  (18 shorter events, 0.2 us)
Async XLA Ops:
  0.6 71.1 %copy-start = (bf16[1,256,6144]{2,1,0:T(8,128)(2,1)S(1)}, bf16[1,256,6144]{2,1,0:T(8,128)(2,1)}, u32[]{:S(2)}) copy-start(bf16[1,256,6144]{2,1,0:T(8,128)(2,1)} %param.16) | copy-start | bytes 9437188
  0.6 47.7 %copy-start.8 = (s32[256,2]{0,1:T(2,128)S(1)}, s32[256,2]{0,1:T(2,128)}, u32[]{:S(2)}) copy-start(s32[256,2]{0,1:T(2,128)} %param.12) | copy-start | bytes 6148
  45.4 6.4 %collective-permute-start = (bf16[4,4,64,768]{3,2,1,0:T(8,128)(2,1)}, bf16[4,4,64,768]{3,2,1,0:T(8,128)(2,1)}, u32[]{:S(2)}, u32[]{:S(2)}) collective-permute-start(bf16[4,4,64,768]{3,2,1,0:T(8,128)(2,1)} %bitcast.6), channel_id=1, source_target_pairs={{0,1},{1,0},{2,3},{3,2},{4,5},{5,4},{6,7},{7,6},{8,9},{9,8},{10,11... | collective-permute-start | bytes 4718600 | tf_op jit(solution)/shard_map/ppermute | solution.py:25
  66.8 4.0 %copy-start.1 = (bf16[256,6144]{1,0:T(8,128)(2,1)S(1)}, bf16[256,6144]{1,0:T(8,128)(2,1)}, u32[]{:S(2)}) copy-start(bf16[256,6144]{1,0:T(8,128)(2,1)} %reshape.125) | copy-start | bytes 9437188
  66.8 4.0 %copy-start.5 = (bf16[6144,8]{0,1:T(8,128)(2,1)S(1)}, bf16[6144,8]{0,1:T(8,128)(2,1)}, u32[]{:S(2)}) copy-start(bf16[6144,8]{0,1:T(8,128)(2,1)} %param.13) | copy-start | bytes 294916
  80.7 4.8 %copy-start.6 = (bf16[8,512]{1,0:T(8,128)(2,1)S(1)}, bf16[8,512]{1,0:T(8,128)(2,1)}, u32[]{:S(2)}) copy-start(bf16[8,512]{1,0:T(8,128)(2,1)} %param.18) | copy-start | bytes 24580
  80.7 18.5 %copy-start.3 = (bf16[512,224]{0,1:T(8,128)(2,1)S(1)}, bf16[512,224]{0,1:T(8,128)(2,1)}, u32[]{:S(2)}) copy-start(bf16[512,224]{0,1:T(8,128)(2,1)} %param.20) | copy-start | bytes 688132
  80.7 18.7 %copy-start.4 = (bf16[512,224]{0,1:T(8,128)(2,1)S(1)}, bf16[512,224]{0,1:T(8,128)(2,1)}, u32[]{:S(2)}) copy-start(bf16[512,224]{0,1:T(8,128)(2,1)} %param.19) | copy-start | bytes 688132
  85.1 33.0 %collective-permute-start.1 = (bf16[6144,128]{0,1:T(8,128)(2,1)}, bf16[6144,128]{0,1:T(8,128)(2,1)}, u32[]{:S(2)}, u32[]{:S(2)}) collective-permute-start(bf16[6144,128]{0,1:T(8,128)(2,1)} %select_convert_fusion), channel_id=1, source_target_pairs={{0,1},{1,0},{2,3},{3,2},{4,5},{5,4},{6,7},{7,6},{8,9},{9,8},{10,11... | collective-permute-start | bytes 4718600 | tf_op jit(solution)/shard_map/ppermute | solution.py:25
  113.1 15.4 %all-to-all-start.2 = ((bf16[8,32,448]{2,1,0:T(8,128)(2,1)}), bf16[8,32,448]{2,1,0:T(8,128)(2,1)}, u32[]{:S(2)}, u32[]{:S(2)}) async-start(bf16[8,32,448]{2,1,0:T(8,128)(2,1)} %broadcast_in_dim.70), calls=%async_computation.2 | async-start | bytes 524288 | tf_op jit(solution)/shard_map/all_to_all | solution.py:17
  128.5 28.5 %all-to-all-start.5 = ((bf16[16,8,48,128]{3,2,1,0:T(8,128)(2,1)}), bf16[16,8,48,128]{3,2,1,0:T(8,128)(2,1)}, u32[]{:S(2)}, u32[]{:S(2)}) async-start(bf16[16,8,48,128]{3,2,1,0:T(8,128)(2,1)} %bitcast.87), calls=%async_computation.5 | async-start | bytes 3145728 | tf_op jit(solution)/shard_map/all_to_all | solution.py:17
  159.3 11.6 %all-to-all-start.6 = ((bf16[8,48,128]{2,1,0:T(8,128)(2,1)}), bf16[8,48,128]{2,1,0:T(8,128)(2,1)}, u32[]{:S(2)}, u32[]{:S(2)}) async-start(bf16[8,48,128]{2,1,0:T(8,128)(2,1)} %reduce_sum.78), calls=%async_computation.6 | async-start | bytes 196608 | tf_op jit(solution)/shard_map/all_to_all | solution.py:17
  172.4 28.1 %copy-start.7 = (bf16[8,512]{1,0:T(8,128)(2,1)S(1)}, bf16[8,512]{1,0:T(8,128)(2,1)}, u32[]{:S(2)}) copy-start(bf16[8,512]{1,0:T(8,128)(2,1)} %param.18) | copy-start | bytes 24580
  172.4 13.0 %all-to-all-start.7 = ((bf16[8,48,128]{2,1,0:T(8,128)(2,1)}), bf16[8,48,128]{2,1,0:T(8,128)(2,1)}, u32[]{:S(2)}, u32[]{:S(2)}) async-start(bf16[8,48,128]{2,1,0:T(8,128)(2,1)} %broadcast_in_dim.79), calls=%async_computation.7 | async-start | bytes 196608 | tf_op jit(solution)/shard_map/all_to_all | solution.py:17
  216.9 0.7 copy-start.2
  235.6 10.1 %all-to-all-start.11 = ((bf16[8,32,224]{2,1,0:T(8,128)(2,1)}), bf16[8,32,224]{2,1,0:T(8,128)(2,1)}, u32[]{:S(2)}, u32[]{:S(2)}) async-start(bf16[8,32,224]{2,1,0:T(8,128)(2,1)} %broadcast_in_dim.81), calls=%async_computation.11 | async-start | bytes 262144 | tf_op jit(solution)/shard_map/all_to_all | solution.py:17

commit v2 on v1

v2 whole, which is shorter than its diff:
```python
import functools
import math

import jax
import jax.numpy as jnp
from jax import lax
from jax.experimental import pallas as pl
from jax.experimental.pallas import tpu as pltpu
from jax.sharding import Mesh
from jax.sharding import PartitionSpec as P

NX, NZ, NY, NC = 4, 8, 4, 2
ND = NX * NZ
NE = NY * NC
DP = ("x", "z")
EX = ("y", "c")
BF = jnp.bfloat16
F32 = jnp.float32
VMEM_BYTES = 28 * 1024 * 1024
STEPS = 8


def exchange(values, axes):
    return lax.all_to_all(values, axes, 0, 0, tiled=False)


def spread(values, axes, count):
    return exchange(jnp.broadcast_to(values[None], (count,) + values.shape), axes)


def swap_cores(values):
    return lax.ppermute(values, "c", [(0, 1), (1, 0)])


def along_y(values, shift):
    return lax.ppermute(values, "y", [(i, (i + shift) % NY) for i in range(NY)])


def expert_sum(values, core):
    half = values.shape[0] // 2
    low, high = values[:half], values[half:]
    give = jnp.where(core == 0, high, low).astype(BF)
    keep = jnp.where(core == 0, low, high)
    mine = (keep + swap_cores(give).astype(F32)).astype(BF)
    others = [along_y(mine, s) for s in range(1, NY)]
    total = mine.astype(F32)
    for term in others:
        total = total + term.astype(F32)
    total = total.astype(BF)
    other = swap_cores(total)
    first = jnp.where(core == 0, total, other)
    second = jnp.where(core == 0, other, total)
    return jnp.concatenate([first, second], axis=0).astype(F32)


def dot(a, b):
    return jnp.dot(a, b, preferred_element_type=F32)


def dot_tn(a, b):
    return lax.dot_general(a, b, (((0,), (0,)), ((), ())), preferred_element_type=F32)


def dot_nt(a, b):
    return lax.dot_general(a, b, (((1,), (1,)), ((), ())), preferred_element_type=F32)


def own_kernel(where_ref, x0, x1, wg, wu, rt, gate_out, up_out, logit_out):
    step = pl.program_id(0)

    @pl.when(step == 0)
    def _():
        x = x0[...]
        gate_out[...] = dot(x, wg[0])
        up_out[...] = dot(x, wu[0])
        logit_out[...] = dot(x, rt[...])

    @pl.when(step == 1)
    def _():
        x = x1[...]
        gate_out[...] += dot(x, wg[0])
        up_out[...] += dot(x, wu[0])
        logit_out[...] += dot(x, rt[...])


def rest_kernel(where_ref, *refs):
    xs = refs[:6]
    wg, wu, rt, gate_in, up_in, logit_in, ids, wd = refs[6:14]
    keeps = refs[14:18]
    gives = refs[18:22]
    gate_acc, up_acc, logit_acc, hidden, block = refs[22:]
    step = pl.program_id(0)
    row = where_ref[6]
    core = where_ref[7]

    for j in range(6):

        @pl.when(step == j)
        def _(j=j):
            x = xs[j][...]
            if j == 0:
                gate_acc[...] = gate_in[...] + dot(x, wg[0])
                up_acc[...] = up_in[...] + dot(x, wu[0])
                logit_acc[...] = logit_in[...] + dot(x, rt[...])
            else:
                gate_acc[...] += dot(x, wg[0])
                up_acc[...] += dot(x, wu[0])
                logit_acc[...] += dot(x, rt[...])

    @pl.when(step == 5)
    def _():
        expert = row * NC + core
        logits = logit_acc[...]
        lane = lax.broadcasted_iota(jnp.int32, logits.shape, 1)
        first = ids[:, 0:1]
        second = ids[:, 1:2]
        l0 = jnp.sum(jnp.where(lane == first, logits, 0.0), axis=1, keepdims=True)
        l1 = jnp.sum(jnp.where(lane == second, logits, 0.0), axis=1, keepdims=True)
        gate = jnp.where(first == expert, jax.nn.sigmoid(l0 - l1), 0.0) + jnp.where(
            second == expert, jax.nn.sigmoid(l1 - l0), 0.0
        )
        named = (first == expert) | (second == expert)
        g = gate_acc[...]
        active = g * jax.nn.sigmoid(g) * up_acc[...] * gate
        hidden[...] = jnp.where(named, active, 0.0).astype(BF)

    @pl.when(step >= 6)
    def _():
        res = dot_nt(wd[...], hidden[...])
        block[...] = res.reshape(block.shape)
        half = block.shape[3] // 2
        for s in range(NY):
            at = lax.rem(row + s, NY)
            low = block[:, at, :, :half]
            high = block[:, at, :, half:]
            keeps[s][...] = jnp.where(core == 0, low, high).astype(BF)
            gives[s][...] = jnp.where(core == 0, high, low).astype(BF)


def expert_own(where, x0, x1, w_gate, w_up, router, tokens, chunk):
    hid = w_gate.shape[2]
    experts = router.shape[1]
    whole = lambda i, w: (0, 0)
    return pl.pallas_call(
        own_kernel,
        out_shape=(
            jax.ShapeDtypeStruct((tokens, hid), F32),
            jax.ShapeDtypeStruct((tokens, hid), F32),
            jax.ShapeDtypeStruct((tokens, experts), F32),
        ),
        grid_spec=pltpu.PrefetchScalarGridSpec(
            num_scalar_prefetch=1,
            grid=(2,),
            in_specs=[
                pl.BlockSpec((tokens, chunk), whole),
                pl.BlockSpec((tokens, chunk), whole),
                pl.BlockSpec((1, chunk, hid), lambda i, w: (0, w[i], 0)),
                pl.BlockSpec((1, chunk, hid), lambda i, w: (0, w[i], 0)),
                pl.BlockSpec((chunk, experts), lambda i, w: (w[i], 0)),
            ],
            out_specs=[
                pl.BlockSpec((tokens, hid), whole),
                pl.BlockSpec((tokens, hid), whole),
                pl.BlockSpec((tokens, experts), whole),
            ],
        ),
        compiler_params=pltpu.CompilerParams(vmem_limit_bytes=VMEM_BYTES),
        cost_estimate=pl.CostEstimate(
            flops=4 * tokens * 2 * chunk * hid,
            bytes_accessed=4 * chunk * (2 * hid + tokens) + 8 * tokens * hid,
            transcendentals=0,
        ),
    )(where, x0, x1, w_gate, w_up, router)


def expert_rest(where, xs, w_gate, w_up, router, sums, ids, down_t, tokens, chunk):
    hid = w_gate.shape[2]
    experts = router.shape[1]
    width = down_t.shape[0]
    group = width // (ND * NY)
    rows = width // STEPS
    whole = lambda i, w: (0, 0)
    at = lambda i, w: w[jnp.minimum(i, 5)]
    late = lambda i: jnp.maximum(i - 6, 0)
    out = jax.ShapeDtypeStruct((ND, group, tokens // 2), BF)
    return pl.pallas_call(
        rest_kernel,
        out_shape=(out,) * 8,
        grid_spec=pltpu.PrefetchScalarGridSpec(
            num_scalar_prefetch=1,
            grid=(6 + STEPS,),
            in_specs=[pl.BlockSpec((tokens, chunk), whole)] * 6
            + [
                pl.BlockSpec((1, chunk, hid), lambda i, w: (0, at(i, w), 0)),
                pl.BlockSpec((1, chunk, hid), lambda i, w: (0, at(i, w), 0)),
                pl.BlockSpec((chunk, experts), lambda i, w: (at(i, w), 0)),
                pl.BlockSpec((tokens, hid), whole),
                pl.BlockSpec((tokens, hid), whole),
                pl.BlockSpec((tokens, experts), whole),
                pl.BlockSpec((tokens, 2), whole),
                pl.BlockSpec((rows, hid), lambda i, w: (late(i), 0)),
            ],
            out_specs=[
                pl.BlockSpec((ND // STEPS, group, tokens // 2), lambda i, w: (late(i), 0, 0))
            ]
            * 8,
            scratch_shapes=[
                pltpu.VMEM((tokens, hid), F32),
                pltpu.VMEM((tokens, hid), F32),
                pltpu.VMEM((tokens, experts), F32),
                pltpu.VMEM((tokens, hid), BF),
                pltpu.VMEM((ND // STEPS, NY, group, tokens), F32),
            ],
        ),
        compiler_params=pltpu.CompilerParams(vmem_limit_bytes=VMEM_BYTES),
        cost_estimate=pl.CostEstimate(
            flops=4 * tokens * 6 * chunk * hid + 2 * tokens * hid * width,
            bytes_accessed=12 * chunk * (2 * hid + tokens) + 2 * width * (hid + tokens),
            transcendentals=tokens * hid,
        ),
    )(where, *xs, w_gate, w_up, router, *sums, ids, down_t)


def body(
    teacher_in,
    route_ids,
    router,
    w_gate,
    w_up,
    w_down,
    projection,
    student_in,
    s_gate,
    s_up,
    s_down,
):
    core = lax.axis_index("c")
    row = lax.axis_index("y")
    expert = row * NC + core
    tok_dp, width = teacher_in.shape
    tokens = route_ids.shape[0]
    sff_dev = s_gate.shape[1]
    sd_dev = student_in.shape[1]
    chunk = width // NE
    half = tokens // 2
    group = width // (ND * NY)

    part = lax.dynamic_slice_in_dim(teacher_in, expert * chunk, chunk, 1)
    sent = jnp.concatenate([part, student_in], axis=1)
    arrived = spread(sent, DP, ND).reshape(tokens, chunk + sd_dev)
    own = arrived[:, :chunk]
    student_all = arrived[:, chunk:]
    down_t = w_down[0].T

    far = [along_y(own, s) for s in range(1, NY)]
    own_other = swap_cores(own)
    far_other = [swap_cores(v) for v in far]

    def places(shift):
        r = lax.rem(row - shift + NY, NY)
        return [r * NC + core, r * NC + 1 - core]

    here = jnp.stack(places(0)).astype(jnp.int32)
    sums = expert_own(here, own, own_other, w_gate, w_up, router, tokens, chunk)
    xs, spots = [], []
    for s in (1, 3, 2):
        xs += [far[s - 1], far_other[s - 1]]
        spots += places(s)
    there = jnp.stack(spots + [row, core]).astype(jnp.int32)
    parts = expert_rest(
        there, xs, w_gate, w_up, router, sums, route_ids, down_t, tokens, chunk
    )
    keeps, gives = parts[:4], parts[4:]

    pair_sums = expert_sum(
        jnp.concatenate([dot(student_all, s_gate), dot(student_all, s_up)], axis=1), core
    )
    gate_s = pair_sums[:, :sff_dev]
    up_s = pair_sums[:, sff_dev:]
    sigma = jax.nn.sigmoid(gate_s)
    active_s = gate_s * sigma
    hidden_s = (active_s * up_s).astype(BF)
    student_part = dot(hidden_s, s_down)

    arriving = []
    mine = None
    for s in (2, 1, 3, 0):
        both = (keeps[s].astype(F32) + swap_cores(gives[s]).astype(F32)).astype(BF)
        if s:
            arriving.append(along_y(both, s))
        else:
            mine = both
    total = mine.astype(F32)
    for term in arriving:
        total = total + term.astype(F32)
    terms = exchange(total.astype(BF), DP)
    summed = jnp.sum(terms.astype(F32), axis=0).astype(BF)
    pieces = [summed] + [along_y(summed, s) for s in range(1, NY)]
    mine = jnp.concatenate(pieces, axis=0)
    other = swap_cores(mine)
    cols = lax.dynamic_slice_in_dim(projection, expert * sd_dev, sd_dev, 1)
    cols = jnp.concatenate(
        [
            lax.dynamic_slice_in_dim(cols, lax.rem(row - s + NY, NY) * group, group, 0)
            for s in range(NY)
        ],
        axis=0,
    )
    first = jnp.where(core == 0, mine, other)
    second = jnp.where(core == 0, other, mine)
    target = dot_tn(jnp.concatenate([first, second], axis=1), cols)

    out_part = (student_part - target).astype(BF)
    terms = exchange(out_part.reshape(ND, tok_dp, sd_dev), DP)
    mismatch = student_in.astype(F32) + jnp.sum(terms.astype(F32), axis=0)
    cotangent = (mismatch * (1.0 / math.sqrt(tokens))).astype(BF)
    cotangent_all = spread(cotangent, DP, ND).reshape(tokens, sd_dev)
    grad_down = dot_tn(hidden_s, cotangent_all).astype(BF)
    d_hidden = expert_sum(dot_nt(cotangent_all, s_down), core)
    d_gate = (d_hidden * up_s * sigma * (1.0 + gate_s * (1.0 - sigma))).astype(BF)
    d_up = (d_hidden * active_s).astype(BF)
    grad_gate = dot_tn(student_all, d_gate).astype(BF)
    grad_up = dot_tn(student_all, d_up).astype(BF)
    return (grad_gate, grad_up, grad_down, mismatch)


def solution(mesh):
    fine = Mesh(mesh.devices.reshape(NX, NZ, NY, NC), ("x", "z", "y", "c"))
    return jax.shard_map(
        body,
        mesh=fine,
        in_specs=(
            P(DP, None),
            P(),
            P(),
            P(EX, None, DP),
            P(EX, None, DP),
            P(EX, DP, None),
            P(DP, None),
            P(DP, EX),
            P(EX, DP),
            P(EX, DP),
            P(DP, EX),
        ),
        out_specs=(P(EX, DP), P(EX, DP), P(DP, EX), P(DP, EX)),
        check_vma=False,
    )
```

time: 251 us -> 179 us (0.71)
  blocking collectives: 110 us -> 58.5 us
  starting transfers between devices: 31.1 us -> 62.2 us
  matrix products: 24.4 us -> 4.04 us
  other arithmetic: 22 us -> 3.2 us
  local copies, waits for them, and re-layouts: 24.5 us -> 12.4 us
  Pallas kernels: 0 us -> 11.3 us
  waiting for transfers between devices: 36.9 us -> 25.7 us
    all_to_all x7 -> x3, blocking collectives: 110 us -> 58.5 us  [exchange(): return lax.all_to_all(values, axes, 0, 0, tiled=False)]
    ppermute x2 -> x13, starting transfers between devices: 3.39 us -> 30.5 us  [swap_cores(): return lax.ppermute(values, 'c', [(0, 1), (1, 0)])]
    all_to_all x5 -> x1, waiting for transfers between devices: 33.6 us -> 7.94 us  [exchange(): return lax.all_to_all(values, axes, 0, 0, tiled=False)]
    ppermute x0 -> x15, starting transfers between devices: none -> 23.3 us  [along_y(): return lax.ppermute(values, 'y', [(i, (i + shift) % NY) for i in range(NY)])]
    dot_general x11 -> x8, matrix products: 24.4 us -> 4.04 us  [the longest x4 3.04 us: dot_tn(): lax.dot_general(a, b, (((0,), (0,)), ((), ())), preferred_element_type=F32)]
    all_to_all x5 -> x1, starting transfers between devices: 27.7 us -> 8.38 us  [exchange(): return lax.all_to_all(values, axes, 0, 0, tiled=False)]
    ppermute x0 -> x15, waiting for transfers between devices: none -> 15.3 us  [along_y(): return lax.ppermute(values, 'y', [(i, (i + shift) % NY) for i in range(NY)])]
    pallas_call x0 -> x2, Pallas kernels: none -> 11.3 us  [the longest x1 8.46 us: expert_rest(): pl.pallas_call(rest_kernel, out_shape=(out,) * 8, grid_spec=pltpu.Prefetc...]
  transfers between devices with their start and end apart: 7 -> 29, of which waited for: 5 -> 12; matrix products, arithmetic and copies ran while one was open for 8% -> 6% of each run, Pallas kernels for 0% -> 2%
where the time goes in v2:
time: 179 us; the launch traced here: 178 us
  starting transfers between devices  62.2 us (35%)
  blocking collectives  58.5 us (33%)
  waiting for transfers between devices  25.7 us (14%)
  local copies, waits for them, and re-layouts  12.4 us (7%)
  Pallas kernels  11.3 us (6%)
  matrix products  4.04 us (2%)
  other arithmetic  3.2 us (2%)
    all_to_all x3, blocking collectives, exchange(): return lax.all_to_all(values, axes, 0, 0, tiled=False)  58.5 us
    ppermute x13, starting transfers between devices, swap_cores(): return lax.ppermute(values, 'c', [(0, 1), (1, 0)])  30.5 us
    ppermute x15, starting transfers between devices, along_y(): return lax.ppermute(values, 'y', [(i, (i + shift) % NY) for i in range(NY)])  23.3 us
    ppermute x15, waiting for transfers between devices, along_y(): return lax.ppermute(values, 'y', [(i, (i + shift) % NY) for i in range(NY)])  15.3 us
    unnamed x27, local copies, waits for them, and re-layouts  10.3 us
    pallas_call x1, Pallas kernels, expert_rest(): pl.pallas_call(rest_kernel, out_shape=(out,) * 8, grid_spec=pltpu.Prefetc...  8.46 us
    all_to_all x1, starting transfers between devices, exchange(): return lax.all_to_all(values, axes, 0, 0, tiled=False)  8.38 us
    all_to_all x1, waiting for transfers between devices, exchange(): return lax.all_to_all(values, axes, 0, 0, tiled=False)  7.94 us
  transfers between devices with their start and end apart: 29, of which 12 were waited for; matrix products, arithmetic and copies ran while one was open for 6% of the time, Pallas kernels for 2%

profile of v2, /device:TPU:1, one launch (start us, length us, event | category | flops | bytes accessed | tf_op | source)
XLA Modules:
  0.0 178.3 jit_solution(8878591444703241833)
XLA Ops:
  0.7 0.8 constant_dynamic-slice_fusion
  1.4 0.7 pad_maximum_fusion.5
  2.2 28.0 %all_to_all.20 = bf16[32,8,1280]{2,1,0:T(8,128)(2,1)S(1)} all-to-all(bf16[32,8,1280]{2,1,0:T(8,128)(2,1)S(1)} %broadcast_in_dim.4), channel_id=1, replica_groups=mesh['x'=4,'z'=8,'y'=4,'c'=2] {'x','z'}, dimensions={0} | all-to-all | bytes 1310720 | tf_op jit(solution)/shard_map/all_to_all | solution.py:24
  30.2 3.0 %collective-permute-start.9 = (bf16[256,768]{1,0:T(8,128)(2,1)S(1)}, bf16[256,768]{1,0:T(8,128)(2,1)S(1)}, u32[]{:S(2)}, u32[]{:S(2)}) collective-permute-start(bf16[256,768]{1,0:T(8,128)(2,1)S(1)} %slice.37.x0), channel_id=1, source_target_pairs={{0,4},{2,6},{4,0},{6,2},{1,5},{3,7},{5,1},{7,3},{8,12},{10,14},{12... | collective-permute-start | bytes 1179656 | tf_op jit(solution)/shard_map/ppermute | solution.py:36
  33.2 0.4 collective-permute-start.5
  33.6 2.3 %collective-permute-start.7 = (bf16[256,768]{1,0:T(8,128)(2,1)S(1)}, bf16[256,768]{1,0:T(8,128)(2,1)S(1)}, u32[]{:S(2)}, u32[]{:S(2)}) collective-permute-start(bf16[256,768]{1,0:T(8,128)(2,1)S(1)} %slice.37.x0), channel_id=1, source_target_pairs={{0,6},{2,0},{4,2},{6,4},{1,7},{3,1},{5,3},{7,5},{8,14},{10,8},{12,... | collective-permute-start | bytes 1179656 | tf_op jit(solution)/shard_map/ppermute | solution.py:36
  35.9 5.9 %collective-permute-start.11 = (bf16[256,768]{1,0:T(8,128)(2,1)S(1)}, bf16[256,768]{1,0:T(8,128)(2,1)}, u32[]{:S(2)}, u32[]{:S(2)}) collective-permute-start(bf16[256,768]{1,0:T(8,128)(2,1)S(1)} %slice.37.x0), channel_id=1, source_target_pairs={{0,1},{1,0},{2,3},{3,2},{4,5},{5,4},{6,7},{7,6},{8,9},{9,8},{10,11... | collective-permute-start | bytes 1179656 | tf_op jit(solution)/shard_map/ppermute | solution.py:32
  41.8 5.9 %collective-permute-start.10 = (bf16[256,768]{1,0:T(8,128)(2,1)S(1)}, bf16[256,768]{1,0:T(8,128)(2,1)}, u32[]{:S(2)}, u32[]{:S(2)}) collective-permute-start(bf16[256,768]{1,0:T(8,128)(2,1)S(1)} %collective-permute-done.9.refs_4_), channel_id=1, source_target_pairs={{0,1},{1,0},{2,3},{3,2},{4,5},{5,4},{6,7},{7,6},{8,9},{9,8},{10,11... | collective-permute-start | bytes 1179656 | tf_op jit(solution)/shard_map/ppermute | solution.py:32
  47.7 0.9 collective-permute-done.5.refs_0_
  48.6 3.2 %collective-permute-start.6 = (bf16[256,768]{1,0:T(8,128)(2,1)S(1)}, bf16[256,768]{1,0:T(8,128)(2,1)}, u32[]{:S(2)}, u32[]{:S(2)}) collective-permute-start(bf16[256,768]{1,0:T(8,128)(2,1)S(1)} %collective-permute-done.5.refs_0_), channel_id=1, source_target_pairs={{0,1},{1,0},{2,3},{3,2},{4,5},{5,4},{6,7},{7,6},{8,9},{9,8},{10,11... | collective-permute-start | bytes 1179656 | tf_op jit(solution)/shard_map/ppermute | solution.py:32
  51.8 0.4 collective-permute-start.8
  52.2 1.6 copy.17.rt.refs_8_
  53.8 4.7 %copy.16 = bf16[1,256,6144]{1,2,0:T(8,128)(2,1)} copy(bf16[1,256,6144]{2,1,0:T(8,128)(2,1)} %param.16) | data formatting | bytes 6291456 | tf_op args[5]
  58.5 0.1 copy.18.refs_12_
  58.8 1.9 %copy-done.1 = bf16[1,6144,256]{2,1,0:T(8,128)(2,1)S(1)} copy-done((bf16[1,6144,256]{2,1,0:T(8,128)(2,1)S(1)}, bf16[1,6144,256]{2,1,0:T(8,128)(2,1)}, u32[]{:S(2)}) %copy-start.1) | copy-done | bytes 3145752
  60.7 1.9 %copy-done.3 = bf16[1,6144,256]{2,1,0:T(8,128)(2,1)S(1)} copy-done((bf16[1,6144,256]{2,1,0:T(8,128)(2,1)S(1)}, bf16[1,6144,256]{2,1,0:T(8,128)(2,1)}, u32[]{:S(2)}) %copy-start.3) | copy-done | bytes 3145752
  62.6 2.8 %shard_map.138 = (f32[256,256]{1,0:T(8,128)S(1)}, f32[256,256]{1,0:T(8,128)S(1)}, f32[256,8]{1,0:T(8,128)S(1)}) custom-call(s32[2]{0:T(128)S(1)} %pad_add_fusion.where_ref, bf16[256,768]{1,0:T(8,128)(2,1)S(1)} %slice.37.x0, bf16[256,768]{1,0:T(8,128)(2,1)} %collective-permute-done.11.x1, bf16[1,6144,256]{2,1,0:T(8,128)(2,1)S(1)} %copy-done.1, ...), custom_call_target="tpu_custom_call" | custom-call | flops 402653184 | bytes 2883584 | tf_op jit(solution)/shard_map/pallas_call | solution.py:144
  65.5 8.5 %shard_map.139 = (bf16[32,48,128]{2,1,0:T(8,128)(2,1)S(1)}, bf16[32,48,128]{2,1,0:T(8,128)(2,1)S(1)}, bf16[32,48,128]{2,1,0:T(8,128)(2,1)S(1)}, bf16[32,48,128]{...) custom-call(s32[8]{0:T(128)S(1)} %stack.44.where_ref, ...), custom_call_target="tpu_custom_call" | custom-call | flops 2013265920 | bytes 13369344 | tf_op jit(solution)/shard_map/pallas_call | solution.py:186
  74.0 0.2 collective-permute-start.13
  74.2 0.3 fusion.20
  74.5 0.5 collective-permute-start.15
  74.9 0.3 fusion.22
  75.2 0.2 collective-permute-start.17
  75.4 0.4 collective-permute-start.12
  75.8 0.1 add_convert_fusion.3
  75.9 2.2 %collective-permute-start.14 = (bf16[32,48,128]{2,1,0:T(8,128)(2,1)S(1)}, bf16[32,48,128]{2,1,0:T(8,128)(2,1)S(1)}, u32[]{:S(2)}, u32[]{:S(2)}) collective-permute-start(bf16[32,48,128]{2,1,0:T(8,128)(2,1)S(1)} %add_convert_fusion.3), channel_id=1, source_target_pairs={{0,4},{2,6},{4,0},{6,2},{1,5},{3,7},{5,1},{7,3},{8,12},{10,14},{12... | collective-permute-start | bytes 1179656 | tf_op jit(solution)/shard_map/ppermute | solution.py:36
  78.1 0.1 add_convert_fusion.2
  78.2 1.1 collective-permute-start.16
  79.3 0.1 add_convert_fusion.1
  79.4 1.7 collective-permute-start.18
  81.2 1.3 collective-permute-start
  82.5 1.0 collective-permute-done
  83.6 1.7 collective-permute-start.2
  85.3 3.1 %collective-permute-done.14 = bf16[32,48,128]{2,1,0:T(8,128)(2,1)S(1)} collective-permute-done((bf16[32,48,128]{2,1,0:T(8,128)(2,1)S(1)}, bf16[32,48,128]{2,1,0:T(8,128)(2,1)S(1)}, u32[]{:S(2)}, u32[]{:S(2)}) %collective-permute-start.14) | collective-permute-done | bytes 393248 | tf_op jit(solution)/shard_map/ppermute | solution.py:36
  88.3 2.4 %collective-permute-start.3 = (bf16[128,448]{0,1:T(8,128)(2,1)S(1)}, bf16[128,448]{0,1:T(8,128)(2,1)S(1)}, u32[]{:S(2)}, u32[]{:S(2)}) collective-permute-start(bf16[128,448]{0,1:T(8,128)(2,1)S(1)} %add_convert_fusion.6), channel_id=1, source_target_pairs={{0,6},{2,0},{4,2},{6,4},{1,7},{3,1},{5,3},{7,5},{8,14},{10,8},{12,... | collective-permute-start | bytes 344072 | tf_op jit(solution)/shard_map/ppermute | solution.py:36
  90.7 6.5 %collective-permute-done.16 = bf16[32,48,128]{2,1,0:T(8,128)(2,1)S(1)} collective-permute-done((bf16[32,48,128]{2,1,0:T(8,128)(2,1)S(1)}, bf16[32,48,128]{2,1,0:T(8,128)(2,1)S(1)}, u32[]{:S(2)}, u32[]{:S(2)}) %collective-permute-start.16) | collective-permute-done | bytes 393248 | tf_op jit(solution)/shard_map/ppermute | solution.py:36
  97.2 1.0 add_convert_fusion
  98.1 8.4 %all-to-all-start.1 = ((bf16[32,48,128]{2,1,0:T(8,128)(2,1)}), bf16[32,48,128]{2,1,0:T(8,128)(2,1)S(1)}, u32[]{:S(2)}, u32[]{:S(2)}) async-start(bf16[32,48,128]{2,1,0:T(8,128)(2,1)} %add_convert_fusion), calls=%async_computation.1 | async-start | bytes 786432 | tf_op jit(solution)/shard_map/all_to_all | solution.py:24
  106.7 1.4 collective-permute-start.4
  108.2 1.1 fusion.36
  109.4 7.9 %all-to-all-done.1 = bf16[32,48,128]{2,1,0:T(8,128)(2,1)S(1)} async-done(((bf16[32,48,128]{2,1,0:T(8,128)(2,1)}), bf16[32,48,128]{2,1,0:T(8,128)(2,1)S(1)}, u32[]{:S(2)}, u32[]{:S(2)}) %all-to-all-start.1) | async-done | bytes 393248 | tf_op jit(solution)/shard_map/all_to_all | solution.py:24
  117.4 2.6 %collective-permute-start.19 = (bf16[48,128]{1,0:T(8,128)(2,1)S(1)}, bf16[48,128]{1,0:T(8,128)(2,1)S(1)}, u32[]{:S(2)}, u32[]{:S(2)}) collective-permute-start(bf16[48,128]{1,0:T(8,128)(2,1)S(1)} %reduce_sum.21), channel_id=1, source_target_pairs={{0,2},{2,4},{4,6},{6,0},{1,3},{3,5},{5,7},{7,1},{8,10},{10,12},{12... | collective-permute-start | bytes 36872 | tf_op jit(solution)/shard_map/ppermute | solution.py:36
  119.9 2.1 %collective-permute-start.20 = (bf16[48,128]{1,0:T(8,128)(2,1)S(1)}, bf16[48,128]{1,0:T(8,128)(2,1)S(1)}, u32[]{:S(2)}, u32[]{:S(2)}) collective-permute-start(bf16[48,128]{1,0:T(8,128)(2,1)S(1)} %reduce_sum.21), channel_id=1, source_target_pairs={{0,4},{2,6},{4,0},{6,2},{1,5},{3,7},{5,1},{7,3},{8,12},{10,14},{12... | collective-permute-start | bytes 36872 | tf_op jit(solution)/shard_map/ppermute | solution.py:36
  122.1 0.4 collective-permute-start.21
  122.5 1.5 collective-permute-done.20
  124.0 0.6 collective-permute-done.21
  124.6 5.9 %collective-permute-start.22 = (bf16[192,128]{1,0:T(8,128)(2,1)S(1)}, bf16[192,128]{1,0:T(8,128)(2,1)S(1)}, u32[]{:S(2)}, u32[]{:S(2)}) collective-permute-start(bf16[192,128]{1,0:T(8,128)(2,1)S(1)} %pad_maximum_fusion.4), channel_id=1, source_target_pairs={{0,1},{1,0},{2,3},{3,2},{4,5},{5,4},{6,7},{7,6},{8,9},{9,8},{10,11... | collective-permute-start | bytes 147464 | tf_op jit(solution)/shard_map/ppermute | solution.py:32
  130.5 0.2 fusion.37
  130.7 0.6 collective-permute-done.22
  131.4 0.2 fusion.1
  131.6 14.3 %all_to_all.21 = bf16[32,8,512]{2,1,0:T(8,128)(2,1)S(1)} all-to-all(bf16[32,8,512]{2,1,0:T(8,128)(2,1)S(1)} %fusion.1), channel_id=1, replica_groups=mesh['x'=4,'z'=8,'y'=4,'c'=2] {'x','z'}, dimensions={0} | all-to-all | bytes 524288 | tf_op jit(solution)/shard_map/all_to_all | solution.py:24
  146.0 0.6 multiply_convert_fusion.1
  146.6 16.2 %all_to_all.22 = bf16[32,8,512]{2,1,0:T(8,128)(2,1)S(1)} all-to-all(bf16[32,8,512]{2,1,0:T(8,128)(2,1)S(1)} %broadcast_in_dim.5), channel_id=1, replica_groups=mesh['x'=4,'z'=8,'y'=4,'c'=2] {'x','z'}, dimensions={0} | all-to-all | bytes 524288 | tf_op jit(solution)/shard_map/all_to_all | solution.py:24
  162.8 0.3 fusion.3
  163.1 3.7 %collective-permute-start.23 = (bf16[128,224]{0,1:T(8,128)(2,1)S(1)}, bf16[128,224]{0,1:T(8,128)(2,1)S(1)}, u32[]{:S(2)}, u32[]{:S(2)}) collective-permute-start(bf16[128,224]{0,1:T(8,128)(2,1)S(1)} %select_convert_fusion.1), channel_id=1, source_target_pairs={{0,1},{1,0},{2,3},{3,2},{4,5},{5,4},{6,7},{7,6},{8,9},{9,8},{10,11... | collective-permute-start | bytes 172040 | tf_op jit(solution)/shard_map/ppermute | solution.py:32
  166.7 0.9 collective-permute-done.23
  167.7 2.5 %collective-permute-start.25 = (bf16[128,224]{0,1:T(8,128)(2,1)S(1)}, bf16[128,224]{0,1:T(8,128)(2,1)S(1)}, u32[]{:S(2)}, u32[]{:S(2)}) collective-permute-start(bf16[128,224]{0,1:T(8,128)(2,1)S(1)} %add_convert_fusion.8), channel_id=1, source_target_pairs={{0,4},{2,6},{4,0},{6,2},{1,5},{3,7},{5,1},{7,3},{8,12},{10,14},{12... | collective-permute-start | bytes 172040 | tf_op jit(solution)/shard_map/ppermute | solution.py:36
  170.2 0.9 collective-permute-start.26
  171.1 1.7 collective-permute-done.24
  172.8 1.0 collective-permute-done.26
  173.9 1.5 collective-permute-start.27
  175.4 0.9 convolution_convert_fusion.2
  176.4 0.9 convolution_convert_fusion
  177.3 1.0 convolution_convert_fusion.1
  (61 shorter events, 1.2 us)
Async XLA Ops:
  0.6 129.8 %copy-start = (bf16[224,512]{1,0:T(8,128)(2,1)S(1)}, bf16[224,512]{1,0:T(8,128)(2,1)}, u32[]{:S(2)}) copy-start(bf16[224,512]{1,0:T(8,128)(2,1)} %param.21) | copy-start | bytes 688132
  30.2 22.0 %copy-start.5 = (bf16[32,8,1280]{2,1,0:T(8,128)(2,1)}, bf16[32,8,1280]{2,1,0:T(8,128)(2,1)S(1)}, u32[]{:S(2)}) copy-start(bf16[32,8,1280]{2,1,0:T(8,128)(2,1)S(1)} %all_to_all.20) | copy-start | bytes 1966084
  30.2 11.5 %collective-permute-start.9 = (bf16[256,768]{1,0:T(8,128)(2,1)S(1)}, bf16[256,768]{1,0:T(8,128)(2,1)S(1)}, u32[]{:S(2)}, u32[]{:S(2)}) collective-permute-start(bf16[256,768]{1,0:T(8,128)(2,1)S(1)} %slice.37.x0), channel_id=1, source_target_pairs={{0,4},{2,6},{4,0},{6,2},{1,5},{3,7},{5,1},{7,3},{8,12},{10,14},{12... | collective-permute-start | bytes 1179656 | tf_op jit(solution)/shard_map/ppermute | solution.py:36
  33.2 15.3 %collective-permute-start.5 = (bf16[256,768]{1,0:T(8,128)(2,1)S(1)}, bf16[256,768]{1,0:T(8,128)(2,1)S(1)}, u32[]{:S(2)}, u32[]{:S(2)}) collective-permute-start(bf16[256,768]{1,0:T(8,128)(2,1)S(1)} %slice.37.x0), channel_id=1, source_target_pairs={{0,2},{2,4},{4,6},{6,0},{1,3},{3,5},{5,7},{7,1},{8,10},{10,12},{12... | collective-permute-start | bytes 1179656 | tf_op jit(solution)/shard_map/ppermute | solution.py:36
  33.6 18.2 %collective-permute-start.7 = (bf16[256,768]{1,0:T(8,128)(2,1)S(1)}, bf16[256,768]{1,0:T(8,128)(2,1)S(1)}, u32[]{:S(2)}, u32[]{:S(2)}) collective-permute-start(bf16[256,768]{1,0:T(8,128)(2,1)S(1)} %slice.37.x0), channel_id=1, source_target_pairs={{0,6},{2,0},{4,2},{6,4},{1,7},{3,1},{5,3},{7,5},{8,14},{10,8},{12,... | collective-permute-start | bytes 1179656 | tf_op jit(solution)/shard_map/ppermute | solution.py:36
  35.9 22.9 %collective-permute-start.11 = (bf16[256,768]{1,0:T(8,128)(2,1)S(1)}, bf16[256,768]{1,0:T(8,128)(2,1)}, u32[]{:S(2)}, u32[]{:S(2)}) collective-permute-start(bf16[256,768]{1,0:T(8,128)(2,1)S(1)} %slice.37.x0), channel_id=1, source_target_pairs={{0,1},{1,0},{2,3},{3,2},{4,5},{5,4},{6,7},{7,6},{8,9},{9,8},{10,11... | collective-permute-start | bytes 1179656 | tf_op jit(solution)/shard_map/ppermute | solution.py:32
  41.8 23.6 %collective-permute-start.10 = (bf16[256,768]{1,0:T(8,128)(2,1)S(1)}, bf16[256,768]{1,0:T(8,128)(2,1)}, u32[]{:S(2)}, u32[]{:S(2)}) collective-permute-start(bf16[256,768]{1,0:T(8,128)(2,1)S(1)} %collective-permute-done.9.refs_4_), channel_id=1, source_target_pairs={{0,1},{1,0},{2,3},{3,2},{4,5},{5,4},{6,7},{7,6},{8,9},{9,8},{10,11... | collective-permute-start | bytes 1179656 | tf_op jit(solution)/shard_map/ppermute | solution.py:32
  48.6 16.8 %collective-permute-start.6 = (bf16[256,768]{1,0:T(8,128)(2,1)S(1)}, bf16[256,768]{1,0:T(8,128)(2,1)}, u32[]{:S(2)}, u32[]{:S(2)}) collective-permute-start(bf16[256,768]{1,0:T(8,128)(2,1)S(1)} %collective-permute-done.5.refs_0_), channel_id=1, source_target_pairs={{0,1},{1,0},{2,3},{3,2},{4,5},{5,4},{6,7},{7,6},{8,9},{9,8},{10,11... | collective-permute-start | bytes 1179656 | tf_op jit(solution)/shard_map/ppermute | solution.py:32
  51.8 13.6 %collective-permute-start.8 = (bf16[256,768]{1,0:T(8,128)(2,1)S(1)}, bf16[256,768]{1,0:T(8,128)(2,1)}, u32[]{:S(2)}, u32[]{:S(2)}) collective-permute-start(bf16[256,768]{1,0:T(8,128)(2,1)S(1)} %collective-permute-done.7.refs_2_), channel_id=1, source_target_pairs={{0,1},{1,0},{2,3},{3,2},{4,5},{5,4},{6,7},{7,6},{8,9},{9,8},{10,11... | collective-permute-start | bytes 1179656 | tf_op jit(solution)/shard_map/ppermute | solution.py:32
  53.8 4.7 %copy-start.11 = (s32[256,2]{0,1:T(2,128)S(1)}, s32[256,2]{0,1:T(2,128)}, u32[]{:S(2)}) copy-start(s32[256,2]{0,1:T(2,128)} %param.12) | copy-start | bytes 6148
  58.8 1.9 %copy-start.1 = (bf16[1,6144,256]{2,1,0:T(8,128)(2,1)S(1)}, bf16[1,6144,256]{2,1,0:T(8,128)(2,1)}, u32[]{:S(2)}) copy-start(bf16[1,6144,256]{2,1,0:T(8,128)(2,1)} %refs_6_.1) | copy-start | bytes 9437188
  60.7 1.9 %copy-start.3 = (bf16[1,6144,256]{2,1,0:T(8,128)(2,1)S(1)}, bf16[1,6144,256]{2,1,0:T(8,128)(2,1)}, u32[]{:S(2)}) copy-start(bf16[1,6144,256]{2,1,0:T(8,128)(2,1)} %refs_7_.1) | copy-start | bytes 9437188
  62.6 2.9 %copy-start.2 = (bf16[1,6144,256]{2,1,0:T(8,128)(2,1)S(1)}, bf16[1,6144,256]{2,1,0:T(8,128)(2,1)}, u32[]{:S(2)}) copy-start(bf16[1,6144,256]{2,1,0:T(8,128)(2,1)} %refs_6_.1) | copy-start | bytes 9437188
  62.6 3.0 %copy-start.4 = (bf16[1,256,6144]{1,2,0:T(8,128)(2,1)S(1)}, bf16[1,256,6144]{1,2,0:T(8,128)(2,1)}, u32[]{:S(2)}) copy-start(bf16[1,256,6144]{1,2,0:T(8,128)(2,1)} %copy.16) | copy-start | bytes 9437188
  65.5 8.7 %copy-start.6 = (bf16[32,8,1280]{2,1,0:T(8,128)(2,1)S(1)}, bf16[32,8,1280]{2,1,0:T(8,128)(2,1)}, u32[]{:S(2)}) copy-start(bf16[32,8,1280]{2,1,0:T(8,128)(2,1)} %copy-done.5) | copy-start | bytes 1966084
  65.5 8.7 %copy-start.8 = (bf16[512,224]{0,1:T(8,128)(2,1)S(1)}, bf16[512,224]{0,1:T(8,128)(2,1)}, u32[]{:S(2)}) copy-start(bf16[512,224]{0,1:T(8,128)(2,1)} %param.20) | copy-start | bytes 688132
  65.5 9.4 %copy-start.9 = (bf16[512,224]{0,1:T(8,128)(2,1)S(1)}, bf16[512,224]{0,1:T(8,128)(2,1)}, u32[]{:S(2)}) copy-start(bf16[512,224]{0,1:T(8,128)(2,1)} %param.19) | copy-start | bytes 688132
  74.0 1.8 %collective-permute-start.13 = (bf16[32,48,128]{2,1,0:T(8,128)(2,1)S(1)}, bf16[32,48,128]{2,1,0:T(8,128)(2,1)S(1)}, u32[]{:S(2)}, u32[]{:S(2)}) collective-permute-start(bf16[32,48,128]{2,1,0:T(8,128)(2,1)S(1)} %get-tuple-element.21), channel_id=1, source_target_pairs={{0,1},{1,0},{2,3},{3,2},{4,5},{5,4},{6,7},{7,6},{8,9},{9,8},{10,11... | collective-permute-start | bytes 1179656 | tf_op jit(solution)/shard_map/ppermute | solution.py:32
  74.5 3.6 %collective-permute-start.15 = (bf16[32,48,128]{2,1,0:T(8,128)(2,1)S(1)}, bf16[32,48,128]{2,1,0:T(8,128)(2,1)S(1)}, u32[]{:S(2)}, u32[]{:S(2)}) collective-permute-start(bf16[32,48,128]{2,1,0:T(8,128)(2,1)S(1)} %get-tuple-element.23), channel_id=1, source_target_pairs={{0,1},{1,0},{2,3},{3,2},{4,5},{5,4},{6,7},{7,6},{8,9},{9,8},{10,11... | collective-permute-start | bytes 1179656 | tf_op jit(solution)/shard_map/ppermute | solution.py:32
  75.2 4.1 %collective-permute-start.17 = (bf16[32,48,128]{2,1,0:T(8,128)(2,1)S(1)}, bf16[32,48,128]{2,1,0:T(8,128)(2,1)S(1)}, u32[]{:S(2)}, u32[]{:S(2)}) collective-permute-start(bf16[32,48,128]{2,1,0:T(8,128)(2,1)S(1)} %get-tuple-element.25), channel_id=1, source_target_pairs={{0,1},{1,0},{2,3},{3,2},{4,5},{5,4},{6,7},{7,6},{8,9},{9,8},{10,11... | collective-permute-start | bytes 1179656 | tf_op jit(solution)/shard_map/ppermute | solution.py:32
  75.4 8.2 %collective-permute-start.12 = (bf16[32,48,128]{2,1,0:T(8,128)(2,1)S(1)}, bf16[32,48,128]{2,1,0:T(8,128)(2,1)S(1)}, u32[]{:S(2)}, u32[]{:S(2)}) collective-permute-start(bf16[32,48,128]{2,1,0:T(8,128)(2,1)S(1)} %get-tuple-element.19), channel_id=1, source_target_pairs={{0,1},{1,0},{2,3},{3,2},{4,5},{5,4},{6,7},{7,6},{8,9},{9,8},{10,11... | collective-permute-start | bytes 1179656 | tf_op jit(solution)/shard_map/ppermute | solution.py:32
  75.9 12.4 %collective-permute-start.14 = (bf16[32,48,128]{2,1,0:T(8,128)(2,1)S(1)}, bf16[32,48,128]{2,1,0:T(8,128)(2,1)S(1)}, u32[]{:S(2)}, u32[]{:S(2)}) collective-permute-start(bf16[32,48,128]{2,1,0:T(8,128)(2,1)S(1)} %add_convert_fusion.3), channel_id=1, source_target_pairs={{0,4},{2,6},{4,0},{6,2},{1,5},{3,7},{5,1},{7,3},{8,12},{10,14},{12... | collective-permute-start | bytes 1179656 | tf_op jit(solution)/shard_map/ppermute | solution.py:36
  78.2 19.0 %collective-permute-start.16 = (bf16[32,48,128]{2,1,0:T(8,128)(2,1)S(1)}, bf16[32,48,128]{2,1,0:T(8,128)(2,1)S(1)}, u32[]{:S(2)}, u32[]{:S(2)}) collective-permute-start(bf16[32,48,128]{2,1,0:T(8,128)(2,1)S(1)} %add_convert_fusion.2), channel_id=1, source_target_pairs={{0,2},{2,4},{4,6},{6,0},{1,3},{3,5},{5,7},{7,1},{8,10},{10,12},{12... | collective-permute-start | bytes 1179656 | tf_op jit(solution)/shard_map/ppermute | solution.py:36
  79.4 17.7 %collective-permute-start.18 = (bf16[32,48,128]{2,1,0:T(8,128)(2,1)S(1)}, bf16[32,48,128]{2,1,0:T(8,128)(2,1)S(1)}, u32[]{:S(2)}, u32[]{:S(2)}) collective-permute-start(bf16[32,48,128]{2,1,0:T(8,128)(2,1)S(1)} %add_convert_fusion.1), channel_id=1, source_target_pairs={{0,6},{2,0},{4,2},{6,4},{1,7},{3,1},{5,3},{7,5},{8,14},{10,8},{12,... | collective-permute-start | bytes 1179656 | tf_op jit(solution)/shard_map/ppermute | solution.py:36
  81.2 2.3 %collective-permute-start = (bf16[128,448]{0,1:T(8,128)(2,1)S(1)}, bf16[128,448]{0,1:T(8,128)(2,1)S(1)}, u32[]{:S(2)}, u32[]{:S(2)}) collective-permute-start(bf16[128,448]{0,1:T(8,128)(2,1)S(1)} %select_convert_fusion), channel_id=1, source_target_pairs={{0,1},{1,0},{2,3},{3,2},{4,5},{5,4},{6,7},{7,6},{8,9},{9,8},{10,11... | collective-permute-start | bytes 344072 | tf_op jit(solution)/shard_map/ppermute | solution.py:32
  83.5 23.1 %collective-permute-start.1 = (bf16[128,448]{0,1:T(8,128)(2,1)S(1)}, bf16[128,448]{0,1:T(8,128)(2,1)S(1)}, u32[]{:S(2)}, u32[]{:S(2)}) collective-permute-start(bf16[128,448]{0,1:T(8,128)(2,1)S(1)} %add_convert_fusion.6), channel_id=1, source_target_pairs={{0,2},{2,4},{4,6},{6,0},{1,3},{3,5},{5,7},{7,1},{8,10},{10,12},{12... | collective-permute-start | bytes 344072 | tf_op jit(solution)/shard_map/ppermute | solution.py:36
  83.6 23.0 %collective-permute-start.2 = (bf16[128,448]{0,1:T(8,128)(2,1)S(1)}, bf16[128,448]{0,1:T(8,128)(2,1)S(1)}, u32[]{:S(2)}, u32[]{:S(2)}) collective-permute-start(bf16[128,448]{0,1:T(8,128)(2,1)S(1)} %add_convert_fusion.6), channel_id=1, source_target_pairs={{0,4},{2,6},{4,0},{6,2},{1,5},{3,7},{5,1},{7,3},{8,12},{10,14},{12... | collective-permute-start | bytes 344072 | tf_op jit(solution)/shard_map/ppermute | solution.py:36
  88.3 18.3 %collective-permute-start.3 = (bf16[128,448]{0,1:T(8,128)(2,1)S(1)}, bf16[128,448]{0,1:T(8,128)(2,1)S(1)}, u32[]{:S(2)}, u32[]{:S(2)}) collective-permute-start(bf16[128,448]{0,1:T(8,128)(2,1)S(1)} %add_convert_fusion.6), channel_id=1, source_target_pairs={{0,6},{2,0},{4,2},{6,4},{1,7},{3,1},{5,3},{7,5},{8,14},{10,8},{12,... | collective-permute-start | bytes 344072 | tf_op jit(solution)/shard_map/ppermute | solution.py:36
  98.1 19.2 %all-to-all-start.1 = ((bf16[32,48,128]{2,1,0:T(8,128)(2,1)}), bf16[32,48,128]{2,1,0:T(8,128)(2,1)S(1)}, u32[]{:S(2)}, u32[]{:S(2)}) async-start(bf16[32,48,128]{2,1,0:T(8,128)(2,1)} %add_convert_fusion), calls=%async_computation.1 | async-start | bytes 786432 | tf_op jit(solution)/shard_map/all_to_all | solution.py:24
  106.5 39.4 %copy-start.10 = (bf16[8,512]{1,0:T(8,128)(2,1)S(1)}, bf16[8,512]{1,0:T(8,128)(2,1)}, u32[]{:S(2)}) copy-start(bf16[8,512]{1,0:T(8,128)(2,1)} %param.18) | copy-start | bytes 24580
  106.7 2.6 %collective-permute-start.4 = (bf16[128,448]{0,1:T(8,128)(2,1)S(1)}, bf16[128,448]{0,1:T(8,128)(2,1)S(1)}, u32[]{:S(2)}, u32[]{:S(2)}) collective-permute-start(bf16[128,448]{0,1:T(8,128)(2,1)S(1)} %add_convert_fusion.5), channel_id=1, source_target_pairs={{0,1},{1,0},{2,3},{3,2},{4,5},{5,4},{6,7},{7,6},{8,9},{9,8},{10,11... | collective-permute-start | bytes 344072 | tf_op jit(solution)/shard_map/ppermute | solution.py:32
  117.4 5.1 %collective-permute-start.19 = (bf16[48,128]{1,0:T(8,128)(2,1)S(1)}, bf16[48,128]{1,0:T(8,128)(2,1)S(1)}, u32[]{:S(2)}, u32[]{:S(2)}) collective-permute-start(bf16[48,128]{1,0:T(8,128)(2,1)S(1)} %reduce_sum.21), channel_id=1, source_target_pairs={{0,2},{2,4},{4,6},{6,0},{1,3},{3,5},{5,7},{7,1},{8,10},{10,12},{12... | collective-permute-start | bytes 36872 | tf_op jit(solution)/shard_map/ppermute | solution.py:36
  119.9 4.0 %collective-permute-start.20 = (bf16[48,128]{1,0:T(8,128)(2,1)S(1)}, bf16[48,128]{1,0:T(8,128)(2,1)S(1)}, u32[]{:S(2)}, u32[]{:S(2)}) collective-permute-start(bf16[48,128]{1,0:T(8,128)(2,1)S(1)} %reduce_sum.21), channel_id=1, source_target_pairs={{0,4},{2,6},{4,0},{6,2},{1,5},{3,7},{5,1},{7,3},{8,12},{10,14},{12... | collective-permute-start | bytes 36872 | tf_op jit(solution)/shard_map/ppermute | solution.py:36
  122.1 2.5 %collective-permute-start.21 = (bf16[48,128]{1,0:T(8,128)(2,1)S(1)}, bf16[48,128]{1,0:T(8,128)(2,1)S(1)}, u32[]{:S(2)}, u32[]{:S(2)}) collective-permute-start(bf16[48,128]{1,0:T(8,128)(2,1)S(1)} %reduce_sum.21), channel_id=1, source_target_pairs={{0,6},{2,0},{4,2},{6,4},{1,7},{3,1},{5,3},{7,5},{8,14},{10,8},{12,... | collective-permute-start | bytes 36872 | tf_op jit(solution)/shard_map/ppermute | solution.py:36
  122.5 53.9 %copy-start.7 = (bf16[32,8,1280]{2,1,0:T(8,128)(2,1)S(1)}, bf16[32,8,1280]{2,1,0:T(8,128)(2,1)}, u32[]{:S(2)}) copy-start(bf16[32,8,1280]{2,1,0:T(8,128)(2,1)} %copy-done.5) | copy-start | bytes 1966084
  124.6 6.7 %collective-permute-start.22 = (bf16[192,128]{1,0:T(8,128)(2,1)S(1)}, bf16[192,128]{1,0:T(8,128)(2,1)S(1)}, u32[]{:S(2)}, u32[]{:S(2)}) collective-permute-start(bf16[192,128]{1,0:T(8,128)(2,1)S(1)} %pad_maximum_fusion.4), channel_id=1, source_target_pairs={{0,1},{1,0},{2,3},{3,2},{4,5},{5,4},{6,7},{7,6},{8,9},{9,8},{10,11... | collective-permute-start | bytes 147464 | tf_op jit(solution)/shard_map/ppermute | solution.py:32
  163.1 4.6 %collective-permute-start.23 = (bf16[128,224]{0,1:T(8,128)(2,1)S(1)}, bf16[128,224]{0,1:T(8,128)(2,1)S(1)}, u32[]{:S(2)}, u32[]{:S(2)}) collective-permute-start(bf16[128,224]{0,1:T(8,128)(2,1)S(1)} %select_convert_fusion.1), channel_id=1, source_target_pairs={{0,1},{1,0},{2,3},{3,2},{4,5},{5,4},{6,7},{7,6},{8,9},{9,8},{10,11... | collective-permute-start | bytes 172040 | tf_op jit(solution)/shard_map/ppermute | solution.py:32
  167.6 5.1 %collective-permute-start.24 = (bf16[128,224]{0,1:T(8,128)(2,1)S(1)}, bf16[128,224]{0,1:T(8,128)(2,1)S(1)}, u32[]{:S(2)}, u32[]{:S(2)}) collective-permute-start(bf16[128,224]{0,1:T(8,128)(2,1)S(1)} %add_convert_fusion.8), channel_id=1, source_target_pairs={{0,2},{2,4},{4,6},{6,0},{1,3},{3,5},{5,7},{7,1},{8,10},{10,12},{12... | collective-permute-start | bytes 172040 | tf_op jit(solution)/shard_map/ppermute | solution.py:36
  167.7 5.1 %collective-permute-start.25 = (bf16[128,224]{0,1:T(8,128)(2,1)S(1)}, bf16[128,224]{0,1:T(8,128)(2,1)S(1)}, u32[]{:S(2)}, u32[]{:S(2)}) collective-permute-start(bf16[128,224]{0,1:T(8,128)(2,1)S(1)} %add_convert_fusion.8), channel_id=1, source_target_pairs={{0,4},{2,6},{4,0},{6,2},{1,5},{3,7},{5,1},{7,3},{8,12},{10,14},{12... | collective-permute-start | bytes 172040 | tf_op jit(solution)/shard_map/ppermute | solution.py:36
  170.2 3.6 %collective-permute-start.26 = (bf16[128,224]{0,1:T(8,128)(2,1)S(1)}, bf16[128,224]{0,1:T(8,128)(2,1)S(1)}, u32[]{:S(2)}, u32[]{:S(2)}) collective-permute-start(bf16[128,224]{0,1:T(8,128)(2,1)S(1)} %add_convert_fusion.8), channel_id=1, source_target_pairs={{0,6},{2,0},{4,2},{6,4},{1,7},{3,1},{5,3},{7,5},{8,14},{10,8},{12,... | collective-permute-start | bytes 172040 | tf_op jit(solution)/shard_map/ppermute | solution.py:36
  173.9 2.4 %collective-permute-start.27 = (bf16[128,224]{0,1:T(8,128)(2,1)S(1)}, bf16[128,224]{0,1:T(8,128)(2,1)S(1)}, u32[]{:S(2)}, u32[]{:S(2)}) collective-permute-start(bf16[128,224]{0,1:T(8,128)(2,1)S(1)} %add_convert_fusion.7), channel_id=1, source_target_pairs={{0,1},{1,0},{2,3},{3,2},{4,5},{5,4},{6,7},{7,6},{8,9},{9,8},{10,11... | collective-permute-start | bytes 172040 | tf_op jit(solution)/shard_map/ppermute | solution.py:32

commit v3 on v1

v3 whole, which is shorter than its diff:
```python
import math

import jax
import jax.numpy as jnp
from jax import lax
from jax.experimental import pallas as pl
from jax.experimental.pallas import tpu as pltpu
from jax.sharding import Mesh
from jax.sharding import PartitionSpec as P

NX, NZ, NY, NC = 4, 8, 4, 2
ND = NX * NZ
NE = NY * NC
DP = ("x", "z")
EX = ("y", "c")
BF = jnp.bfloat16
F32 = jnp.float32
VMEM_BYTES = 60 * 1024 * 1024
STEPS = 4


def exchange(values, axes):
    return lax.all_to_all(values, axes, 0, 0, tiled=False)


def spread(values, axes, count):
    return exchange(jnp.broadcast_to(values[None], (count,) + values.shape), axes)


def swap_cores(values):
    return lax.ppermute(values, "c", [(0, 1), (1, 0)])


def along_y(values, shift):
    return lax.ppermute(values, "y", [(i, (i + shift) % NY) for i in range(NY)])


def core_sum(values, core):
    half = values.shape[0] // 2
    low, high = values[:half], values[half:]
    give = jnp.where(core == 0, high, low).astype(BF)
    keep = jnp.where(core == 0, low, high)
    return (keep + swap_cores(give).astype(F32)).astype(BF)


def row_sum(mine, beside):
    others = [along_y(mine, s) for s in range(1, NY)]
    others, beside = lax.optimization_barrier((others, beside))
    total = mine.astype(F32)
    for term in others:
        total = total + term.astype(F32)
    total = total.astype(BF)
    return total, swap_cores(total), beside


def in_order(mine, other, core):
    first = jnp.where(core == 0, mine, other)
    second = jnp.where(core == 0, other, mine)
    return jnp.concatenate([first, second], axis=0)


def dot(a, b):
    return jnp.dot(a, b, preferred_element_type=F32)


def dot_tn(a, b):
    return lax.dot_general(a, b, (((0,), (0,)), ((), ())), preferred_element_type=F32)


def dot_nt(a, b):
    return lax.dot_general(a, b, (((1,), (1,)), ((), ())), preferred_element_type=F32)


def two_parts(core, chunk):
    mine = pl.multiple_of(core * chunk, 256)
    rest = pl.multiple_of((1 - core) * chunk, 256)
    return pl.ds(mine, chunk), pl.ds(rest, chunk)


def weight_copies(where_ref, j, hbm_refs, buffers, sems):
    depth = buffers[0].shape[1]
    start = pl.multiple_of(where_ref[j] * depth, 512)
    return [
        pltpu.make_async_copy(src.at[0, pl.ds(start, depth), :], buf.at[j], sems.at[i, j])
        for i, (src, buf) in enumerate(zip(hbm_refs, buffers))
    ]


def products(a, b, spot, wg, wu, rt, core):
    chunk = a.shape[1]
    mine, rest = two_parts(core, chunk)
    base = spot * (2 * chunk)
    r0 = rt[:, pl.ds(pl.multiple_of(base + core * chunk, 256), chunk)]
    r1 = rt[:, pl.ds(pl.multiple_of(base + (1 - core) * chunk, 256), chunk)]
    return (
        dot(a, wg[mine, :]) + dot(b, wg[rest, :]),
        dot(a, wu[mine, :]) + dot(b, wu[rest, :]),
        dot_nt(a, r0) + dot_nt(b, r1),
    )


def expert_kernel(where, *refs):
    xs = refs[:8]
    wg, wu, rt, ids, wd = refs[8:13]
    keeps = refs[13:17]
    gives = refs[17:21]
    gbuf, ubuf, dbuf, hidden, block, sems, dsems = refs[21:]
    row = where[0]
    core = where[NY]
    copies = [weight_copies(where, j, (wg, wu), (gbuf, ubuf), sems) for j in range(NY)]
    rows = dbuf.shape[1]
    downs = [
        pltpu.make_async_copy(wd.at[pl.ds(j * rows, rows), :], dbuf.at[j], dsems.at[j])
        for j in range(STEPS)
    ]
    for group in copies:
        for copy in group:
            copy.start()
    for copy in downs:
        copy.start()
    g = u = logits = None
    for j in range(NY):
        for copy in copies[j]:
            copy.wait()
        gate, up, logit = products(
            xs[2 * j][...], xs[2 * j + 1][...], where[j], gbuf.at[j], ubuf.at[j], rt, core
        )
        if j == 0:
            g, u, logits = gate, up, logit
        else:
            g, u, logits = g + gate, u + up, logits + logit

    expert = row * NC + core
    lane = lax.broadcasted_iota(jnp.int32, logits.shape, 1)
    first = ids[:, 0:1]
    second = ids[:, 1:2]
    l0 = jnp.sum(jnp.where(lane == first, logits, 0.0), axis=1, keepdims=True)
    l1 = jnp.sum(jnp.where(lane == second, logits, 0.0), axis=1, keepdims=True)
    gate = jnp.where(first == expert, jax.nn.sigmoid(l0 - l1), 0.0) + jnp.where(
        second == expert, jax.nn.sigmoid(l1 - l0), 0.0
    )
    named = (first == expert) | (second == expert)
    active = jnp.where(named, g * jax.nn.sigmoid(g) * u * gate, 0.0)
    half = active.shape[0] // 2
    low = active[:half]
    high = active[half:]
    hidden[:half] = jnp.where(core == 0, low, high).astype(BF)
    hidden[half:] = jnp.where(core == 0, high, low).astype(BF)

    count = block.shape[0]
    for j in range(STEPS):
        downs[j].wait()
        res = dot_nt(dbuf[j], hidden[...])
        block[...] = res.astype(BF).reshape(block.shape)
        for s in range(NY):
            at = lax.rem(row + s, NY)
            keeps[s][j * count : (j + 1) * count] = block[:, at, :, :half]
            gives[s][j * count : (j + 1) * count] = block[:, at, :, half:]


IN_SMEM = pl.BlockSpec(memory_space=pltpu.SMEM)
IN_VMEM = pl.BlockSpec(memory_space=pltpu.VMEM)
IN_HBM = pl.BlockSpec(memory_space=pltpu.HBM)


def expert_products(where, xs, w_gate, w_up, router_t, ids, down_t, tokens, chunk):
    hid = w_gate.shape[2]
    width = down_t.shape[0]
    group = width // (ND * NY)
    out = jax.ShapeDtypeStruct((ND, group, tokens // 2), BF)
    return pl.pallas_call(
        expert_kernel,
        out_shape=(out,) * 8,
        in_specs=[IN_SMEM]
        + [IN_VMEM] * 8
        + [IN_HBM, IN_HBM, IN_VMEM, IN_VMEM, IN_HBM],
        out_specs=[IN_VMEM] * 8,
        scratch_shapes=[
            pltpu.VMEM((NY, 2 * chunk, hid), BF),
            pltpu.VMEM((NY, 2 * chunk, hid), BF),
            pltpu.VMEM((STEPS, width // STEPS, hid), BF),
            pltpu.VMEM((tokens, hid), BF),
            pltpu.VMEM((ND // STEPS, NY, group, tokens), BF),
            pltpu.SemaphoreType.DMA((2, NY)),
            pltpu.SemaphoreType.DMA((STEPS,)),
        ],
        compiler_params=pltpu.CompilerParams(vmem_limit_bytes=VMEM_BYTES),
        cost_estimate=pl.CostEstimate(
            flops=4 * tokens * NE * chunk * hid + 2 * tokens * hid * width,
            bytes_accessed=2 * NE * chunk * (2 * hid + tokens) + 2 * width * (hid + tokens),
            transcendentals=tokens * hid,
        ),
    )(where, *xs, w_gate, w_up, router_t, ids, down_t)


def grad_kernel(core_ref, own, other, gate, up, student, gate_grad, up_grad):
    half = own.shape[0]
    core = core_ref[0]
    total_gate = None
    for side, d_ref in enumerate((own, other)):
        at = core if side == 0 else 1 - core
        rows = pl.ds(pl.multiple_of(at * half, 128), half)
        d_hidden = d_ref[...].astype(F32)
        g = gate[rows, :]
        sigma = jax.nn.sigmoid(g)
        d_gate = (d_hidden * up[rows, :] * sigma * (1.0 + g * (1.0 - sigma))).astype(BF)
        d_up = (d_hidden * (g * sigma)).astype(BF)
        tokens = student[rows, :]
        if side == 0:
            total_gate = dot_tn(d_gate, tokens)
            total_up = dot_tn(d_up, tokens)
        else:
            gate_grad[...] = (total_gate + dot_tn(d_gate, tokens)).astype(BF)
            up_grad[...] = (total_up + dot_tn(d_up, tokens)).astype(BF)


def weight_grads(core, own, other, gate_s, up_s, student_all):
    out = jax.ShapeDtypeStruct((gate_s.shape[1], student_all.shape[1]), BF)
    return pl.pallas_call(
        grad_kernel,
        out_shape=(out, out),
        in_specs=[pl.BlockSpec(memory_space=pltpu.SMEM)]
        + [pl.BlockSpec(memory_space=pltpu.VMEM)] * 5,
        out_specs=[pl.BlockSpec(memory_space=pltpu.VMEM)] * 2,
        compiler_params=pltpu.CompilerParams(vmem_limit_bytes=16 * 1024 * 1024),
    )(core, own, other, gate_s, up_s, student_all)


def body(
    teacher_in,
    route_ids,
    router,
    w_gate,
    w_up,
    w_down,
    projection,
    student_in,
    s_gate,
    s_up,
    s_down,
):
    core = lax.axis_index("c")
    row = lax.axis_index("y")
    expert = row * NC + core
    tok_dp, width = teacher_in.shape
    tokens = route_ids.shape[0]
    sff_dev = s_gate.shape[1]
    sd_dev = student_in.shape[1]
    chunk = width // NE
    half = tokens // 2
    group = width // (ND * NY)

    part = lax.dynamic_slice_in_dim(teacher_in, expert * chunk, chunk, 1)
    sent = jnp.concatenate([part, student_in], axis=1)
    arrived = spread(sent, DP, ND).reshape(tokens, chunk + sd_dev)
    arrived, down_t = lax.optimization_barrier((arrived, w_down[0].T))
    own = arrived[:, :chunk]
    student_all = arrived[:, chunk:]
    router_t = router.T

    far = [along_y(own, s) for s in range(1, NY)]
    own_other = swap_cores(own)
    far_other = [swap_cores(v) for v in far]
    xs, spots = [own, own_other], [row]
    for s in (1, 3, 2):
        xs += [far[s - 1], far_other[s - 1]]
        spots.append(lax.rem(row - s + NY, NY))
    where = jnp.stack(spots + [core]).astype(jnp.int32)
    parts = expert_products(
        where, xs, w_gate, w_up, router_t, route_ids, down_t, tokens, chunk
    )
    pair_mine = core_sum(
        jnp.concatenate([dot(student_all, s_gate), dot(student_all, s_up)], axis=1), core
    )
    keeps, gives = parts[:4], parts[4:]

    arriving = []
    mine = None
    for s in (2, 1, 3, 0):
        both = (keeps[s].astype(F32) + swap_cores(gives[s]).astype(F32)).astype(BF)
        if s:
            arriving.append(along_y(both, s))
        else:
            mine = both
    total = mine.astype(F32)
    for term in arriving:
        total = total + term.astype(F32)
    terms = exchange(total.astype(BF), DP)
    pair_mine, pair_other, _ = row_sum(pair_mine, row)
    pair_sums = in_order(pair_mine, pair_other, core).astype(F32)
    gate_s = pair_sums[:, :sff_dev]
    up_s = pair_sums[:, sff_dev:]
    hidden_s = (gate_s * jax.nn.sigmoid(gate_s) * up_s).astype(BF)
    student_part = dot(hidden_s, s_down)
    summed = jnp.sum(terms.astype(F32), axis=0).astype(BF)
    pieces = [summed] + [along_y(summed, s) for s in range(1, NY)]
    mine = jnp.concatenate(pieces, axis=0)
    other = swap_cores(mine)
    cols = lax.dynamic_slice_in_dim(projection, expert * sd_dev, sd_dev, 1)
    cols = jnp.concatenate(
        [
            lax.dynamic_slice_in_dim(cols, lax.rem(row - s + NY, NY) * group, group, 0)
            for s in range(NY)
        ],
        axis=0,
    )
    first = jnp.where(core == 0, mine, other)
    second = jnp.where(core == 0, other, mine)
    target = dot_tn(jnp.concatenate([first, second], axis=1), cols)

    out_part = (student_part - target).astype(BF)
    terms = exchange(out_part.reshape(ND, tok_dp, sd_dev), DP)
    mismatch = student_in.astype(F32) + jnp.sum(terms.astype(F32), axis=0)
    cotangent = (mismatch * (1.0 / math.sqrt(tokens))).astype(BF)
    cotangent_all = spread(cotangent, DP, ND).reshape(tokens, sd_dev)
    grad_down = dot_tn(hidden_s, cotangent_all).astype(BF)
    d_mine, d_other, grad_down = row_sum(
        core_sum(dot_nt(cotangent_all, s_down), core), grad_down
    )
    core_at = jnp.reshape(core, (1,)).astype(jnp.int32)
    grad_gate, grad_up = weight_grads(core_at, d_mine, d_other, gate_s, up_s, student_all)
    grad_gate = grad_gate.T
    grad_up = grad_up.T
    return (grad_gate, grad_up, grad_down, mismatch)


def solution(mesh):
    fine = Mesh(mesh.devices.reshape(NX, NZ, NY, NC), ("x", "z", "y", "c"))
    return jax.shard_map(
        body,
        mesh=fine,
        in_specs=(
            P(DP, None),
            P(),
            P(),
            P(EX, None, DP),
            P(EX, None, DP),
            P(EX, DP, None),
            P(DP, None),
            P(DP, EX),
            P(EX, DP),
            P(EX, DP),
            P(DP, EX),
        ),
        out_specs=(P(EX, DP), P(EX, DP), P(DP, EX), P(DP, EX)),
        check_vma=False,
    )
```

time: 251 us -> 172 us (0.69)
  blocking collectives: 110 us -> 30.4 us
  starting transfers between devices: 31.1 us -> 73.8 us
  matrix products: 24.4 us -> 2.14 us
  other arithmetic: 22 us -> 5.42 us
  local copies, waits for them, and re-layouts: 24.5 us -> 9.6 us
  Pallas kernels: 0 us -> 12.5 us
    all_to_all x7 -> x2, blocking collectives: 110 us -> 30.4 us  [exchange(): return lax.all_to_all(values, axes, 0, 0, tiled=False)]
    ppermute x2 -> x13, starting transfers between devices: 3.39 us -> 30.4 us  [swap_cores(): return lax.ppermute(values, 'c', [(0, 1), (1, 0)])]
    ppermute x0 -> x15, starting transfers between devices: none -> 23.1 us  [along_y(): return lax.ppermute(values, 'y', [(i, (i + shift) % NY) for i in range(NY)])]
    dot_general x11 -> x6, matrix products: 24.4 us -> 2.14 us  [the longest x2 1.18 us: dot_tn(): lax.dot_general(a, b, (((0,), (0,)), ((), ())), preferred_element_type=F32)]
    all_to_all x5 -> x2, waiting for transfers between devices: 33.6 us -> 19.6 us  [exchange(): return lax.all_to_all(values, axes, 0, 0, tiled=False)]
    ppermute x0 -> x15, waiting for transfers between devices: none -> 13.2 us  [along_y(): return lax.ppermute(values, 'y', [(i, (i + shift) % NY) for i in range(NY)])]
    pallas_call x0 -> x2, Pallas kernels: none -> 12.5 us  [the longest x1 11.3 us: expert_products(): pl.pallas_call(expert_kernel, out_shape=(out,) * 8, in_specs=[IN_SMEM] +...]
    convert_element_type x5 -> x11, other arithmetic: 13.7 us -> 3.8 us  [the longest x3 2.31 us: body(): both = (keeps[s].astype(F32) + swap_cores(gives[s]).astype(F32)).astype(BF)]
  transfers between devices with their start and end apart: 7 -> 30, of which waited for: 5 -> 16; matrix products, arithmetic and copies ran while one was open for 8% -> 7% of each run, Pallas kernels for 0% -> 0%
where the time goes in v3:
time: 172 us
  starting transfers between devices  73.8 us (43%)
  waiting for transfers between devices  36.7 us (21%)
  blocking collectives  30.4 us (18%)
  Pallas kernels  12.5 us (7%)
  local copies, waits for them, and re-layouts  9.6 us (6%)
  other arithmetic  5.42 us (3%)
  matrix products  2.14 us (1%)
    all_to_all x2, blocking collectives, exchange(): return lax.all_to_all(values, axes, 0, 0, tiled=False)  30.4 us
    ppermute x13, starting transfers between devices, swap_cores(): return lax.ppermute(values, 'c', [(0, 1), (1, 0)])  30.4 us
    ppermute x15, starting transfers between devices, along_y(): return lax.ppermute(values, 'y', [(i, (i + shift) % NY) for i in range(NY)])  23.1 us
    all_to_all x2, starting transfers between devices, exchange(): return lax.all_to_all(values, axes, 0, 0, tiled=False)  20.2 us
    all_to_all x2, waiting for transfers between devices, exchange(): return lax.all_to_all(values, axes, 0, 0, tiled=False)  19.6 us
    ppermute x15, waiting for transfers between devices, along_y(): return lax.ppermute(values, 'y', [(i, (i + shift) % NY) for i in range(NY)])  13.2 us
    pallas_call x1, Pallas kernels, expert_products(): pl.pallas_call(expert_kernel, out_shape=(out,) * 8, in_specs=[IN_SMEM] +...  11.3 us
    unnamed x28, local copies, waits for them, and re-layouts  6.16 us
  transfers between devices with their start and end apart: 30, of which 16 were waited for; matrix products, arithmetic and copies ran while one was open for 7% of the time, Pallas kernels for 0%

profile of v3, /device:TPU:1, one launch (start us, length us, event | category | flops | bytes accessed | tf_op | source)
XLA Modules:
  0.0 171.6 jit_solution(16456797884283674517)
XLA Ops:
  0.7 0.8 constant_dynamic-slice_fusion
  1.4 0.7 pad_maximum_fusion.2
  2.1 0.9 broadcast_in_dim.4
  3.0 11.9 %all-to-all-start = ((bf16[32,8,1280]{2,1,0:T(8,128)(2,1)}), bf16[32,8,1280]{2,1,0:T(8,128)(2,1)S(1)}, u32[]{:S(2)}, u32[]{:S(2)}) async-start(bf16[32,8,1280]{2,1,0:T(8,128)(2,1)} %broadcast_in_dim.4), calls=%async_computation | async-start | bytes 1310720 | tf_op jit(solution)/shard_map/all_to_all | solution.py:23
  14.9 4.7 %copy.15 = bf16[1,256,6144]{1,2,0:T(8,128)(2,1)} copy(bf16[1,256,6144]{2,1,0:T(8,128)(2,1)} %param.16) | data formatting | bytes 6291456 | tf_op args[5]
  19.5 11.7 %all-to-all-done = bf16[32,8,1280]{2,1,0:T(8,128)(2,1)S(1)} async-done(((bf16[32,8,1280]{2,1,0:T(8,128)(2,1)}), bf16[32,8,1280]{2,1,0:T(8,128)(2,1)S(1)}, u32[]{:S(2)}, u32[]{:S(2)}) %all-to-all-start) | async-done | bytes 655392 | tf_op jit(solution)/shard_map/all_to_all | solution.py:23
  31.3 3.0 %collective-permute-start.10 = (bf16[256,768]{1,0:T(8,128)(2,1)S(1)}, bf16[256,768]{1,0:T(8,128)(2,1)S(1)}, u32[]{:S(2)}, u32[]{:S(2)}) collective-permute-start(bf16[256,768]{1,0:T(8,128)(2,1)S(1)} %slice.29.refs_0_), channel_id=1, source_target_pairs={{0,4},{2,6},{4,0},{6,2},{1,5},{3,7},{5,1},{7,3},{8,12},{10,14},{12... | collective-permute-start | bytes 1179656 | tf_op jit(solution)/shard_map/ppermute | solution.py:35
  34.3 0.4 collective-permute-start.6
  34.7 2.3 %collective-permute-start.8 = (bf16[256,768]{1,0:T(8,128)(2,1)S(1)}, bf16[256,768]{1,0:T(8,128)(2,1)S(1)}, u32[]{:S(2)}, u32[]{:S(2)}) collective-permute-start(bf16[256,768]{1,0:T(8,128)(2,1)S(1)} %slice.29.refs_0_), channel_id=1, source_target_pairs={{0,6},{2,0},{4,2},{6,4},{1,7},{3,1},{5,3},{7,5},{8,14},{10,8},{12,... | collective-permute-start | bytes 1179656 | tf_op jit(solution)/shard_map/ppermute | solution.py:35
  37.0 5.9 %collective-permute-start.5 = (bf16[256,768]{1,0:T(8,128)(2,1)S(1)}, bf16[256,768]{1,0:T(8,128)(2,1)S(1)}, u32[]{:S(2)}, u32[]{:S(2)}) collective-permute-start(bf16[256,768]{1,0:T(8,128)(2,1)S(1)} %slice.29.refs_0_), channel_id=1, source_target_pairs={{0,1},{1,0},{2,3},{3,2},{4,5},{5,4},{6,7},{7,6},{8,9},{9,8},{10,11... | collective-permute-start | bytes 1179656 | tf_op jit(solution)/shard_map/ppermute | solution.py:31
  42.8 5.9 %collective-permute-start.11 = (bf16[256,768]{1,0:T(8,128)(2,1)S(1)}, bf16[256,768]{1,0:T(8,128)(2,1)S(1)}, u32[]{:S(2)}, u32[]{:S(2)}) collective-permute-start(bf16[256,768]{1,0:T(8,128)(2,1)S(1)} %collective-permute-done.10.refs_6_), channel_id=1, source_target_pairs={{0,1},{1,0},{2,3},{3,2},{4,5},{5,4},{6,7},{7,6},{8,9},{9,8},{10,11... | collective-permute-start | bytes 1179656 | tf_op jit(solution)/shard_map/ppermute | solution.py:31
  48.7 0.9 collective-permute-done.6.refs_2_
  49.6 3.2 %collective-permute-start.7 = (bf16[256,768]{1,0:T(8,128)(2,1)S(1)}, bf16[256,768]{1,0:T(8,128)(2,1)}, u32[]{:S(2)}, u32[]{:S(2)}) collective-permute-start(bf16[256,768]{1,0:T(8,128)(2,1)S(1)} %collective-permute-done.6.refs_2_), channel_id=1, source_target_pairs={{0,1},{1,0},{2,3},{3,2},{4,5},{5,4},{6,7},{7,6},{8,9},{9,8},{10,11... | collective-permute-start | bytes 1179656 | tf_op jit(solution)/shard_map/ppermute | solution.py:31
  52.8 0.4 collective-permute-start.9
  53.2 0.8 copy.18.refs_11_
  54.0 0.6 stack.20.where
  54.9 0.5 copy-done.5
  55.5 11.3 %shard_map.138 = (bf16[32,48,128]{2,1,0:T(8,128)(2,1)}, bf16[32,48,128]{2,1,0:T(8,128)(2,1)}, bf16[32,48,128]{2,1,0:T(8,128)(2,1)}, bf16[32,48,128]{2,1,0:T(8,12...) custom-call(s32[5]{0:T(128)} %stack.20.where, ...), custom_call_target="tpu_custom_call" | custom-call | flops 2415919104 | bytes 15728640 | tf_op jit(solution)/shard_map/pallas_call | solution.py:171
  67.1 0.3 fusion.17
  67.4 0.5 collective-permute-start.15
  67.9 0.3 fusion.19
  68.1 0.2 collective-permute-start.17
  68.3 0.4 collective-permute-start.12
  68.7 0.2 collective-permute-done.13
  68.9 1.1 add_convert_fusion.3
  70.0 2.0 %collective-permute-start.14 = (bf16[32,48,128]{2,1,0:T(8,128)(2,1)S(1)}, bf16[32,48,128]{2,1,0:T(8,128)(2,1)S(1)}, u32[]{:S(2)}, u32[]{:S(2)}) collective-permute-start(bf16[32,48,128]{2,1,0:T(8,128)(2,1)S(1)} %add_convert_fusion.3), channel_id=1, source_target_pairs={{0,4},{2,6},{4,0},{6,2},{1,5},{3,7},{5,1},{7,3},{8,12},{10,14},{12... | collective-permute-start | bytes 1179656 | tf_op jit(solution)/shard_map/ppermute | solution.py:35
  72.0 1.1 add_convert_fusion.2
  73.1 1.1 collective-permute-start.16
  74.4 1.7 collective-permute-start.18
  76.2 1.3 collective-permute-start
  77.5 1.0 collective-permute-done
  78.8 1.7 collective-permute-start.2
  80.5 1.8 %collective-permute-done.14 = bf16[32,48,128]{2,1,0:T(8,128)(2,1)S(1)} collective-permute-done((bf16[32,48,128]{2,1,0:T(8,128)(2,1)S(1)}, bf16[32,48,128]{2,1,0:T(8,128)(2,1)S(1)}, u32[]{:S(2)}, u32[]{:S(2)}) %collective-permute-start.14) | collective-permute-done | bytes 393248 | tf_op jit(solution)/shard_map/ppermute | solution.py:35
  82.2 2.4 %collective-permute-start.3 = (bf16[128,448]{1,0:T(8,128)(2,1)S(1)}, bf16[128,448]{1,0:T(8,128)(2,1)S(1)}, u32[]{:S(2)}, u32[]{:S(2)}) collective-permute-start(bf16[128,448]{1,0:T(8,128)(2,1)S(1)} %add_convert_fusion.6), channel_id=1, source_target_pairs={{0,6},{2,0},{4,2},{6,4},{1,7},{3,1},{5,3},{7,5},{8,14},{10,8},{12,... | collective-permute-start | bytes 344072 | tf_op jit(solution)/shard_map/ppermute | solution.py:35
  84.6 6.5 %collective-permute-done.16 = bf16[32,48,128]{2,1,0:T(8,128)(2,1)S(1)} collective-permute-done((bf16[32,48,128]{2,1,0:T(8,128)(2,1)S(1)}, bf16[32,48,128]{2,1,0:T(8,128)(2,1)S(1)}, u32[]{:S(2)}, u32[]{:S(2)}) %collective-permute-start.16) | collective-permute-done | bytes 393248 | tf_op jit(solution)/shard_map/ppermute | solution.py:35
  91.1 1.0 add_convert_fusion
  92.1 8.4 %all-to-all-start.1 = ((bf16[32,48,128]{2,1,0:T(8,128)(2,1)}), bf16[32,48,128]{2,1,0:T(8,128)(2,1)S(1)}, u32[]{:S(2)}, u32[]{:S(2)}) async-start(bf16[32,48,128]{2,1,0:T(8,128)(2,1)} %add_convert_fusion), calls=%async_computation.1 | async-start | bytes 786432 | tf_op jit(solution)/shard_map/all_to_all | solution.py:23
  100.7 1.4 collective-permute-start.4
  102.1 1.1 fusion.21
  103.3 7.9 %all-to-all-done.1 = bf16[32,48,128]{2,1,0:T(8,128)(2,1)S(1)} async-done(((bf16[32,48,128]{2,1,0:T(8,128)(2,1)}), bf16[32,48,128]{2,1,0:T(8,128)(2,1)S(1)}, u32[]{:S(2)}, u32[]{:S(2)}) %all-to-all-start.1) | async-done | bytes 393248 | tf_op jit(solution)/shard_map/all_to_all | solution.py:23
  111.3 2.6 %collective-permute-start.19 = (bf16[48,128]{1,0:T(8,128)(2,1)S(1)}, bf16[48,128]{1,0:T(8,128)(2,1)S(1)}, u32[]{:S(2)}, u32[]{:S(2)}) collective-permute-start(bf16[48,128]{1,0:T(8,128)(2,1)S(1)} %reduce_sum.21), channel_id=1, source_target_pairs={{0,2},{2,4},{4,6},{6,0},{1,3},{3,5},{5,7},{7,1},{8,10},{10,12},{12... | collective-permute-start | bytes 36872 | tf_op jit(solution)/shard_map/ppermute | solution.py:35
  113.9 2.1 %collective-permute-start.20 = (bf16[48,128]{1,0:T(8,128)(2,1)S(1)}, bf16[48,128]{1,0:T(8,128)(2,1)S(1)}, u32[]{:S(2)}, u32[]{:S(2)}) collective-permute-start(bf16[48,128]{1,0:T(8,128)(2,1)S(1)} %reduce_sum.21), channel_id=1, source_target_pairs={{0,4},{2,6},{4,0},{6,2},{1,5},{3,7},{5,1},{7,3},{8,12},{10,14},{12... | collective-permute-start | bytes 36872 | tf_op jit(solution)/shard_map/ppermute | solution.py:35
  116.0 0.4 collective-permute-start.21
  116.5 1.4 collective-permute-done.20
  118.0 0.6 collective-permute-done.21
  118.6 5.9 %collective-permute-start.22 = (bf16[192,128]{1,0:T(8,128)(2,1)S(1)}, bf16[192,128]{1,0:T(8,128)(2,1)S(1)}, u32[]{:S(2)}, u32[]{:S(2)}) collective-permute-start(bf16[192,128]{1,0:T(8,128)(2,1)S(1)} %pad_maximum_fusion.1), channel_id=1, source_target_pairs={{0,1},{1,0},{2,3},{3,2},{4,5},{5,4},{6,7},{7,6},{8,9},{9,8},{10,11... | collective-permute-start | bytes 147464 | tf_op jit(solution)/shard_map/ppermute | solution.py:31
  124.4 0.2 fusion.23
  124.6 0.7 collective-permute-done.22
  125.3 0.2 fusion.1
  125.6 14.3 %all_to_all.20 = bf16[32,8,512]{2,1,0:T(8,128)(2,1)S(1)} all-to-all(bf16[32,8,512]{2,1,0:T(8,128)(2,1)S(1)} %fusion.1), channel_id=1, replica_groups=mesh['x'=4,'z'=8,'y'=4,'c'=2] {'x','z'}, dimensions={0} | all-to-all | bytes 524288 | tf_op jit(solution)/shard_map/all_to_all | solution.py:23
  139.9 0.6 multiply_convert_fusion.1
  140.5 16.2 %all_to_all.21 = bf16[32,8,512]{2,1,0:T(8,128)(2,1)S(1)} all-to-all(bf16[32,8,512]{2,1,0:T(8,128)(2,1)S(1)} %broadcast_in_dim.5), channel_id=1, replica_groups=mesh['x'=4,'z'=8,'y'=4,'c'=2] {'x','z'}, dimensions={0} | all-to-all | bytes 524288 | tf_op jit(solution)/shard_map/all_to_all | solution.py:23
  156.7 0.2 fusion.4
  157.0 3.7 %collective-permute-start.23 = (bf16[128,224]{1,0:T(8,128)(2,1)S(1)}, bf16[128,224]{1,0:T(8,128)(2,1)S(1)}, u32[]{:S(2)}, u32[]{:S(2)}) collective-permute-start(bf16[128,224]{1,0:T(8,128)(2,1)S(1)} %select_convert_fusion.1), channel_id=1, source_target_pairs={{0,1},{1,0},{2,3},{3,2},{4,5},{5,4},{6,7},{7,6},{8,9},{9,8},{10,11... | collective-permute-start | bytes 172040 | tf_op jit(solution)/shard_map/ppermute | solution.py:31
  160.7 0.9 collective-permute-done.23
  161.7 2.5 %collective-permute-start.25 = (bf16[128,224]{1,0:T(8,128)(2,1)S(1)}, bf16[128,224]{1,0:T(8,128)(2,1)S(1)}, u32[]{:S(2)}, u32[]{:S(2)}) collective-permute-start(bf16[128,224]{1,0:T(8,128)(2,1)S(1)} %add_convert_fusion.8), channel_id=1, source_target_pairs={{0,4},{2,6},{4,0},{6,2},{1,5},{3,7},{5,1},{7,3},{8,12},{10,14},{12... | collective-permute-start | bytes 172040 | tf_op jit(solution)/shard_map/ppermute | solution.py:35
  164.2 0.9 collective-permute-start.26
  165.1 0.9 convolution_convert_fusion
  166.0 0.7 collective-permute-done.24
  166.7 0.4 collective-permute-done.25
  167.2 0.9 collective-permute-done.26
  168.1 1.5 collective-permute-start.27
  169.6 0.9 collective-permute-done.27.other
  170.4 1.1 shard_map.139
  (60 shorter events, 1.7 us)
Async XLA Ops:
  0.6 123.8 %copy-start = (bf16[224,512]{1,0:T(8,128)(2,1)S(1)}, bf16[224,512]{1,0:T(8,128)(2,1)}, u32[]{:S(2)}) copy-start(bf16[224,512]{1,0:T(8,128)(2,1)} %param.21) | copy-start | bytes 688132
  3.0 28.3 %all-to-all-start = ((bf16[32,8,1280]{2,1,0:T(8,128)(2,1)}), bf16[32,8,1280]{2,1,0:T(8,128)(2,1)S(1)}, u32[]{:S(2)}, u32[]{:S(2)}) async-start(bf16[32,8,1280]{2,1,0:T(8,128)(2,1)} %broadcast_in_dim.4), calls=%async_computation | async-start | bytes 1310720 | tf_op jit(solution)/shard_map/all_to_all | solution.py:23
  14.9 38.4 %copy-start.12 = (s32[256,2]{0,1:T(2,128)S(1)}, s32[256,2]{0,1:T(2,128)}, u32[]{:S(2)}) copy-start(s32[256,2]{0,1:T(2,128)} %param.12) | copy-start | bytes 6148
  31.3 23.6 %copy-start.1 = (bf16[256,768]{1,0:T(8,128)(2,1)}, bf16[256,768]{1,0:T(8,128)(2,1)S(1)}, u32[]{:S(2)}) copy-start(bf16[256,768]{1,0:T(8,128)(2,1)S(1)} %slice.29.refs_0_) | copy-start | bytes 1179652
  31.3 11.5 %collective-permute-start.10 = (bf16[256,768]{1,0:T(8,128)(2,1)S(1)}, bf16[256,768]{1,0:T(8,128)(2,1)S(1)}, u32[]{:S(2)}, u32[]{:S(2)}) collective-permute-start(bf16[256,768]{1,0:T(8,128)(2,1)S(1)} %slice.29.refs_0_), channel_id=1, source_target_pairs={{0,4},{2,6},{4,0},{6,2},{1,5},{3,7},{5,1},{7,3},{8,12},{10,14},{12... | collective-permute-start | bytes 1179656 | tf_op jit(solution)/shard_map/ppermute | solution.py:35
  34.3 15.3 %collective-permute-start.6 = (bf16[256,768]{1,0:T(8,128)(2,1)S(1)}, bf16[256,768]{1,0:T(8,128)(2,1)S(1)}, u32[]{:S(2)}, u32[]{:S(2)}) collective-permute-start(bf16[256,768]{1,0:T(8,128)(2,1)S(1)} %slice.29.refs_0_), channel_id=1, source_target_pairs={{0,2},{2,4},{4,6},{6,0},{1,3},{3,5},{5,7},{7,1},{8,10},{10,12},{12... | collective-permute-start | bytes 1179656 | tf_op jit(solution)/shard_map/ppermute | solution.py:35
  34.7 18.2 %collective-permute-start.8 = (bf16[256,768]{1,0:T(8,128)(2,1)S(1)}, bf16[256,768]{1,0:T(8,128)(2,1)S(1)}, u32[]{:S(2)}, u32[]{:S(2)}) collective-permute-start(bf16[256,768]{1,0:T(8,128)(2,1)S(1)} %slice.29.refs_0_), channel_id=1, source_target_pairs={{0,6},{2,0},{4,2},{6,4},{1,7},{3,1},{5,3},{7,5},{8,14},{10,8},{12,... | collective-permute-start | bytes 1179656 | tf_op jit(solution)/shard_map/ppermute | solution.py:35
  37.0 17.7 %collective-permute-start.5 = (bf16[256,768]{1,0:T(8,128)(2,1)S(1)}, bf16[256,768]{1,0:T(8,128)(2,1)S(1)}, u32[]{:S(2)}, u32[]{:S(2)}) collective-permute-start(bf16[256,768]{1,0:T(8,128)(2,1)S(1)} %slice.29.refs_0_), channel_id=1, source_target_pairs={{0,1},{1,0},{2,3},{3,2},{4,5},{5,4},{6,7},{7,6},{8,9},{9,8},{10,11... | collective-permute-start | bytes 1179656 | tf_op jit(solution)/shard_map/ppermute | solution.py:31
  42.8 12.1 %copy-start.2 = (bf16[256,768]{1,0:T(8,128)(2,1)}, bf16[256,768]{1,0:T(8,128)(2,1)S(1)}, u32[]{:S(2)}) copy-start(bf16[256,768]{1,0:T(8,128)(2,1)S(1)} %collective-permute-done.10.refs_6_) | copy-start | bytes 1179652
  42.8 11.8 %collective-permute-start.11 = (bf16[256,768]{1,0:T(8,128)(2,1)S(1)}, bf16[256,768]{1,0:T(8,128)(2,1)S(1)}, u32[]{:S(2)}, u32[]{:S(2)}) collective-permute-start(bf16[256,768]{1,0:T(8,128)(2,1)S(1)} %collective-permute-done.10.refs_6_), channel_id=1, source_target_pairs={{0,1},{1,0},{2,3},{3,2},{4,5},{5,4},{6,7},{7,6},{8,9},{9,8},{10,11... | collective-permute-start | bytes 1179656 | tf_op jit(solution)/shard_map/ppermute | solution.py:31
  49.6 5.3 %copy-start.3 = (bf16[256,768]{1,0:T(8,128)(2,1)}, bf16[256,768]{1,0:T(8,128)(2,1)S(1)}, u32[]{:S(2)}) copy-start(bf16[256,768]{1,0:T(8,128)(2,1)S(1)} %collective-permute-done.6.refs_2_) | copy-start | bytes 1179652
  49.6 5.1 %collective-permute-start.7 = (bf16[256,768]{1,0:T(8,128)(2,1)S(1)}, bf16[256,768]{1,0:T(8,128)(2,1)}, u32[]{:S(2)}, u32[]{:S(2)}) collective-permute-start(bf16[256,768]{1,0:T(8,128)(2,1)S(1)} %collective-permute-done.6.refs_2_), channel_id=1, source_target_pairs={{0,1},{1,0},{2,3},{3,2},{4,5},{5,4},{6,7},{7,6},{8,9},{9,8},{10,11... | collective-permute-start | bytes 1179656 | tf_op jit(solution)/shard_map/ppermute | solution.py:31
  52.8 2.1 %copy-start.4 = (bf16[256,768]{1,0:T(8,128)(2,1)}, bf16[256,768]{1,0:T(8,128)(2,1)S(1)}, u32[]{:S(2)}) copy-start(bf16[256,768]{1,0:T(8,128)(2,1)S(1)} %collective-permute-done.8.refs_4_) | copy-start | bytes 1179652
  52.8 2.0 %collective-permute-start.9 = (bf16[256,768]{1,0:T(8,128)(2,1)S(1)}, bf16[256,768]{1,0:T(8,128)(2,1)}, u32[]{:S(2)}, u32[]{:S(2)}) collective-permute-start(bf16[256,768]{1,0:T(8,128)(2,1)S(1)} %collective-permute-done.8.refs_4_), channel_id=1, source_target_pairs={{0,1},{1,0},{2,3},{3,2},{4,5},{5,4},{6,7},{7,6},{8,9},{9,8},{10,11... | collective-permute-start | bytes 1179656 | tf_op jit(solution)/shard_map/ppermute | solution.py:31
  54.7 0.8 copy-start.5
  54.7 0.9 copy-start.6
  55.5 11.6 %copy-start.9 = (bf16[512,224]{0,1:T(8,128)(2,1)S(1)}, bf16[512,224]{0,1:T(8,128)(2,1)}, u32[]{:S(2)}) copy-start(bf16[512,224]{0,1:T(8,128)(2,1)} %param.20) | copy-start | bytes 688132
  55.5 12.3 %copy-start.10 = (bf16[512,224]{0,1:T(8,128)(2,1)S(1)}, bf16[512,224]{0,1:T(8,128)(2,1)}, u32[]{:S(2)}) copy-start(bf16[512,224]{0,1:T(8,128)(2,1)} %param.19) | copy-start | bytes 688132
  66.9 7.4 %copy-start.8 = (bf16[32,48,128]{2,1,0:T(8,128)(2,1)S(1)}, bf16[32,48,128]{2,1,0:T(8,128)(2,1)}, u32[]{:S(2)}) copy-start(bf16[32,48,128]{2,1,0:T(8,128)(2,1)} %get-tuple-element.34) | copy-start | bytes 1179652
  66.9 24.2 %copy-start.7 = (bf16[32,48,128]{2,1,0:T(8,128)(2,1)S(1)}, bf16[32,48,128]{2,1,0:T(8,128)(2,1)}, u32[]{:S(2)}) copy-start(bf16[32,48,128]{2,1,0:T(8,128)(2,1)} %get-tuple-element.28) | copy-start | bytes 1179652
  66.9 2.0 %collective-permute-start.13 = (bf16[32,48,128]{2,1,0:T(8,128)(2,1)}, bf16[32,48,128]{2,1,0:T(8,128)(2,1)S(1)}, u32[]{:S(2)}, u32[]{:S(2)}) collective-permute-start(bf16[32,48,128]{2,1,0:T(8,128)(2,1)} %get-tuple-element.31), channel_id=1, source_target_pairs={{0,1},{1,0},{2,3},{3,2},{4,5},{5,4},{6,7},{7,6},{8,9},{9,8},{10,11... | collective-permute-start | bytes 1179656 | tf_op jit(solution)/shard_map/ppermute | solution.py:31
  67.4 4.6 %collective-permute-start.15 = (bf16[32,48,128]{2,1,0:T(8,128)(2,1)}, bf16[32,48,128]{2,1,0:T(8,128)(2,1)S(1)}, u32[]{:S(2)}, u32[]{:S(2)}) collective-permute-start(bf16[32,48,128]{2,1,0:T(8,128)(2,1)} %get-tuple-element.33), channel_id=1, source_target_pairs={{0,1},{1,0},{2,3},{3,2},{4,5},{5,4},{6,7},{7,6},{8,9},{9,8},{10,11... | collective-permute-start | bytes 1179656 | tf_op jit(solution)/shard_map/ppermute | solution.py:31
  68.1 6.1 %collective-permute-start.17 = (bf16[32,48,128]{2,1,0:T(8,128)(2,1)}, bf16[32,48,128]{2,1,0:T(8,128)(2,1)S(1)}, u32[]{:S(2)}, u32[]{:S(2)}) collective-permute-start(bf16[32,48,128]{2,1,0:T(8,128)(2,1)} %get-tuple-element.35), channel_id=1, source_target_pairs={{0,1},{1,0},{2,3},{3,2},{4,5},{5,4},{6,7},{7,6},{8,9},{9,8},{10,11... | collective-permute-start | bytes 1179656 | tf_op jit(solution)/shard_map/ppermute | solution.py:31
  68.3 10.4 %collective-permute-start.12 = (bf16[32,48,128]{2,1,0:T(8,128)(2,1)}, bf16[32,48,128]{2,1,0:T(8,128)(2,1)S(1)}, u32[]{:S(2)}, u32[]{:S(2)}) collective-permute-start(bf16[32,48,128]{2,1,0:T(8,128)(2,1)} %get-tuple-element.29), channel_id=1, source_target_pairs={{0,1},{1,0},{2,3},{3,2},{4,5},{5,4},{6,7},{7,6},{8,9},{9,8},{10,11... | collective-permute-start | bytes 1179656 | tf_op jit(solution)/shard_map/ppermute | solution.py:31
  70.0 12.2 %collective-permute-start.14 = (bf16[32,48,128]{2,1,0:T(8,128)(2,1)S(1)}, bf16[32,48,128]{2,1,0:T(8,128)(2,1)S(1)}, u32[]{:S(2)}, u32[]{:S(2)}) collective-permute-start(bf16[32,48,128]{2,1,0:T(8,128)(2,1)S(1)} %add_convert_fusion.3), channel_id=1, source_target_pairs={{0,4},{2,6},{4,0},{6,2},{1,5},{3,7},{5,1},{7,3},{8,12},{10,14},{12... | collective-permute-start | bytes 1179656 | tf_op jit(solution)/shard_map/ppermute | solution.py:35
  73.1 18.0 %collective-permute-start.16 = (bf16[32,48,128]{2,1,0:T(8,128)(2,1)S(1)}, bf16[32,48,128]{2,1,0:T(8,128)(2,1)S(1)}, u32[]{:S(2)}, u32[]{:S(2)}) collective-permute-start(bf16[32,48,128]{2,1,0:T(8,128)(2,1)S(1)} %add_convert_fusion.2), channel_id=1, source_target_pairs={{0,2},{2,4},{4,6},{6,0},{1,3},{3,5},{5,7},{7,1},{8,10},{10,12},{12... | collective-permute-start | bytes 1179656 | tf_op jit(solution)/shard_map/ppermute | solution.py:35
  74.4 16.7 %collective-permute-start.18 = (bf16[32,48,128]{2,1,0:T(8,128)(2,1)S(1)}, bf16[32,48,128]{2,1,0:T(8,128)(2,1)S(1)}, u32[]{:S(2)}, u32[]{:S(2)}) collective-permute-start(bf16[32,48,128]{2,1,0:T(8,128)(2,1)S(1)} %add_convert_fusion.1), channel_id=1, source_target_pairs={{0,6},{2,0},{4,2},{6,4},{1,7},{3,1},{5,3},{7,5},{8,14},{10,8},{12,... | collective-permute-start | bytes 1179656 | tf_op jit(solution)/shard_map/ppermute | solution.py:35
  76.2 2.3 %collective-permute-start = (bf16[128,448]{1,0:T(8,128)(2,1)S(1)}, bf16[128,448]{1,0:T(8,128)(2,1)S(1)}, u32[]{:S(2)}, u32[]{:S(2)}) collective-permute-start(bf16[128,448]{1,0:T(8,128)(2,1)S(1)} %select_convert_fusion), channel_id=1, source_target_pairs={{0,1},{1,0},{2,3},{3,2},{4,5},{5,4},{6,7},{7,6},{8,9},{9,8},{10,11... | collective-permute-start | bytes 344072 | tf_op jit(solution)/shard_map/ppermute | solution.py:31
  78.7 21.9 %collective-permute-start.1 = (bf16[128,448]{1,0:T(8,128)(2,1)S(1)}, bf16[128,448]{1,0:T(8,128)(2,1)S(1)}, u32[]{:S(2)}, u32[]{:S(2)}) collective-permute-start(bf16[128,448]{1,0:T(8,128)(2,1)S(1)} %add_convert_fusion.6), channel_id=1, source_target_pairs={{0,2},{2,4},{4,6},{6,0},{1,3},{3,5},{5,7},{7,1},{8,10},{10,12},{12... | collective-permute-start | bytes 344072 | tf_op jit(solution)/shard_map/ppermute | solution.py:35
  78.8 21.8 %collective-permute-start.2 = (bf16[128,448]{1,0:T(8,128)(2,1)S(1)}, bf16[128,448]{1,0:T(8,128)(2,1)S(1)}, u32[]{:S(2)}, u32[]{:S(2)}) collective-permute-start(bf16[128,448]{1,0:T(8,128)(2,1)S(1)} %add_convert_fusion.6), channel_id=1, source_target_pairs={{0,4},{2,6},{4,0},{6,2},{1,5},{3,7},{5,1},{7,3},{8,12},{10,14},{12... | collective-permute-start | bytes 344072 | tf_op jit(solution)/shard_map/ppermute | solution.py:35
  82.2 18.3 %collective-permute-start.3 = (bf16[128,448]{1,0:T(8,128)(2,1)S(1)}, bf16[128,448]{1,0:T(8,128)(2,1)S(1)}, u32[]{:S(2)}, u32[]{:S(2)}) collective-permute-start(bf16[128,448]{1,0:T(8,128)(2,1)S(1)} %add_convert_fusion.6), channel_id=1, source_target_pairs={{0,6},{2,0},{4,2},{6,4},{1,7},{3,1},{5,3},{7,5},{8,14},{10,8},{12,... | collective-permute-start | bytes 344072 | tf_op jit(solution)/shard_map/ppermute | solution.py:35
  92.1 19.2 %all-to-all-start.1 = ((bf16[32,48,128]{2,1,0:T(8,128)(2,1)}), bf16[32,48,128]{2,1,0:T(8,128)(2,1)S(1)}, u32[]{:S(2)}, u32[]{:S(2)}) async-start(bf16[32,48,128]{2,1,0:T(8,128)(2,1)} %add_convert_fusion), calls=%async_computation.1 | async-start | bytes 786432 | tf_op jit(solution)/shard_map/all_to_all | solution.py:23
  100.6 39.3 %copy-start.11 = (bf16[8,512]{1,0:T(8,128)(2,1)S(1)}, bf16[8,512]{1,0:T(8,128)(2,1)}, u32[]{:S(2)}) copy-start(bf16[8,512]{1,0:T(8,128)(2,1)} %param.18) | copy-start | bytes 24580
  100.7 2.6 %collective-permute-start.4 = (bf16[128,448]{1,0:T(8,128)(2,1)S(1)}, bf16[128,448]{1,0:T(8,128)(2,1)S(1)}, u32[]{:S(2)}, u32[]{:S(2)}) collective-permute-start(bf16[128,448]{1,0:T(8,128)(2,1)S(1)} %add_convert_fusion.5), channel_id=1, source_target_pairs={{0,1},{1,0},{2,3},{3,2},{4,5},{5,4},{6,7},{7,6},{8,9},{9,8},{10,11... | collective-permute-start | bytes 344072 | tf_op jit(solution)/shard_map/ppermute | solution.py:31
  111.3 5.2 %collective-permute-start.19 = (bf16[48,128]{1,0:T(8,128)(2,1)S(1)}, bf16[48,128]{1,0:T(8,128)(2,1)S(1)}, u32[]{:S(2)}, u32[]{:S(2)}) collective-permute-start(bf16[48,128]{1,0:T(8,128)(2,1)S(1)} %reduce_sum.21), channel_id=1, source_target_pairs={{0,2},{2,4},{4,6},{6,0},{1,3},{3,5},{5,7},{7,1},{8,10},{10,12},{12... | collective-permute-start | bytes 36872 | tf_op jit(solution)/shard_map/ppermute | solution.py:35
  113.9 4.0 %collective-permute-start.20 = (bf16[48,128]{1,0:T(8,128)(2,1)S(1)}, bf16[48,128]{1,0:T(8,128)(2,1)S(1)}, u32[]{:S(2)}, u32[]{:S(2)}) collective-permute-start(bf16[48,128]{1,0:T(8,128)(2,1)S(1)} %reduce_sum.21), channel_id=1, source_target_pairs={{0,4},{2,6},{4,0},{6,2},{1,5},{3,7},{5,1},{7,3},{8,12},{10,14},{12... | collective-permute-start | bytes 36872 | tf_op jit(solution)/shard_map/ppermute | solution.py:35
  116.0 2.5 %collective-permute-start.21 = (bf16[48,128]{1,0:T(8,128)(2,1)S(1)}, bf16[48,128]{1,0:T(8,128)(2,1)S(1)}, u32[]{:S(2)}, u32[]{:S(2)}) collective-permute-start(bf16[48,128]{1,0:T(8,128)(2,1)S(1)} %reduce_sum.21), channel_id=1, source_target_pairs={{0,6},{2,0},{4,2},{6,4},{1,7},{3,1},{5,3},{7,5},{8,14},{10,8},{12,... | collective-permute-start | bytes 36872 | tf_op jit(solution)/shard_map/ppermute | solution.py:35
  118.6 6.7 %collective-permute-start.22 = (bf16[192,128]{1,0:T(8,128)(2,1)S(1)}, bf16[192,128]{1,0:T(8,128)(2,1)S(1)}, u32[]{:S(2)}, u32[]{:S(2)}) collective-permute-start(bf16[192,128]{1,0:T(8,128)(2,1)S(1)} %pad_maximum_fusion.1), channel_id=1, source_target_pairs={{0,1},{1,0},{2,3},{3,2},{4,5},{5,4},{6,7},{7,6},{8,9},{9,8},{10,11... | collective-permute-start | bytes 147464 | tf_op jit(solution)/shard_map/ppermute | solution.py:31
  157.0 4.6 %collective-permute-start.23 = (bf16[128,224]{1,0:T(8,128)(2,1)S(1)}, bf16[128,224]{1,0:T(8,128)(2,1)S(1)}, u32[]{:S(2)}, u32[]{:S(2)}) collective-permute-start(bf16[128,224]{1,0:T(8,128)(2,1)S(1)} %select_convert_fusion.1), channel_id=1, source_target_pairs={{0,1},{1,0},{2,3},{3,2},{4,5},{5,4},{6,7},{7,6},{8,9},{9,8},{10,11... | collective-permute-start | bytes 172040 | tf_op jit(solution)/shard_map/ppermute | solution.py:31
  161.6 5.1 %collective-permute-start.24 = (bf16[128,224]{1,0:T(8,128)(2,1)S(1)}, bf16[128,224]{1,0:T(8,128)(2,1)S(1)}, u32[]{:S(2)}, u32[]{:S(2)}) collective-permute-start(bf16[128,224]{1,0:T(8,128)(2,1)S(1)} %add_convert_fusion.8), channel_id=1, source_target_pairs={{0,2},{2,4},{4,6},{6,0},{1,3},{3,5},{5,7},{7,1},{8,10},{10,12},{12... | collective-permute-start | bytes 172040 | tf_op jit(solution)/shard_map/ppermute | solution.py:35
  161.7 5.5 %collective-permute-start.25 = (bf16[128,224]{1,0:T(8,128)(2,1)S(1)}, bf16[128,224]{1,0:T(8,128)(2,1)S(1)}, u32[]{:S(2)}, u32[]{:S(2)}) collective-permute-start(bf16[128,224]{1,0:T(8,128)(2,1)S(1)} %add_convert_fusion.8), channel_id=1, source_target_pairs={{0,4},{2,6},{4,0},{6,2},{1,5},{3,7},{5,1},{7,3},{8,12},{10,14},{12... | collective-permute-start | bytes 172040 | tf_op jit(solution)/shard_map/ppermute | solution.py:35
  164.2 3.8 %collective-permute-start.26 = (bf16[128,224]{1,0:T(8,128)(2,1)S(1)}, bf16[128,224]{1,0:T(8,128)(2,1)S(1)}, u32[]{:S(2)}, u32[]{:S(2)}) collective-permute-start(bf16[128,224]{1,0:T(8,128)(2,1)S(1)} %add_convert_fusion.8), channel_id=1, source_target_pairs={{0,6},{2,0},{4,2},{6,4},{1,7},{3,1},{5,3},{7,5},{8,14},{10,8},{12,... | collective-permute-start | bytes 172040 | tf_op jit(solution)/shard_map/ppermute | solution.py:35
  168.1 2.4 %collective-permute-start.27 = (bf16[128,224]{1,0:T(8,128)(2,1)S(1)}, bf16[128,224]{1,0:T(8,128)(2,1)S(1)}, u32[]{:S(2)}, u32[]{:S(2)}) collective-permute-start(bf16[128,224]{1,0:T(8,128)(2,1)S(1)} %add_convert_fusion.7.own), channel_id=1, source_target_pairs={{0,1},{1,0},{2,3},{3,2},{4,5},{5,4},{6,7},{7,6},{8,9},{9,8},{10,11... | collective-permute-start | bytes 172040 | tf_op jit(solution)/shard_map/ppermute | solution.py:31

commit v4 on v3

--- a/solution.py
+++ b/solution.py
@@ -104,7 +104,8 @@
     wg, wu, rt, ids, wd = refs[8:13]
     keeps = refs[13:17]
     gives = refs[17:21]
-    gbuf, ubuf, dbuf, hidden, block, sems, dsems = refs[21:]
+    xbuf, gbuf, ubuf, dbuf, hidden, block, obuf, xsems, sems, dsems, osems = refs[21:]
+    outs = tuple(keeps) + tuple(gives)
     row = where[0]
     core = where[NY]
     copies = [weight_copies(where, j, (wg, wu), (gbuf, ubuf), sems) for j in range(NY)]
@@ -113,17 +114,20 @@
         pltpu.make_async_copy(wd.at[pl.ds(j * rows, rows), :], dbuf.at[j], dsems.at[j])
         for j in range(STEPS)
     ]
-    for group in copies:
-        for copy in group:
+    arrivals = [
+        pltpu.make_async_copy(xs[i], xbuf.at[i], xsems.at[i]) for i in range(len(xs))
+    ]
+    for j in range(NY):
+        for copy in copies[j] + arrivals[2 * j : 2 * j + 2]:
             copy.start()
     for copy in downs:
         copy.start()
     g = u = logits = None
     for j in range(NY):
-        for copy in copies[j]:
+        for copy in copies[j] + arrivals[2 * j : 2 * j + 2]:
             copy.wait()
         gate, up, logit = products(
-            xs[2 * j][...], xs[2 * j + 1][...], where[j], gbuf.at[j], ubuf.at[j], rt, core
+            xbuf[2 * j], xbuf[2 * j + 1], where[j], gbuf.at[j], ubuf.at[j], rt, core
         )
         if j == 0:
             g, u, logits = gate, up, logit
@@ -148,19 +152,30 @@
     hidden[half:] = jnp.where(core == 0, high, low).astype(BF)
 
     count = block.shape[0]
+    leaving = []
     for j in range(STEPS):
         downs[j].wait()
         res = dot_nt(dbuf[j], hidden[...])
         block[...] = res.astype(BF).reshape(block.shape)
+        span = pl.ds(j * count, count)
         for s in range(NY):
             at = lax.rem(row + s, NY)
-            keeps[s][j * count : (j + 1) * count] = block[:, at, :, :half]
-            gives[s][j * count : (j + 1) * count] = block[:, at, :, half:]
+            obuf[s, span] = block[:, at, :, :half]
+            obuf[NY + s, span] = block[:, at, :, half:]
+        for i in range(2 * NY):
+            leave = pltpu.make_async_copy(
+                obuf.at[i, span], outs[i].at[span], osems.at[i, j]
+            )
+            leave.start()
+            leaving.append(leave)
+    for leave in leaving:
+        leave.wait()
 
 
 IN_SMEM = pl.BlockSpec(memory_space=pltpu.SMEM)
 IN_VMEM = pl.BlockSpec(memory_space=pltpu.VMEM)
 IN_HBM = pl.BlockSpec(memory_space=pltpu.HBM)
+IN_ANY = pl.BlockSpec(memory_space=pl.ANY)
 
 
 def expert_products(where, xs, w_gate, w_up, router_t, ids, down_t, tokens, chunk):
@@ -172,17 +187,21 @@
         expert_kernel,
         out_shape=(out,) * 8,
         in_specs=[IN_SMEM]
-        + [IN_VMEM] * 8
+        + [IN_ANY] * 8
         + [IN_HBM, IN_HBM, IN_VMEM, IN_VMEM, IN_HBM],
-        out_specs=[IN_VMEM] * 8,
+        out_specs=[IN_ANY] * 8,
         scratch_shapes=[
+            pltpu.VMEM((NE, tokens, chunk), BF),
             pltpu.VMEM((NY, 2 * chunk, hid), BF),
             pltpu.VMEM((NY, 2 * chunk, hid), BF),
             pltpu.VMEM((STEPS, width // STEPS, hid), BF),
             pltpu.VMEM((tokens, hid), BF),
             pltpu.VMEM((ND // STEPS, NY, group, tokens), BF),
+            pltpu.VMEM((2 * NY, ND, group, tokens // 2), BF),
+            pltpu.SemaphoreType.DMA((NE,)),
             pltpu.SemaphoreType.DMA((2, NY)),
             pltpu.SemaphoreType.DMA((STEPS,)),
+            pltpu.SemaphoreType.DMA((2 * NY, STEPS)),
         ],
         compiler_params=pltpu.CompilerParams(vmem_limit_bytes=VMEM_BYTES),
         cost_estimate=pl.CostEstimate(

time: 172 us -> 171 us (level)
  no operation moved by 1% of the time
where the time goes in v4:
time: 171 us
  starting transfers between devices  73.8 us (43%)
  waiting for transfers between devices  36.6 us (21%)
  blocking collectives  30.4 us (18%)
  Pallas kernels  11.6 us (7%)
  local copies, waits for them, and re-layouts  9.6 us (6%)
  other arithmetic  5.42 us (3%)
  matrix products  2.14 us (1%)
    all_to_all x2, blocking collectives, exchange(): return lax.all_to_all(values, axes, 0, 0, tiled=False)  30.4 us
    ppermute x13, starting transfers between devices, swap_cores(): return lax.ppermute(values, 'c', [(0, 1), (1, 0)])  30.4 us
    ppermute x15, starting transfers between devices, along_y(): return lax.ppermute(values, 'y', [(i, (i + shift) % NY) for i in range(NY)])  23.1 us
    all_to_all x2, starting transfers between devices, exchange(): return lax.all_to_all(values, axes, 0, 0, tiled=False)  20.2 us
    all_to_all x2, waiting for transfers between devices, exchange(): return lax.all_to_all(values, axes, 0, 0, tiled=False)  19.6 us
    ppermute x15, waiting for transfers between devices, along_y(): return lax.ppermute(values, 'y', [(i, (i + shift) % NY) for i in range(NY)])  13.2 us
    pallas_call x1, Pallas kernels, expert_products(): pl.pallas_call(expert_kernel, out_shape=(out,) * 8, in_specs=[IN_SMEM] +...  10.4 us
    unnamed x28, local copies, waits for them, and re-layouts  6.16 us
  transfers between devices with their start and end apart: 30, of which 16 were waited for; matrix products, arithmetic and copies ran while one was open for 7% of the time, Pallas kernels for 0%

profile of v4, /device:TPU:1, one launch (start us, length us, event | category | flops | bytes accessed | tf_op | source)
XLA Modules:
  0.0 170.7 jit_solution(14338902527501872871)
XLA Ops:
  0.7 0.8 constant_dynamic-slice_fusion
  1.4 0.7 pad_maximum_fusion.2
  2.1 0.9 broadcast_in_dim.4
  3.0 11.9 %all-to-all-start = ((bf16[32,8,1280]{2,1,0:T(8,128)(2,1)}), bf16[32,8,1280]{2,1,0:T(8,128)(2,1)S(1)}, u32[]{:S(2)}, u32[]{:S(2)}) async-start(bf16[32,8,1280]{2,1,0:T(8,128)(2,1)} %broadcast_in_dim.4), calls=%async_computation | async-start | bytes 1310720 | tf_op jit(solution)/shard_map/all_to_all | solution.py:23
  14.9 4.7 %copy.15 = bf16[1,256,6144]{1,2,0:T(8,128)(2,1)} copy(bf16[1,256,6144]{2,1,0:T(8,128)(2,1)} %param.16) | data formatting | bytes 6291456 | tf_op args[5]
  19.5 11.7 %all-to-all-done = bf16[32,8,1280]{2,1,0:T(8,128)(2,1)S(1)} async-done(((bf16[32,8,1280]{2,1,0:T(8,128)(2,1)}), bf16[32,8,1280]{2,1,0:T(8,128)(2,1)S(1)}, u32[]{:S(2)}, u32[]{:S(2)}) %all-to-all-start) | async-done | bytes 655392 | tf_op jit(solution)/shard_map/all_to_all | solution.py:23
  31.3 3.0 %collective-permute-start.10 = (bf16[256,768]{1,0:T(8,128)(2,1)S(1)}, bf16[256,768]{1,0:T(8,128)(2,1)S(1)}, u32[]{:S(2)}, u32[]{:S(2)}) collective-permute-start(bf16[256,768]{1,0:T(8,128)(2,1)S(1)} %slice.29.refs_0_), channel_id=1, source_target_pairs={{0,4},{2,6},{4,0},{6,2},{1,5},{3,7},{5,1},{7,3},{8,12},{10,14},{12... | collective-permute-start | bytes 1179656 | tf_op jit(solution)/shard_map/ppermute | solution.py:35
  34.3 0.4 collective-permute-start.6
  34.7 2.3 %collective-permute-start.8 = (bf16[256,768]{1,0:T(8,128)(2,1)S(1)}, bf16[256,768]{1,0:T(8,128)(2,1)S(1)}, u32[]{:S(2)}, u32[]{:S(2)}) collective-permute-start(bf16[256,768]{1,0:T(8,128)(2,1)S(1)} %slice.29.refs_0_), channel_id=1, source_target_pairs={{0,6},{2,0},{4,2},{6,4},{1,7},{3,1},{5,3},{7,5},{8,14},{10,8},{12,... | collective-permute-start | bytes 1179656 | tf_op jit(solution)/shard_map/ppermute | solution.py:35
  37.0 5.9 %collective-permute-start.5 = (bf16[256,768]{1,0:T(8,128)(2,1)S(1)}, bf16[256,768]{1,0:T(8,128)(2,1)S(1)}, u32[]{:S(2)}, u32[]{:S(2)}) collective-permute-start(bf16[256,768]{1,0:T(8,128)(2,1)S(1)} %slice.29.refs_0_), channel_id=1, source_target_pairs={{0,1},{1,0},{2,3},{3,2},{4,5},{5,4},{6,7},{7,6},{8,9},{9,8},{10,11... | collective-permute-start | bytes 1179656 | tf_op jit(solution)/shard_map/ppermute | solution.py:31
  42.8 5.9 %collective-permute-start.11 = (bf16[256,768]{1,0:T(8,128)(2,1)S(1)}, bf16[256,768]{1,0:T(8,128)(2,1)S(1)}, u32[]{:S(2)}, u32[]{:S(2)}) collective-permute-start(bf16[256,768]{1,0:T(8,128)(2,1)S(1)} %collective-permute-done.10.refs_6_), channel_id=1, source_target_pairs={{0,1},{1,0},{2,3},{3,2},{4,5},{5,4},{6,7},{7,6},{8,9},{9,8},{10,11... | collective-permute-start | bytes 1179656 | tf_op jit(solution)/shard_map/ppermute | solution.py:31
  48.7 0.9 collective-permute-done.6.refs_2_
  49.6 3.2 %collective-permute-start.7 = (bf16[256,768]{1,0:T(8,128)(2,1)S(1)}, bf16[256,768]{1,0:T(8,128)(2,1)}, u32[]{:S(2)}, u32[]{:S(2)}) collective-permute-start(bf16[256,768]{1,0:T(8,128)(2,1)S(1)} %collective-permute-done.6.refs_2_), channel_id=1, source_target_pairs={{0,1},{1,0},{2,3},{3,2},{4,5},{5,4},{6,7},{7,6},{8,9},{9,8},{10,11... | collective-permute-start | bytes 1179656 | tf_op jit(solution)/shard_map/ppermute | solution.py:31
  52.8 0.4 collective-permute-start.9
  53.2 0.8 copy.18.refs_11_
  54.0 0.6 stack.20.where
  54.9 0.5 copy-done.5
  55.5 10.4 %shard_map.138 = (bf16[32,48,128]{2,1,0:T(8,128)(2,1)}, bf16[32,48,128]{2,1,0:T(8,128)(2,1)}, bf16[32,48,128]{2,1,0:T(8,128)(2,1)}, bf16[32,48,128]{2,1,0:T(8,12...) custom-call(s32[5]{0:T(128)} %stack.20.where, ...), custom_call_target="tpu_custom_call" | custom-call | flops 2415919104 | bytes 15728640 | tf_op jit(solution)/shard_map/pallas_call | solution.py:186
  66.2 0.3 fusion.17
  66.5 0.5 collective-permute-start.15
  66.9 0.3 fusion.19
  67.2 0.2 collective-permute-start.17
  67.4 0.4 collective-permute-start.12
  67.8 0.2 collective-permute-done.13
  68.0 1.1 add_convert_fusion.3
  69.1 2.0 %collective-permute-start.14 = (bf16[32,48,128]{2,1,0:T(8,128)(2,1)S(1)}, bf16[32,48,128]{2,1,0:T(8,128)(2,1)S(1)}, u32[]{:S(2)}, u32[]{:S(2)}) collective-permute-start(bf16[32,48,128]{2,1,0:T(8,128)(2,1)S(1)} %add_convert_fusion.3), channel_id=1, source_target_pairs={{0,4},{2,6},{4,0},{6,2},{1,5},{3,7},{5,1},{7,3},{8,12},{10,14},{12... | collective-permute-start | bytes 1179656 | tf_op jit(solution)/shard_map/ppermute | solution.py:35
  71.1 1.1 add_convert_fusion.2
  72.2 1.1 collective-permute-start.16
  73.4 1.7 collective-permute-start.18
  75.3 1.3 collective-permute-start
  76.6 1.0 collective-permute-done
  77.8 1.7 collective-permute-start.2
  79.5 1.8 %collective-permute-done.14 = bf16[32,48,128]{2,1,0:T(8,128)(2,1)S(1)} collective-permute-done((bf16[32,48,128]{2,1,0:T(8,128)(2,1)S(1)}, bf16[32,48,128]{2,1,0:T(8,128)(2,1)S(1)}, u32[]{:S(2)}, u32[]{:S(2)}) %collective-permute-start.14) | collective-permute-done | bytes 393248 | tf_op jit(solution)/shard_map/ppermute | solution.py:35
  81.3 2.4 %collective-permute-start.3 = (bf16[128,448]{1,0:T(8,128)(2,1)S(1)}, bf16[128,448]{1,0:T(8,128)(2,1)S(1)}, u32[]{:S(2)}, u32[]{:S(2)}) collective-permute-start(bf16[128,448]{1,0:T(8,128)(2,1)S(1)} %add_convert_fusion.6), channel_id=1, source_target_pairs={{0,6},{2,0},{4,2},{6,4},{1,7},{3,1},{5,3},{7,5},{8,14},{10,8},{12,... | collective-permute-start | bytes 344072 | tf_op jit(solution)/shard_map/ppermute | solution.py:35
  83.7 6.5 %collective-permute-done.16 = bf16[32,48,128]{2,1,0:T(8,128)(2,1)S(1)} collective-permute-done((bf16[32,48,128]{2,1,0:T(8,128)(2,1)S(1)}, bf16[32,48,128]{2,1,0:T(8,128)(2,1)S(1)}, u32[]{:S(2)}, u32[]{:S(2)}) %collective-permute-start.16) | collective-permute-done | bytes 393248 | tf_op jit(solution)/shard_map/ppermute | solution.py:35
  90.2 1.0 add_convert_fusion
  91.2 8.4 %all-to-all-start.1 = ((bf16[32,48,128]{2,1,0:T(8,128)(2,1)}), bf16[32,48,128]{2,1,0:T(8,128)(2,1)S(1)}, u32[]{:S(2)}, u32[]{:S(2)}) async-start(bf16[32,48,128]{2,1,0:T(8,128)(2,1)} %add_convert_fusion), calls=%async_computation.1 | async-start | bytes 786432 | tf_op jit(solution)/shard_map/all_to_all | solution.py:23
  99.7 1.5 collective-permute-start.4
  101.2 1.1 fusion.21
  102.4 7.9 %all-to-all-done.1 = bf16[32,48,128]{2,1,0:T(8,128)(2,1)S(1)} async-done(((bf16[32,48,128]{2,1,0:T(8,128)(2,1)}), bf16[32,48,128]{2,1,0:T(8,128)(2,1)S(1)}, u32[]{:S(2)}, u32[]{:S(2)}) %all-to-all-start.1) | async-done | bytes 393248 | tf_op jit(solution)/shard_map/all_to_all | solution.py:23
  110.4 2.6 %collective-permute-start.19 = (bf16[48,128]{1,0:T(8,128)(2,1)S(1)}, bf16[48,128]{1,0:T(8,128)(2,1)S(1)}, u32[]{:S(2)}, u32[]{:S(2)}) collective-permute-start(bf16[48,128]{1,0:T(8,128)(2,1)S(1)} %reduce_sum.21), channel_id=1, source_target_pairs={{0,2},{2,4},{4,6},{6,0},{1,3},{3,5},{5,7},{7,1},{8,10},{10,12},{12... | collective-permute-start | bytes 36872 | tf_op jit(solution)/shard_map/ppermute | solution.py:35
  113.0 2.1 %collective-permute-start.20 = (bf16[48,128]{1,0:T(8,128)(2,1)S(1)}, bf16[48,128]{1,0:T(8,128)(2,1)S(1)}, u32[]{:S(2)}, u32[]{:S(2)}) collective-permute-start(bf16[48,128]{1,0:T(8,128)(2,1)S(1)} %reduce_sum.21), channel_id=1, source_target_pairs={{0,4},{2,6},{4,0},{6,2},{1,5},{3,7},{5,1},{7,3},{8,12},{10,14},{12... | collective-permute-start | bytes 36872 | tf_op jit(solution)/shard_map/ppermute | solution.py:35
  115.1 0.4 collective-permute-start.21
  115.6 1.4 collective-permute-done.20
  117.0 0.6 collective-permute-done.21
  117.6 5.9 %collective-permute-start.22 = (bf16[192,128]{1,0:T(8,128)(2,1)S(1)}, bf16[192,128]{1,0:T(8,128)(2,1)S(1)}, u32[]{:S(2)}, u32[]{:S(2)}) collective-permute-start(bf16[192,128]{1,0:T(8,128)(2,1)S(1)} %pad_maximum_fusion.1), channel_id=1, source_target_pairs={{0,1},{1,0},{2,3},{3,2},{4,5},{5,4},{6,7},{7,6},{8,9},{9,8},{10,11... | collective-permute-start | bytes 147464 | tf_op jit(solution)/shard_map/ppermute | solution.py:31
  123.5 0.2 fusion.23
  123.7 0.7 collective-permute-done.22
  124.4 0.2 fusion.1
  124.7 14.3 %all_to_all.20 = bf16[32,8,512]{2,1,0:T(8,128)(2,1)S(1)} all-to-all(bf16[32,8,512]{2,1,0:T(8,128)(2,1)S(1)} %fusion.1), channel_id=1, replica_groups=mesh['x'=4,'z'=8,'y'=4,'c'=2] {'x','z'}, dimensions={0} | all-to-all | bytes 524288 | tf_op jit(solution)/shard_map/all_to_all | solution.py:23
  139.0 0.6 multiply_convert_fusion.1
  139.6 16.2 %all_to_all.21 = bf16[32,8,512]{2,1,0:T(8,128)(2,1)S(1)} all-to-all(bf16[32,8,512]{2,1,0:T(8,128)(2,1)S(1)} %broadcast_in_dim.5), channel_id=1, replica_groups=mesh['x'=4,'z'=8,'y'=4,'c'=2] {'x','z'}, dimensions={0} | all-to-all | bytes 524288 | tf_op jit(solution)/shard_map/all_to_all | solution.py:23
  155.8 0.2 fusion.4
  156.1 3.7 %collective-permute-start.23 = (bf16[128,224]{1,0:T(8,128)(2,1)S(1)}, bf16[128,224]{1,0:T(8,128)(2,1)S(1)}, u32[]{:S(2)}, u32[]{:S(2)}) collective-permute-start(bf16[128,224]{1,0:T(8,128)(2,1)S(1)} %select_convert_fusion.1), channel_id=1, source_target_pairs={{0,1},{1,0},{2,3},{3,2},{4,5},{5,4},{6,7},{7,6},{8,9},{9,8},{10,11... | collective-permute-start | bytes 172040 | tf_op jit(solution)/shard_map/ppermute | solution.py:31
  159.8 0.9 collective-permute-done.23
  160.8 2.5 %collective-permute-start.25 = (bf16[128,224]{1,0:T(8,128)(2,1)S(1)}, bf16[128,224]{1,0:T(8,128)(2,1)S(1)}, u32[]{:S(2)}, u32[]{:S(2)}) collective-permute-start(bf16[128,224]{1,0:T(8,128)(2,1)S(1)} %add_convert_fusion.8), channel_id=1, source_target_pairs={{0,4},{2,6},{4,0},{6,2},{1,5},{3,7},{5,1},{7,3},{8,12},{10,14},{12... | collective-permute-start | bytes 172040 | tf_op jit(solution)/shard_map/ppermute | solution.py:35
  163.3 0.9 collective-permute-start.26
  164.2 0.9 convolution_convert_fusion
  165.1 0.8 collective-permute-done.24
  165.9 0.4 collective-permute-done.25
  166.2 0.8 collective-permute-done.26
  167.1 1.5 collective-permute-start.27
  168.6 0.9 collective-permute-done.27.other
  169.5 1.1 shard_map.139
  (60 shorter events, 1.7 us)
Async XLA Ops:
  0.6 122.9 %copy-start = (bf16[224,512]{1,0:T(8,128)(2,1)S(1)}, bf16[224,512]{1,0:T(8,128)(2,1)}, u32[]{:S(2)}) copy-start(bf16[224,512]{1,0:T(8,128)(2,1)} %param.21) | copy-start | bytes 688132
  3.0 28.3 %all-to-all-start = ((bf16[32,8,1280]{2,1,0:T(8,128)(2,1)}), bf16[32,8,1280]{2,1,0:T(8,128)(2,1)S(1)}, u32[]{:S(2)}, u32[]{:S(2)}) async-start(bf16[32,8,1280]{2,1,0:T(8,128)(2,1)} %broadcast_in_dim.4), calls=%async_computation | async-start | bytes 1310720 | tf_op jit(solution)/shard_map/all_to_all | solution.py:23
  14.9 38.4 %copy-start.12 = (s32[256,2]{0,1:T(2,128)S(1)}, s32[256,2]{0,1:T(2,128)}, u32[]{:S(2)}) copy-start(s32[256,2]{0,1:T(2,128)} %param.12) | copy-start | bytes 6148
  31.3 23.6 %copy-start.1 = (bf16[256,768]{1,0:T(8,128)(2,1)}, bf16[256,768]{1,0:T(8,128)(2,1)S(1)}, u32[]{:S(2)}) copy-start(bf16[256,768]{1,0:T(8,128)(2,1)S(1)} %slice.29.refs_0_) | copy-start | bytes 1179652
  31.3 11.5 %collective-permute-start.10 = (bf16[256,768]{1,0:T(8,128)(2,1)S(1)}, bf16[256,768]{1,0:T(8,128)(2,1)S(1)}, u32[]{:S(2)}, u32[]{:S(2)}) collective-permute-start(bf16[256,768]{1,0:T(8,128)(2,1)S(1)} %slice.29.refs_0_), channel_id=1, source_target_pairs={{0,4},{2,6},{4,0},{6,2},{1,5},{3,7},{5,1},{7,3},{8,12},{10,14},{12... | collective-permute-start | bytes 1179656 | tf_op jit(solution)/shard_map/ppermute | solution.py:35
  34.3 15.3 %collective-permute-start.6 = (bf16[256,768]{1,0:T(8,128)(2,1)S(1)}, bf16[256,768]{1,0:T(8,128)(2,1)S(1)}, u32[]{:S(2)}, u32[]{:S(2)}) collective-permute-start(bf16[256,768]{1,0:T(8,128)(2,1)S(1)} %slice.29.refs_0_), channel_id=1, source_target_pairs={{0,2},{2,4},{4,6},{6,0},{1,3},{3,5},{5,7},{7,1},{8,10},{10,12},{12... | collective-permute-start | bytes 1179656 | tf_op jit(solution)/shard_map/ppermute | solution.py:35
  34.7 18.2 %collective-permute-start.8 = (bf16[256,768]{1,0:T(8,128)(2,1)S(1)}, bf16[256,768]{1,0:T(8,128)(2,1)S(1)}, u32[]{:S(2)}, u32[]{:S(2)}) collective-permute-start(bf16[256,768]{1,0:T(8,128)(2,1)S(1)} %slice.29.refs_0_), channel_id=1, source_target_pairs={{0,6},{2,0},{4,2},{6,4},{1,7},{3,1},{5,3},{7,5},{8,14},{10,8},{12,... | collective-permute-start | bytes 1179656 | tf_op jit(solution)/shard_map/ppermute | solution.py:35
  37.0 17.7 %collective-permute-start.5 = (bf16[256,768]{1,0:T(8,128)(2,1)S(1)}, bf16[256,768]{1,0:T(8,128)(2,1)S(1)}, u32[]{:S(2)}, u32[]{:S(2)}) collective-permute-start(bf16[256,768]{1,0:T(8,128)(2,1)S(1)} %slice.29.refs_0_), channel_id=1, source_target_pairs={{0,1},{1,0},{2,3},{3,2},{4,5},{5,4},{6,7},{7,6},{8,9},{9,8},{10,11... | collective-permute-start | bytes 1179656 | tf_op jit(solution)/shard_map/ppermute | solution.py:31
  42.8 12.1 %copy-start.2 = (bf16[256,768]{1,0:T(8,128)(2,1)}, bf16[256,768]{1,0:T(8,128)(2,1)S(1)}, u32[]{:S(2)}) copy-start(bf16[256,768]{1,0:T(8,128)(2,1)S(1)} %collective-permute-done.10.refs_6_) | copy-start | bytes 1179652
  42.8 11.8 %collective-permute-start.11 = (bf16[256,768]{1,0:T(8,128)(2,1)S(1)}, bf16[256,768]{1,0:T(8,128)(2,1)S(1)}, u32[]{:S(2)}, u32[]{:S(2)}) collective-permute-start(bf16[256,768]{1,0:T(8,128)(2,1)S(1)} %collective-permute-done.10.refs_6_), channel_id=1, source_target_pairs={{0,1},{1,0},{2,3},{3,2},{4,5},{5,4},{6,7},{7,6},{8,9},{9,8},{10,11... | collective-permute-start | bytes 1179656 | tf_op jit(solution)/shard_map/ppermute | solution.py:31
  49.6 5.3 %copy-start.3 = (bf16[256,768]{1,0:T(8,128)(2,1)}, bf16[256,768]{1,0:T(8,128)(2,1)S(1)}, u32[]{:S(2)}) copy-start(bf16[256,768]{1,0:T(8,128)(2,1)S(1)} %collective-permute-done.6.refs_2_) | copy-start | bytes 1179652
  49.6 5.1 %collective-permute-start.7 = (bf16[256,768]{1,0:T(8,128)(2,1)S(1)}, bf16[256,768]{1,0:T(8,128)(2,1)}, u32[]{:S(2)}, u32[]{:S(2)}) collective-permute-start(bf16[256,768]{1,0:T(8,128)(2,1)S(1)} %collective-permute-done.6.refs_2_), channel_id=1, source_target_pairs={{0,1},{1,0},{2,3},{3,2},{4,5},{5,4},{6,7},{7,6},{8,9},{9,8},{10,11... | collective-permute-start | bytes 1179656 | tf_op jit(solution)/shard_map/ppermute | solution.py:31
  52.8 2.1 %copy-start.4 = (bf16[256,768]{1,0:T(8,128)(2,1)}, bf16[256,768]{1,0:T(8,128)(2,1)S(1)}, u32[]{:S(2)}) copy-start(bf16[256,768]{1,0:T(8,128)(2,1)S(1)} %collective-permute-done.8.refs_4_) | copy-start | bytes 1179652
  52.8 2.0 %collective-permute-start.9 = (bf16[256,768]{1,0:T(8,128)(2,1)S(1)}, bf16[256,768]{1,0:T(8,128)(2,1)}, u32[]{:S(2)}, u32[]{:S(2)}) collective-permute-start(bf16[256,768]{1,0:T(8,128)(2,1)S(1)} %collective-permute-done.8.refs_4_), channel_id=1, source_target_pairs={{0,1},{1,0},{2,3},{3,2},{4,5},{5,4},{6,7},{7,6},{8,9},{9,8},{10,11... | collective-permute-start | bytes 1179656 | tf_op jit(solution)/shard_map/ppermute | solution.py:31
  54.7 0.8 copy-start.5
  54.7 0.9 copy-start.6
  55.5 10.7 %copy-start.9 = (bf16[512,224]{0,1:T(8,128)(2,1)S(1)}, bf16[512,224]{0,1:T(8,128)(2,1)}, u32[]{:S(2)}) copy-start(bf16[512,224]{0,1:T(8,128)(2,1)} %param.20) | copy-start | bytes 688132
  55.5 11.4 %copy-start.10 = (bf16[512,224]{0,1:T(8,128)(2,1)S(1)}, bf16[512,224]{0,1:T(8,128)(2,1)}, u32[]{:S(2)}) copy-start(bf16[512,224]{0,1:T(8,128)(2,1)} %param.19) | copy-start | bytes 688132
  66.0 7.4 %copy-start.8 = (bf16[32,48,128]{2,1,0:T(8,128)(2,1)S(1)}, bf16[32,48,128]{2,1,0:T(8,128)(2,1)}, u32[]{:S(2)}) copy-start(bf16[32,48,128]{2,1,0:T(8,128)(2,1)} %get-tuple-element.34) | copy-start | bytes 1179652
  66.0 24.2 %copy-start.7 = (bf16[32,48,128]{2,1,0:T(8,128)(2,1)S(1)}, bf16[32,48,128]{2,1,0:T(8,128)(2,1)}, u32[]{:S(2)}) copy-start(bf16[32,48,128]{2,1,0:T(8,128)(2,1)} %get-tuple-element.28) | copy-start | bytes 1179652
  66.0 2.0 %collective-permute-start.13 = (bf16[32,48,128]{2,1,0:T(8,128)(2,1)}, bf16[32,48,128]{2,1,0:T(8,128)(2,1)S(1)}, u32[]{:S(2)}, u32[]{:S(2)}) collective-permute-start(bf16[32,48,128]{2,1,0:T(8,128)(2,1)} %get-tuple-element.31), channel_id=1, source_target_pairs={{0,1},{1,0},{2,3},{3,2},{4,5},{5,4},{6,7},{7,6},{8,9},{9,8},{10,11... | collective-permute-start | bytes 1179656 | tf_op jit(solution)/shard_map/ppermute | solution.py:31
  66.5 4.6 %collective-permute-start.15 = (bf16[32,48,128]{2,1,0:T(8,128)(2,1)}, bf16[32,48,128]{2,1,0:T(8,128)(2,1)S(1)}, u32[]{:S(2)}, u32[]{:S(2)}) collective-permute-start(bf16[32,48,128]{2,1,0:T(8,128)(2,1)} %get-tuple-element.33), channel_id=1, source_target_pairs={{0,1},{1,0},{2,3},{3,2},{4,5},{5,4},{6,7},{7,6},{8,9},{9,8},{10,11... | collective-permute-start | bytes 1179656 | tf_op jit(solution)/shard_map/ppermute | solution.py:31
  67.2 6.1 %collective-permute-start.17 = (bf16[32,48,128]{2,1,0:T(8,128)(2,1)}, bf16[32,48,128]{2,1,0:T(8,128)(2,1)S(1)}, u32[]{:S(2)}, u32[]{:S(2)}) collective-permute-start(bf16[32,48,128]{2,1,0:T(8,128)(2,1)} %get-tuple-element.35), channel_id=1, source_target_pairs={{0,1},{1,0},{2,3},{3,2},{4,5},{5,4},{6,7},{7,6},{8,9},{9,8},{10,11... | collective-permute-start | bytes 1179656 | tf_op jit(solution)/shard_map/ppermute | solution.py:31
  67.4 10.4 %collective-permute-start.12 = (bf16[32,48,128]{2,1,0:T(8,128)(2,1)}, bf16[32,48,128]{2,1,0:T(8,128)(2,1)S(1)}, u32[]{:S(2)}, u32[]{:S(2)}) collective-permute-start(bf16[32,48,128]{2,1,0:T(8,128)(2,1)} %get-tuple-element.29), channel_id=1, source_target_pairs={{0,1},{1,0},{2,3},{3,2},{4,5},{5,4},{6,7},{7,6},{8,9},{9,8},{10,11... | collective-permute-start | bytes 1179656 | tf_op jit(solution)/shard_map/ppermute | solution.py:31
  69.1 12.2 %collective-permute-start.14 = (bf16[32,48,128]{2,1,0:T(8,128)(2,1)S(1)}, bf16[32,48,128]{2,1,0:T(8,128)(2,1)S(1)}, u32[]{:S(2)}, u32[]{:S(2)}) collective-permute-start(bf16[32,48,128]{2,1,0:T(8,128)(2,1)S(1)} %add_convert_fusion.3), channel_id=1, source_target_pairs={{0,4},{2,6},{4,0},{6,2},{1,5},{3,7},{5,1},{7,3},{8,12},{10,14},{12... | collective-permute-start | bytes 1179656 | tf_op jit(solution)/shard_map/ppermute | solution.py:35
  72.2 18.0 %collective-permute-start.16 = (bf16[32,48,128]{2,1,0:T(8,128)(2,1)S(1)}, bf16[32,48,128]{2,1,0:T(8,128)(2,1)S(1)}, u32[]{:S(2)}, u32[]{:S(2)}) collective-permute-start(bf16[32,48,128]{2,1,0:T(8,128)(2,1)S(1)} %add_convert_fusion.2), channel_id=1, source_target_pairs={{0,2},{2,4},{4,6},{6,0},{1,3},{3,5},{5,7},{7,1},{8,10},{10,12},{12... | collective-permute-start | bytes 1179656 | tf_op jit(solution)/shard_map/ppermute | solution.py:35
  73.4 16.7 %collective-permute-start.18 = (bf16[32,48,128]{2,1,0:T(8,128)(2,1)S(1)}, bf16[32,48,128]{2,1,0:T(8,128)(2,1)S(1)}, u32[]{:S(2)}, u32[]{:S(2)}) collective-permute-start(bf16[32,48,128]{2,1,0:T(8,128)(2,1)S(1)} %add_convert_fusion.1), channel_id=1, source_target_pairs={{0,6},{2,0},{4,2},{6,4},{1,7},{3,1},{5,3},{7,5},{8,14},{10,8},{12,... | collective-permute-start | bytes 1179656 | tf_op jit(solution)/shard_map/ppermute | solution.py:35
  75.3 2.3 %collective-permute-start = (bf16[128,448]{1,0:T(8,128)(2,1)S(1)}, bf16[128,448]{1,0:T(8,128)(2,1)S(1)}, u32[]{:S(2)}, u32[]{:S(2)}) collective-permute-start(bf16[128,448]{1,0:T(8,128)(2,1)S(1)} %select_convert_fusion), channel_id=1, source_target_pairs={{0,1},{1,0},{2,3},{3,2},{4,5},{5,4},{6,7},{7,6},{8,9},{9,8},{10,11... | collective-permute-start | bytes 344072 | tf_op jit(solution)/shard_map/ppermute | solution.py:31
  77.7 21.9 %collective-permute-start.1 = (bf16[128,448]{1,0:T(8,128)(2,1)S(1)}, bf16[128,448]{1,0:T(8,128)(2,1)S(1)}, u32[]{:S(2)}, u32[]{:S(2)}) collective-permute-start(bf16[128,448]{1,0:T(8,128)(2,1)S(1)} %add_convert_fusion.6), channel_id=1, source_target_pairs={{0,2},{2,4},{4,6},{6,0},{1,3},{3,5},{5,7},{7,1},{8,10},{10,12},{12... | collective-permute-start | bytes 344072 | tf_op jit(solution)/shard_map/ppermute | solution.py:35
  77.8 21.8 %collective-permute-start.2 = (bf16[128,448]{1,0:T(8,128)(2,1)S(1)}, bf16[128,448]{1,0:T(8,128)(2,1)S(1)}, u32[]{:S(2)}, u32[]{:S(2)}) collective-permute-start(bf16[128,448]{1,0:T(8,128)(2,1)S(1)} %add_convert_fusion.6), channel_id=1, source_target_pairs={{0,4},{2,6},{4,0},{6,2},{1,5},{3,7},{5,1},{7,3},{8,12},{10,14},{12... | collective-permute-start | bytes 344072 | tf_op jit(solution)/shard_map/ppermute | solution.py:35
  81.3 18.3 %collective-permute-start.3 = (bf16[128,448]{1,0:T(8,128)(2,1)S(1)}, bf16[128,448]{1,0:T(8,128)(2,1)S(1)}, u32[]{:S(2)}, u32[]{:S(2)}) collective-permute-start(bf16[128,448]{1,0:T(8,128)(2,1)S(1)} %add_convert_fusion.6), channel_id=1, source_target_pairs={{0,6},{2,0},{4,2},{6,4},{1,7},{3,1},{5,3},{7,5},{8,14},{10,8},{12,... | collective-permute-start | bytes 344072 | tf_op jit(solution)/shard_map/ppermute | solution.py:35
  91.2 19.2 %all-to-all-start.1 = ((bf16[32,48,128]{2,1,0:T(8,128)(2,1)}), bf16[32,48,128]{2,1,0:T(8,128)(2,1)S(1)}, u32[]{:S(2)}, u32[]{:S(2)}) async-start(bf16[32,48,128]{2,1,0:T(8,128)(2,1)} %add_convert_fusion), calls=%async_computation.1 | async-start | bytes 786432 | tf_op jit(solution)/shard_map/all_to_all | solution.py:23
  99.7 39.3 %copy-start.11 = (bf16[8,512]{1,0:T(8,128)(2,1)S(1)}, bf16[8,512]{1,0:T(8,128)(2,1)}, u32[]{:S(2)}) copy-start(bf16[8,512]{1,0:T(8,128)(2,1)} %param.18) | copy-start | bytes 24580
  99.7 2.6 %collective-permute-start.4 = (bf16[128,448]{1,0:T(8,128)(2,1)S(1)}, bf16[128,448]{1,0:T(8,128)(2,1)S(1)}, u32[]{:S(2)}, u32[]{:S(2)}) collective-permute-start(bf16[128,448]{1,0:T(8,128)(2,1)S(1)} %add_convert_fusion.5), channel_id=1, source_target_pairs={{0,1},{1,0},{2,3},{3,2},{4,5},{5,4},{6,7},{7,6},{8,9},{9,8},{10,11... | collective-permute-start | bytes 344072 | tf_op jit(solution)/shard_map/ppermute | solution.py:31
  110.4 5.2 %collective-permute-start.19 = (bf16[48,128]{1,0:T(8,128)(2,1)S(1)}, bf16[48,128]{1,0:T(8,128)(2,1)S(1)}, u32[]{:S(2)}, u32[]{:S(2)}) collective-permute-start(bf16[48,128]{1,0:T(8,128)(2,1)S(1)} %reduce_sum.21), channel_id=1, source_target_pairs={{0,2},{2,4},{4,6},{6,0},{1,3},{3,5},{5,7},{7,1},{8,10},{10,12},{12... | collective-permute-start | bytes 36872 | tf_op jit(solution)/shard_map/ppermute | solution.py:35
  113.0 4.0 %collective-permute-start.20 = (bf16[48,128]{1,0:T(8,128)(2,1)S(1)}, bf16[48,128]{1,0:T(8,128)(2,1)S(1)}, u32[]{:S(2)}, u32[]{:S(2)}) collective-permute-start(bf16[48,128]{1,0:T(8,128)(2,1)S(1)} %reduce_sum.21), channel_id=1, source_target_pairs={{0,4},{2,6},{4,0},{6,2},{1,5},{3,7},{5,1},{7,3},{8,12},{10,14},{12... | collective-permute-start | bytes 36872 | tf_op jit(solution)/shard_map/ppermute | solution.py:35
  115.1 2.5 %collective-permute-start.21 = (bf16[48,128]{1,0:T(8,128)(2,1)S(1)}, bf16[48,128]{1,0:T(8,128)(2,1)S(1)}, u32[]{:S(2)}, u32[]{:S(2)}) collective-permute-start(bf16[48,128]{1,0:T(8,128)(2,1)S(1)} %reduce_sum.21), channel_id=1, source_target_pairs={{0,6},{2,0},{4,2},{6,4},{1,7},{3,1},{5,3},{7,5},{8,14},{10,8},{12,... | collective-permute-start | bytes 36872 | tf_op jit(solution)/shard_map/ppermute | solution.py:35
  117.6 6.7 %collective-permute-start.22 = (bf16[192,128]{1,0:T(8,128)(2,1)S(1)}, bf16[192,128]{1,0:T(8,128)(2,1)S(1)}, u32[]{:S(2)}, u32[]{:S(2)}) collective-permute-start(bf16[192,128]{1,0:T(8,128)(2,1)S(1)} %pad_maximum_fusion.1), channel_id=1, source_target_pairs={{0,1},{1,0},{2,3},{3,2},{4,5},{5,4},{6,7},{7,6},{8,9},{9,8},{10,11... | collective-permute-start | bytes 147464 | tf_op jit(solution)/shard_map/ppermute | solution.py:31
  156.1 4.6 %collective-permute-start.23 = (bf16[128,224]{1,0:T(8,128)(2,1)S(1)}, bf16[128,224]{1,0:T(8,128)(2,1)S(1)}, u32[]{:S(2)}, u32[]{:S(2)}) collective-permute-start(bf16[128,224]{1,0:T(8,128)(2,1)S(1)} %select_convert_fusion.1), channel_id=1, source_target_pairs={{0,1},{1,0},{2,3},{3,2},{4,5},{5,4},{6,7},{7,6},{8,9},{9,8},{10,11... | collective-permute-start | bytes 172040 | tf_op jit(solution)/shard_map/ppermute | solution.py:31
  160.7 5.2 %collective-permute-start.24 = (bf16[128,224]{1,0:T(8,128)(2,1)S(1)}, bf16[128,224]{1,0:T(8,128)(2,1)S(1)}, u32[]{:S(2)}, u32[]{:S(2)}) collective-permute-start(bf16[128,224]{1,0:T(8,128)(2,1)S(1)} %add_convert_fusion.8), channel_id=1, source_target_pairs={{0,2},{2,4},{4,6},{6,0},{1,3},{3,5},{5,7},{7,1},{8,10},{10,12},{12... | collective-permute-start | bytes 172040 | tf_op jit(solution)/shard_map/ppermute | solution.py:35
  160.8 5.4 %collective-permute-start.25 = (bf16[128,224]{1,0:T(8,128)(2,1)S(1)}, bf16[128,224]{1,0:T(8,128)(2,1)S(1)}, u32[]{:S(2)}, u32[]{:S(2)}) collective-permute-start(bf16[128,224]{1,0:T(8,128)(2,1)S(1)} %add_convert_fusion.8), channel_id=1, source_target_pairs={{0,4},{2,6},{4,0},{6,2},{1,5},{3,7},{5,1},{7,3},{8,12},{10,14},{12... | collective-permute-start | bytes 172040 | tf_op jit(solution)/shard_map/ppermute | solution.py:35
  163.3 3.8 %collective-permute-start.26 = (bf16[128,224]{1,0:T(8,128)(2,1)S(1)}, bf16[128,224]{1,0:T(8,128)(2,1)S(1)}, u32[]{:S(2)}, u32[]{:S(2)}) collective-permute-start(bf16[128,224]{1,0:T(8,128)(2,1)S(1)} %add_convert_fusion.8), channel_id=1, source_target_pairs={{0,6},{2,0},{4,2},{6,4},{1,7},{3,1},{5,3},{7,5},{8,14},{10,8},{12,... | collective-permute-start | bytes 172040 | tf_op jit(solution)/shard_map/ppermute | solution.py:35
  167.1 2.4 %collective-permute-start.27 = (bf16[128,224]{1,0:T(8,128)(2,1)S(1)}, bf16[128,224]{1,0:T(8,128)(2,1)S(1)}, u32[]{:S(2)}, u32[]{:S(2)}) collective-permute-start(bf16[128,224]{1,0:T(8,128)(2,1)S(1)} %add_convert_fusion.7.own), channel_id=1, source_target_pairs={{0,1},{1,0},{2,3},{3,2},{4,5},{5,4},{6,7},{7,6},{8,9},{9,8},{10,11... | collective-permute-start | bytes 172040 | tf_op jit(solution)/shard_map/ppermute | solution.py:31

commit v5 on v4

--- a/solution.py
+++ b/solution.py
@@ -99,15 +99,16 @@
     )
 
 
-def expert_kernel(where, *refs):
+def expert_kernel(*refs):
     xs = refs[:8]
     wg, wu, rt, ids, wd = refs[8:13]
     keeps = refs[13:17]
     gives = refs[17:21]
     xbuf, gbuf, ubuf, dbuf, hidden, block, obuf, xsems, sems, dsems, osems = refs[21:]
     outs = tuple(keeps) + tuple(gives)
-    row = where[0]
-    core = where[NY]
+    row = lax.axis_index("y")
+    core = lax.axis_index("c")
+    where = [row] + [lax.rem(row - s + NY, NY) for s in (1, 3, 2)]
     copies = [weight_copies(where, j, (wg, wu), (gbuf, ubuf), sems) for j in range(NY)]
     rows = dbuf.shape[1]
     downs = [
@@ -172,13 +173,45 @@
         leave.wait()
 
 
-IN_SMEM = pl.BlockSpec(memory_space=pltpu.SMEM)
 IN_VMEM = pl.BlockSpec(memory_space=pltpu.VMEM)
 IN_HBM = pl.BlockSpec(memory_space=pltpu.HBM)
 IN_ANY = pl.BlockSpec(memory_space=pl.ANY)
 
 
-def expert_products(where, xs, w_gate, w_up, router_t, ids, down_t, tokens, chunk):
+def first_kernel(teacher, student, out, part, own, sems):
+    chunk = part.shape[1]
+    place = lax.axis_index("y") * NC + lax.axis_index("c")
+    start = pl.multiple_of(place * chunk, 256)
+    copies = [
+        pltpu.make_async_copy(teacher.at[:, pl.ds(start, chunk)], part, sems.at[0]),
+        pltpu.make_async_copy(student, own, sems.at[1]),
+    ]
+    for copy in copies:
+        copy.start()
+    for copy in copies:
+        copy.wait()
+    for d in range(ND):
+        out[d, :, :chunk] = part[...]
+        out[d, :, chunk:] = own[...]
+
+
+def first_payload(teacher_in, student_in, chunk):
+    rows, cols = student_in.shape
+    return pl.pallas_call(
+        first_kernel,
+        out_shape=jax.ShapeDtypeStruct((ND, rows, chunk + cols), BF),
+        in_specs=[IN_ANY, IN_ANY],
+        out_specs=IN_VMEM,
+        scratch_shapes=[
+            pltpu.VMEM((rows, chunk), BF),
+            pltpu.VMEM((rows, cols), BF),
+            pltpu.SemaphoreType.DMA((2,)),
+        ],
+        compiler_params=pltpu.CompilerParams(vmem_limit_bytes=VMEM_BYTES),
+    )(teacher_in, student_in)
+
+
+def expert_products(xs, w_gate, w_up, router_t, ids, down_t, tokens, chunk):
     hid = w_gate.shape[2]
     width = down_t.shape[0]
     group = width // (ND * NY)
@@ -186,8 +219,7 @@
     return pl.pallas_call(
         expert_kernel,
         out_shape=(out,) * 8,
-        in_specs=[IN_SMEM]
-        + [IN_ANY] * 8
+        in_specs=[IN_ANY] * 8
         + [IN_HBM, IN_HBM, IN_VMEM, IN_VMEM, IN_HBM],
         out_specs=[IN_ANY] * 8,
         scratch_shapes=[
@@ -209,12 +241,12 @@
             bytes_accessed=2 * NE * chunk * (2 * hid + tokens) + 2 * width * (hid + tokens),
             transcendentals=tokens * hid,
         ),
-    )(where, *xs, w_gate, w_up, router_t, ids, down_t)
-
-
-def grad_kernel(core_ref, own, other, gate, up, student, gate_grad, up_grad):
+    )(*xs, w_gate, w_up, router_t, ids, down_t)
+
+
+def grad_kernel(own, other, gate, up, student, gate_grad, up_grad):
     half = own.shape[0]
-    core = core_ref[0]
+    core = lax.axis_index("c")
     total_gate = None
     for side, d_ref in enumerate((own, other)):
         at = core if side == 0 else 1 - core
@@ -233,16 +265,15 @@
             up_grad[...] = (total_up + dot_tn(d_up, tokens)).astype(BF)
 
 
-def weight_grads(core, own, other, gate_s, up_s, student_all):
+def weight_grads(own, other, gate_s, up_s, student_all):
     out = jax.ShapeDtypeStruct((gate_s.shape[1], student_all.shape[1]), BF)
     return pl.pallas_call(
         grad_kernel,
         out_shape=(out, out),
-        in_specs=[pl.BlockSpec(memory_space=pltpu.SMEM)]
-        + [pl.BlockSpec(memory_space=pltpu.VMEM)] * 5,
+        in_specs=[pl.BlockSpec(memory_space=pltpu.VMEM)] * 5,
         out_specs=[pl.BlockSpec(memory_space=pltpu.VMEM)] * 2,
         compiler_params=pltpu.CompilerParams(vmem_limit_bytes=16 * 1024 * 1024),
-    )(core, own, other, gate_s, up_s, student_all)
+    )(own, other, gate_s, up_s, student_all)
 
 
 def body(
@@ -269,9 +300,8 @@
     half = tokens // 2
     group = width // (ND * NY)
 
-    part = lax.dynamic_slice_in_dim(teacher_in, expert * chunk, chunk, 1)
-    sent = jnp.concatenate([part, student_in], axis=1)
-    arrived = spread(sent, DP, ND).reshape(tokens, chunk + sd_dev)
+    sent = first_payload(teacher_in, student_in, chunk)
+    arrived = exchange(sent, DP).reshape(tokens, chunk + sd_dev)
     arrived, down_t = lax.optimization_barrier((arrived, w_down[0].T))
     own = arrived[:, :chunk]
     student_all = arrived[:, chunk:]
@@ -280,13 +310,11 @@
     far = [along_y(own, s) for s in range(1, NY)]
     own_other = swap_cores(own)
     far_other = [swap_cores(v) for v in far]
-    xs, spots = [own, own_other], [row]
+    xs = [own, own_other]
     for s in (1, 3, 2):
         xs += [far[s - 1], far_other[s - 1]]
-        spots.append(lax.rem(row - s + NY, NY))
-    where = jnp.stack(spots + [core]).astype(jnp.int32)
     parts = expert_products(
-        where, xs, w_gate, w_up, router_t, route_ids, down_t, tokens, chunk
+        xs, w_gate, w_up, router_t, route_ids, down_t, tokens, chunk
     )
     pair_mine = core_sum(
         jnp.concatenate([dot(student_all, s_gate), dot(student_all, s_up)], axis=1), core
@@ -336,8 +364,7 @@
     d_mine, d_other, grad_down = row_sum(
         core_sum(dot_nt(cotangent_all, s_down), core), grad_down
     )
-    core_at = jnp.reshape(core, (1,)).astype(jnp.int32)
-    grad_gate, grad_up = weight_grads(core_at, d_mine, d_other, gate_s, up_s, student_all)
+    grad_gate, grad_up = weight_grads(d_mine, d_other, gate_s, up_s, student_all)
     grad_gate = grad_gate.T
     grad_up = grad_up.T
     return (grad_gate, grad_up, grad_down, mismatch)

time: 171 us -> 170 us (level)
  local copies, waits for them, and re-layouts: 9.6 us -> 6.73 us
    pallas_call x1 -> x2, Pallas kernels: 10.4 us -> 12.1 us  [the longest x1 10.4 us: expert_products(): pl.pallas_call(expert_kernel, out_shape=(out,) * 8, in_specs=[IN_ANY] * 8...]
where the time goes in v5:
time: 170 us
  starting transfers between devices  74.6 us (44%)
  waiting for transfers between devices  36.8 us (22%)
  blocking collectives  30.5 us (18%)
  Pallas kernels  13.2 us (8%)
  local copies, waits for them, and re-layouts  6.73 us (4%)
  other arithmetic  4.72 us (3%)
  matrix products  2.15 us (1%)
    ppermute x13, starting transfers between devices, swap_cores(): return lax.ppermute(values, 'c', [(0, 1), (1, 0)])  30.5 us
    all_to_all x2, blocking collectives, exchange(): return lax.all_to_all(values, axes, 0, 0, tiled=False)  30.5 us
    ppermute x15, starting transfers between devices, along_y(): return lax.ppermute(values, 'y', [(i, (i + shift) % NY) for i in range(NY)])  23.8 us
    all_to_all x2, starting transfers between devices, exchange(): return lax.all_to_all(values, axes, 0, 0, tiled=False)  20.3 us
    all_to_all x2, waiting for transfers between devices, exchange(): return lax.all_to_all(values, axes, 0, 0, tiled=False)  19.6 us
    ppermute x15, waiting for transfers between devices, along_y(): return lax.ppermute(values, 'y', [(i, (i + shift) % NY) for i in range(NY)])  12.9 us
    pallas_call x1, Pallas kernels, expert_products(): pl.pallas_call(expert_kernel, out_shape=(out,) * 8, in_specs=[IN_ANY] * 8...  10.4 us
    unnamed x28, local copies, waits for them, and re-layouts  5.54 us
  transfers between devices with their start and end apart: 30, of which 16 were waited for; matrix products, arithmetic and copies ran while one was open for 7% of the time, Pallas kernels for 0%

profile of v5, /device:TPU:1, one launch (start us, length us, event | category | flops | bytes accessed | tf_op | source)
XLA Modules:
  0.0 169.6 jit_solution(8200968693407304691)
XLA Ops:
  0.6 1.7 shard_map.138
  2.3 11.9 %all-to-all-start = ((bf16[32,8,1280]{2,1,0:T(8,128)(2,1)}), bf16[32,8,1280]{2,1,0:T(8,128)(2,1)S(1)}, u32[]{:S(2)}, u32[]{:S(2)}) async-start(bf16[32,8,1280]{2,1,0:T(8,128)(2,1)} %shard_map.138), calls=%async_computation | async-start | bytes 1310720 | tf_op jit(solution)/shard_map/all_to_all | solution.py:23
  14.2 4.7 %copy.15 = bf16[1,256,6144]{1,2,0:T(8,128)(2,1)} copy(bf16[1,256,6144]{2,1,0:T(8,128)(2,1)} %param.16) | data formatting | bytes 6291456 | tf_op args[5]
  18.9 11.7 %all-to-all-done = bf16[32,8,1280]{2,1,0:T(8,128)(2,1)S(1)} async-done(((bf16[32,8,1280]{2,1,0:T(8,128)(2,1)}), bf16[32,8,1280]{2,1,0:T(8,128)(2,1)S(1)}, u32[]{:S(2)}, u32[]{:S(2)}) %all-to-all-start) | async-done | bytes 655392 | tf_op jit(solution)/shard_map/all_to_all | solution.py:23
  30.6 3.0 %collective-permute-start.10 = (bf16[256,768]{1,0:T(8,128)(2,1)S(1)}, bf16[256,768]{1,0:T(8,128)(2,1)S(1)}, u32[]{:S(2)}, u32[]{:S(2)}) collective-permute-start(bf16[256,768]{1,0:T(8,128)(2,1)S(1)} %slice.29.refs_0_), channel_id=1, source_target_pairs={{0,4},{2,6},{4,0},{6,2},{1,5},{3,7},{5,1},{7,3},{8,12},{10,14},{12... | collective-permute-start | bytes 1179656 | tf_op jit(solution)/shard_map/ppermute | solution.py:35
  33.6 0.4 collective-permute-start.6
  34.0 2.3 %collective-permute-start.8 = (bf16[256,768]{1,0:T(8,128)(2,1)S(1)}, bf16[256,768]{1,0:T(8,128)(2,1)S(1)}, u32[]{:S(2)}, u32[]{:S(2)}) collective-permute-start(bf16[256,768]{1,0:T(8,128)(2,1)S(1)} %slice.29.refs_0_), channel_id=1, source_target_pairs={{0,6},{2,0},{4,2},{6,4},{1,7},{3,1},{5,3},{7,5},{8,14},{10,8},{12,... | collective-permute-start | bytes 1179656 | tf_op jit(solution)/shard_map/ppermute | solution.py:35
  36.3 5.9 %collective-permute-start.5 = (bf16[256,768]{1,0:T(8,128)(2,1)S(1)}, bf16[256,768]{1,0:T(8,128)(2,1)S(1)}, u32[]{:S(2)}, u32[]{:S(2)}) collective-permute-start(bf16[256,768]{1,0:T(8,128)(2,1)S(1)} %slice.29.refs_0_), channel_id=1, source_target_pairs={{0,1},{1,0},{2,3},{3,2},{4,5},{5,4},{6,7},{7,6},{8,9},{9,8},{10,11... | collective-permute-start | bytes 1179656 | tf_op jit(solution)/shard_map/ppermute | solution.py:31
  42.2 5.9 %collective-permute-start.11 = (bf16[256,768]{1,0:T(8,128)(2,1)S(1)}, bf16[256,768]{1,0:T(8,128)(2,1)S(1)}, u32[]{:S(2)}, u32[]{:S(2)}) collective-permute-start(bf16[256,768]{1,0:T(8,128)(2,1)S(1)} %collective-permute-done.10.refs_6_), channel_id=1, source_target_pairs={{0,1},{1,0},{2,3},{3,2},{4,5},{5,4},{6,7},{7,6},{8,9},{9,8},{10,11... | collective-permute-start | bytes 1179656 | tf_op jit(solution)/shard_map/ppermute | solution.py:31
  48.1 0.9 collective-permute-done.6.refs_2_
  49.0 3.2 %collective-permute-start.7 = (bf16[256,768]{1,0:T(8,128)(2,1)S(1)}, bf16[256,768]{1,0:T(8,128)(2,1)}, u32[]{:S(2)}, u32[]{:S(2)}) collective-permute-start(bf16[256,768]{1,0:T(8,128)(2,1)S(1)} %collective-permute-done.6.refs_2_), channel_id=1, source_target_pairs={{0,1},{1,0},{2,3},{3,2},{4,5},{5,4},{6,7},{7,6},{8,9},{9,8},{10,11... | collective-permute-start | bytes 1179656 | tf_op jit(solution)/shard_map/ppermute | solution.py:31
  52.2 0.4 collective-permute-start.9
  52.6 0.8 copy.18.refs_11_
  53.4 0.3 collective-permute-done.7.refs_3_
  53.7 0.6 collective-permute-done.9.refs_5_
  54.3 10.4 %shard_map.139 = (bf16[32,48,128]{2,1,0:T(8,128)(2,1)}, bf16[32,48,128]{2,1,0:T(8,128)(2,1)}, bf16[32,48,128]{2,1,0:T(8,128)(2,1)}, bf16[32,48,128]{2,1,0:T(8,12...) custom-call(bf16[256,768]{1,0:T(8,128)(2,1)} %copy-done.1, ...), custom_call_target="tpu_custom_call" | custom-call | flops 2415919104 | bytes 15728640 | tf_op jit(solution)/shard_map/pallas_call | solution.py:219
  64.7 0.5 collective-permute-start.13
  65.2 0.3 fusion.17
  65.4 0.2 collective-permute-start.15
  65.7 0.3 fusion.19
  65.9 0.5 collective-permute-start.17
  66.4 0.3 collective-permute-start.12
  66.7 1.1 add_convert_fusion.3
  67.8 2.2 %collective-permute-start.14 = (bf16[32,48,128]{2,1,0:T(8,128)(2,1)S(1)}, bf16[32,48,128]{2,1,0:T(8,128)(2,1)S(1)}, u32[]{:S(2)}, u32[]{:S(2)}) collective-permute-start(bf16[32,48,128]{2,1,0:T(8,128)(2,1)S(1)} %add_convert_fusion.3), channel_id=1, source_target_pairs={{0,4},{2,6},{4,0},{6,2},{1,5},{3,7},{5,1},{7,3},{8,12},{10,14},{12... | collective-permute-start | bytes 1179656 | tf_op jit(solution)/shard_map/ppermute | solution.py:35
  70.1 1.1 add_convert_fusion.2
  71.2 0.9 collective-permute-start.16
  72.2 2.0 %collective-permute-start.18 = (bf16[32,48,128]{2,1,0:T(8,128)(2,1)S(1)}, bf16[32,48,128]{2,1,0:T(8,128)(2,1)S(1)}, u32[]{:S(2)}, u32[]{:S(2)}) collective-permute-start(bf16[32,48,128]{2,1,0:T(8,128)(2,1)S(1)} %add_convert_fusion.1), channel_id=1, source_target_pairs={{0,6},{2,0},{4,2},{6,4},{1,7},{3,1},{5,3},{7,5},{8,14},{10,8},{12,... | collective-permute-start | bytes 1179656 | tf_op jit(solution)/shard_map/ppermute | solution.py:35
  74.1 0.1 select_convert_fusion
  74.3 1.3 collective-permute-start
  75.6 1.0 collective-permute-done
  76.5 0.2 add_convert_fusion.6
  76.8 1.7 %collective-permute-start.2 = (bf16[128,448]{1,0:T(8,128)(2,1)S(1)}, bf16[128,448]{1,0:T(8,128)(2,1)S(1)}, u32[]{:S(2)}, u32[]{:S(2)}) collective-permute-start(bf16[128,448]{1,0:T(8,128)(2,1)S(1)} %add_convert_fusion.6), channel_id=1, source_target_pairs={{0,4},{2,6},{4,0},{6,2},{1,5},{3,7},{5,1},{7,3},{8,12},{10,14},{12... | collective-permute-start | bytes 344072 | tf_op jit(solution)/shard_map/ppermute | solution.py:35
  78.5 1.3 collective-permute-done.14
  79.8 2.5 %collective-permute-start.3 = (bf16[128,448]{1,0:T(8,128)(2,1)S(1)}, bf16[128,448]{1,0:T(8,128)(2,1)S(1)}, u32[]{:S(2)}, u32[]{:S(2)}) collective-permute-start(bf16[128,448]{1,0:T(8,128)(2,1)S(1)} %add_convert_fusion.6), channel_id=1, source_target_pairs={{0,6},{2,0},{4,2},{6,4},{1,7},{3,1},{5,3},{7,5},{8,14},{10,8},{12,... | collective-permute-start | bytes 344072 | tf_op jit(solution)/shard_map/ppermute | solution.py:35
  82.3 6.6 %collective-permute-done.16 = bf16[32,48,128]{2,1,0:T(8,128)(2,1)S(1)} collective-permute-done((bf16[32,48,128]{2,1,0:T(8,128)(2,1)S(1)}, bf16[32,48,128]{2,1,0:T(8,128)(2,1)S(1)}, u32[]{:S(2)}, u32[]{:S(2)}) %collective-permute-start.16) | collective-permute-done | bytes 393248 | tf_op jit(solution)/shard_map/ppermute | solution.py:35
  88.9 1.0 add_convert_fusion
  89.9 8.4 %all-to-all-start.1 = ((bf16[32,48,128]{2,1,0:T(8,128)(2,1)}), bf16[32,48,128]{2,1,0:T(8,128)(2,1)S(1)}, u32[]{:S(2)}, u32[]{:S(2)}) async-start(bf16[32,48,128]{2,1,0:T(8,128)(2,1)} %add_convert_fusion), calls=%async_computation.1 | async-start | bytes 786432 | tf_op jit(solution)/shard_map/all_to_all | solution.py:23
  98.5 1.5 collective-permute-start.4
  100.0 1.1 fusion.21
  101.2 7.9 %all-to-all-done.1 = bf16[32,48,128]{2,1,0:T(8,128)(2,1)S(1)} async-done(((bf16[32,48,128]{2,1,0:T(8,128)(2,1)}), bf16[32,48,128]{2,1,0:T(8,128)(2,1)S(1)}, u32[]{:S(2)}, u32[]{:S(2)}) %all-to-all-start.1) | async-done | bytes 393248 | tf_op jit(solution)/shard_map/all_to_all | solution.py:23
  109.1 2.8 %collective-permute-start.19 = (bf16[48,128]{1,0:T(8,128)(2,1)S(1)}, bf16[48,128]{1,0:T(8,128)(2,1)S(1)}, u32[]{:S(2)}, u32[]{:S(2)}) collective-permute-start(bf16[48,128]{1,0:T(8,128)(2,1)S(1)} %reduce_sum.21), channel_id=1, source_target_pairs={{0,2},{2,4},{4,6},{6,0},{1,3},{3,5},{5,7},{7,1},{8,10},{10,12},{12... | collective-permute-start | bytes 36872 | tf_op jit(solution)/shard_map/ppermute | solution.py:35
  112.0 1.9 %collective-permute-start.20 = (bf16[48,128]{1,0:T(8,128)(2,1)S(1)}, bf16[48,128]{1,0:T(8,128)(2,1)S(1)}, u32[]{:S(2)}, u32[]{:S(2)}) collective-permute-start(bf16[48,128]{1,0:T(8,128)(2,1)S(1)} %reduce_sum.21), channel_id=1, source_target_pairs={{0,4},{2,6},{4,0},{6,2},{1,5},{3,7},{5,1},{7,3},{8,12},{10,14},{12... | collective-permute-start | bytes 36872 | tf_op jit(solution)/shard_map/ppermute | solution.py:35
  113.9 0.6 collective-permute-start.21
  114.5 0.1 fusion.22
  114.6 1.4 collective-permute-done.20
  116.0 0.4 collective-permute-done.21
  116.4 5.9 %collective-permute-start.22 = (bf16[192,128]{1,0:T(8,128)(2,1)S(1)}, bf16[192,128]{1,0:T(8,128)(2,1)S(1)}, u32[]{:S(2)}, u32[]{:S(2)}) collective-permute-start(bf16[192,128]{1,0:T(8,128)(2,1)S(1)} %pad_maximum_fusion.1), channel_id=1, source_target_pairs={{0,1},{1,0},{2,3},{3,2},{4,5},{5,4},{6,7},{7,6},{8,9},{9,8},{10,11... | collective-permute-start | bytes 147464 | tf_op jit(solution)/shard_map/ppermute | solution.py:31
  122.3 0.2 fusion.23
  122.5 0.7 collective-permute-done.22
  123.2 0.3 fusion.1
  123.5 14.3 %all_to_all.20 = bf16[32,8,512]{2,1,0:T(8,128)(2,1)S(1)} all-to-all(bf16[32,8,512]{2,1,0:T(8,128)(2,1)S(1)} %fusion.1), channel_id=1, replica_groups=mesh['x'=4,'z'=8,'y'=4,'c'=2] {'x','z'}, dimensions={0} | all-to-all | bytes 524288 | tf_op jit(solution)/shard_map/all_to_all | solution.py:23
  137.8 0.6 multiply_convert_fusion.1
  138.4 16.2 %all_to_all.21 = bf16[32,8,512]{2,1,0:T(8,128)(2,1)S(1)} all-to-all(bf16[32,8,512]{2,1,0:T(8,128)(2,1)S(1)} %broadcast_in_dim.2), channel_id=1, replica_groups=mesh['x'=4,'z'=8,'y'=4,'c'=2] {'x','z'}, dimensions={0} | all-to-all | bytes 524288 | tf_op jit(solution)/shard_map/all_to_all | solution.py:23
  154.6 0.2 fusion.4
  154.9 3.7 %collective-permute-start.23 = (bf16[128,224]{1,0:T(8,128)(2,1)S(1)}, bf16[128,224]{1,0:T(8,128)(2,1)S(1)}, u32[]{:S(2)}, u32[]{:S(2)}) collective-permute-start(bf16[128,224]{1,0:T(8,128)(2,1)S(1)} %select_convert_fusion.1), channel_id=1, source_target_pairs={{0,1},{1,0},{2,3},{3,2},{4,5},{5,4},{6,7},{7,6},{8,9},{9,8},{10,11... | collective-permute-start | bytes 172040 | tf_op jit(solution)/shard_map/ppermute | solution.py:31
  158.6 0.9 collective-permute-done.23
  159.6 2.7 %collective-permute-start.25 = (bf16[128,224]{1,0:T(8,128)(2,1)S(1)}, bf16[128,224]{1,0:T(8,128)(2,1)S(1)}, u32[]{:S(2)}, u32[]{:S(2)}) collective-permute-start(bf16[128,224]{1,0:T(8,128)(2,1)S(1)} %add_convert_fusion.8), channel_id=1, source_target_pairs={{0,4},{2,6},{4,0},{6,2},{1,5},{3,7},{5,1},{7,3},{8,12},{10,14},{12... | collective-permute-start | bytes 172040 | tf_op jit(solution)/shard_map/ppermute | solution.py:35
  162.3 0.7 collective-permute-start.26
  163.0 0.9 convolution_convert_fusion
  163.9 1.3 collective-permute-done.25
  165.2 0.9 collective-permute-done.26
  166.2 1.4 collective-permute-start.27
  167.6 0.9 collective-permute-done.27.other
  168.5 1.1 shard_map.140
  (57 shorter events, 0.9 us)
Async XLA Ops:
  0.6 121.7 %copy-start = (bf16[224,512]{1,0:T(8,128)(2,1)S(1)}, bf16[224,512]{1,0:T(8,128)(2,1)}, u32[]{:S(2)}) copy-start(bf16[224,512]{1,0:T(8,128)(2,1)} %param.21) | copy-start | bytes 688132
  2.3 28.3 %all-to-all-start = ((bf16[32,8,1280]{2,1,0:T(8,128)(2,1)}), bf16[32,8,1280]{2,1,0:T(8,128)(2,1)S(1)}, u32[]{:S(2)}, u32[]{:S(2)}) async-start(bf16[32,8,1280]{2,1,0:T(8,128)(2,1)} %shard_map.138), calls=%async_computation | async-start | bytes 1310720 | tf_op jit(solution)/shard_map/all_to_all | solution.py:23
  14.2 38.4 %copy-start.12 = (s32[256,2]{0,1:T(2,128)S(1)}, s32[256,2]{0,1:T(2,128)}, u32[]{:S(2)}) copy-start(s32[256,2]{0,1:T(2,128)} %param.12) | copy-start | bytes 6148
  30.6 23.6 %copy-start.1 = (bf16[256,768]{1,0:T(8,128)(2,1)}, bf16[256,768]{1,0:T(8,128)(2,1)S(1)}, u32[]{:S(2)}) copy-start(bf16[256,768]{1,0:T(8,128)(2,1)S(1)} %slice.29.refs_0_) | copy-start | bytes 1179652
  30.6 11.5 %collective-permute-start.10 = (bf16[256,768]{1,0:T(8,128)(2,1)S(1)}, bf16[256,768]{1,0:T(8,128)(2,1)S(1)}, u32[]{:S(2)}, u32[]{:S(2)}) collective-permute-start(bf16[256,768]{1,0:T(8,128)(2,1)S(1)} %slice.29.refs_0_), channel_id=1, source_target_pairs={{0,4},{2,6},{4,0},{6,2},{1,5},{3,7},{5,1},{7,3},{8,12},{10,14},{12... | collective-permute-start | bytes 1179656 | tf_op jit(solution)/shard_map/ppermute | solution.py:35
  33.6 15.3 %collective-permute-start.6 = (bf16[256,768]{1,0:T(8,128)(2,1)S(1)}, bf16[256,768]{1,0:T(8,128)(2,1)S(1)}, u32[]{:S(2)}, u32[]{:S(2)}) collective-permute-start(bf16[256,768]{1,0:T(8,128)(2,1)S(1)} %slice.29.refs_0_), channel_id=1, source_target_pairs={{0,2},{2,4},{4,6},{6,0},{1,3},{3,5},{5,7},{7,1},{8,10},{10,12},{12... | collective-permute-start | bytes 1179656 | tf_op jit(solution)/shard_map/ppermute | solution.py:35
  34.0 18.2 %collective-permute-start.8 = (bf16[256,768]{1,0:T(8,128)(2,1)S(1)}, bf16[256,768]{1,0:T(8,128)(2,1)S(1)}, u32[]{:S(2)}, u32[]{:S(2)}) collective-permute-start(bf16[256,768]{1,0:T(8,128)(2,1)S(1)} %slice.29.refs_0_), channel_id=1, source_target_pairs={{0,6},{2,0},{4,2},{6,4},{1,7},{3,1},{5,3},{7,5},{8,14},{10,8},{12,... | collective-permute-start | bytes 1179656 | tf_op jit(solution)/shard_map/ppermute | solution.py:35
  36.3 17.1 %collective-permute-start.5 = (bf16[256,768]{1,0:T(8,128)(2,1)S(1)}, bf16[256,768]{1,0:T(8,128)(2,1)S(1)}, u32[]{:S(2)}, u32[]{:S(2)}) collective-permute-start(bf16[256,768]{1,0:T(8,128)(2,1)S(1)} %slice.29.refs_0_), channel_id=1, source_target_pairs={{0,1},{1,0},{2,3},{3,2},{4,5},{5,4},{6,7},{7,6},{8,9},{9,8},{10,11... | collective-permute-start | bytes 1179656 | tf_op jit(solution)/shard_map/ppermute | solution.py:31
  42.2 12.1 %copy-start.2 = (bf16[256,768]{1,0:T(8,128)(2,1)}, bf16[256,768]{1,0:T(8,128)(2,1)S(1)}, u32[]{:S(2)}) copy-start(bf16[256,768]{1,0:T(8,128)(2,1)S(1)} %collective-permute-done.10.refs_6_) | copy-start | bytes 1179652
  42.2 11.2 %collective-permute-start.11 = (bf16[256,768]{1,0:T(8,128)(2,1)S(1)}, bf16[256,768]{1,0:T(8,128)(2,1)S(1)}, u32[]{:S(2)}, u32[]{:S(2)}) collective-permute-start(bf16[256,768]{1,0:T(8,128)(2,1)S(1)} %collective-permute-done.10.refs_6_), channel_id=1, source_target_pairs={{0,1},{1,0},{2,3},{3,2},{4,5},{5,4},{6,7},{7,6},{8,9},{9,8},{10,11... | collective-permute-start | bytes 1179656 | tf_op jit(solution)/shard_map/ppermute | solution.py:31
  49.0 5.3 %copy-start.3 = (bf16[256,768]{1,0:T(8,128)(2,1)}, bf16[256,768]{1,0:T(8,128)(2,1)S(1)}, u32[]{:S(2)}) copy-start(bf16[256,768]{1,0:T(8,128)(2,1)S(1)} %collective-permute-done.6.refs_2_) | copy-start | bytes 1179652
  49.0 4.7 %collective-permute-start.7 = (bf16[256,768]{1,0:T(8,128)(2,1)S(1)}, bf16[256,768]{1,0:T(8,128)(2,1)}, u32[]{:S(2)}, u32[]{:S(2)}) collective-permute-start(bf16[256,768]{1,0:T(8,128)(2,1)S(1)} %collective-permute-done.6.refs_2_), channel_id=1, source_target_pairs={{0,1},{1,0},{2,3},{3,2},{4,5},{5,4},{6,7},{7,6},{8,9},{9,8},{10,11... | collective-permute-start | bytes 1179656 | tf_op jit(solution)/shard_map/ppermute | solution.py:31
  52.2 2.1 %copy-start.4 = (bf16[256,768]{1,0:T(8,128)(2,1)}, bf16[256,768]{1,0:T(8,128)(2,1)S(1)}, u32[]{:S(2)}) copy-start(bf16[256,768]{1,0:T(8,128)(2,1)S(1)} %collective-permute-done.8.refs_4_) | copy-start | bytes 1179652
  52.2 2.0 %collective-permute-start.9 = (bf16[256,768]{1,0:T(8,128)(2,1)S(1)}, bf16[256,768]{1,0:T(8,128)(2,1)}, u32[]{:S(2)}, u32[]{:S(2)}) collective-permute-start(bf16[256,768]{1,0:T(8,128)(2,1)S(1)} %collective-permute-done.8.refs_4_), channel_id=1, source_target_pairs={{0,1},{1,0},{2,3},{3,2},{4,5},{5,4},{6,7},{7,6},{8,9},{9,8},{10,11... | collective-permute-start | bytes 1179656 | tf_op jit(solution)/shard_map/ppermute | solution.py:31
  53.4 0.9 copy-start.5
  53.4 0.9 copy-start.6
  54.3 10.9 %copy-start.9 = (bf16[512,224]{0,1:T(8,128)(2,1)S(1)}, bf16[512,224]{0,1:T(8,128)(2,1)}, u32[]{:S(2)}) copy-start(bf16[512,224]{0,1:T(8,128)(2,1)} %param.20) | copy-start | bytes 688132
  54.3 11.4 %copy-start.10 = (bf16[512,224]{0,1:T(8,128)(2,1)S(1)}, bf16[512,224]{0,1:T(8,128)(2,1)}, u32[]{:S(2)}) copy-start(bf16[512,224]{0,1:T(8,128)(2,1)} %param.19) | copy-start | bytes 688132
  64.7 7.4 %copy-start.8 = (bf16[32,48,128]{2,1,0:T(8,128)(2,1)S(1)}, bf16[32,48,128]{2,1,0:T(8,128)(2,1)}, u32[]{:S(2)}) copy-start(bf16[32,48,128]{2,1,0:T(8,128)(2,1)} %get-tuple-element.34) | copy-start | bytes 1179652
  64.7 24.2 %copy-start.7 = (bf16[32,48,128]{2,1,0:T(8,128)(2,1)S(1)}, bf16[32,48,128]{2,1,0:T(8,128)(2,1)}, u32[]{:S(2)}) copy-start(bf16[32,48,128]{2,1,0:T(8,128)(2,1)} %get-tuple-element.28) | copy-start | bytes 1179652
  64.7 2.0 %collective-permute-start.13 = (bf16[32,48,128]{2,1,0:T(8,128)(2,1)}, bf16[32,48,128]{2,1,0:T(8,128)(2,1)S(1)}, u32[]{:S(2)}, u32[]{:S(2)}) collective-permute-start(bf16[32,48,128]{2,1,0:T(8,128)(2,1)} %get-tuple-element.31), channel_id=1, source_target_pairs={{0,1},{1,0},{2,3},{3,2},{4,5},{5,4},{6,7},{7,6},{8,9},{9,8},{10,11... | collective-permute-start | bytes 1179656 | tf_op jit(solution)/shard_map/ppermute | solution.py:31
  65.4 4.6 %collective-permute-start.15 = (bf16[32,48,128]{2,1,0:T(8,128)(2,1)}, bf16[32,48,128]{2,1,0:T(8,128)(2,1)S(1)}, u32[]{:S(2)}, u32[]{:S(2)}) collective-permute-start(bf16[32,48,128]{2,1,0:T(8,128)(2,1)} %get-tuple-element.33), channel_id=1, source_target_pairs={{0,1},{1,0},{2,3},{3,2},{4,5},{5,4},{6,7},{7,6},{8,9},{9,8},{10,11... | collective-permute-start | bytes 1179656 | tf_op jit(solution)/shard_map/ppermute | solution.py:31
  65.9 6.1 %collective-permute-start.17 = (bf16[32,48,128]{2,1,0:T(8,128)(2,1)}, bf16[32,48,128]{2,1,0:T(8,128)(2,1)S(1)}, u32[]{:S(2)}, u32[]{:S(2)}) collective-permute-start(bf16[32,48,128]{2,1,0:T(8,128)(2,1)} %get-tuple-element.35), channel_id=1, source_target_pairs={{0,1},{1,0},{2,3},{3,2},{4,5},{5,4},{6,7},{7,6},{8,9},{9,8},{10,11... | collective-permute-start | bytes 1179656 | tf_op jit(solution)/shard_map/ppermute | solution.py:31
  66.4 10.4 %collective-permute-start.12 = (bf16[32,48,128]{2,1,0:T(8,128)(2,1)}, bf16[32,48,128]{2,1,0:T(8,128)(2,1)S(1)}, u32[]{:S(2)}, u32[]{:S(2)}) collective-permute-start(bf16[32,48,128]{2,1,0:T(8,128)(2,1)} %get-tuple-element.29), channel_id=1, source_target_pairs={{0,1},{1,0},{2,3},{3,2},{4,5},{5,4},{6,7},{7,6},{8,9},{9,8},{10,11... | collective-permute-start | bytes 1179656 | tf_op jit(solution)/shard_map/ppermute | solution.py:31
  67.8 12.0 %collective-permute-start.14 = (bf16[32,48,128]{2,1,0:T(8,128)(2,1)S(1)}, bf16[32,48,128]{2,1,0:T(8,128)(2,1)S(1)}, u32[]{:S(2)}, u32[]{:S(2)}) collective-permute-start(bf16[32,48,128]{2,1,0:T(8,128)(2,1)S(1)} %add_convert_fusion.3), channel_id=1, source_target_pairs={{0,4},{2,6},{4,0},{6,2},{1,5},{3,7},{5,1},{7,3},{8,12},{10,14},{12... | collective-permute-start | bytes 1179656 | tf_op jit(solution)/shard_map/ppermute | solution.py:35
  71.2 17.7 %collective-permute-start.16 = (bf16[32,48,128]{2,1,0:T(8,128)(2,1)S(1)}, bf16[32,48,128]{2,1,0:T(8,128)(2,1)S(1)}, u32[]{:S(2)}, u32[]{:S(2)}) collective-permute-start(bf16[32,48,128]{2,1,0:T(8,128)(2,1)S(1)} %add_convert_fusion.2), channel_id=1, source_target_pairs={{0,2},{2,4},{4,6},{6,0},{1,3},{3,5},{5,7},{7,1},{8,10},{10,12},{12... | collective-permute-start | bytes 1179656 | tf_op jit(solution)/shard_map/ppermute | solution.py:35
  72.2 16.7 %collective-permute-start.18 = (bf16[32,48,128]{2,1,0:T(8,128)(2,1)S(1)}, bf16[32,48,128]{2,1,0:T(8,128)(2,1)S(1)}, u32[]{:S(2)}, u32[]{:S(2)}) collective-permute-start(bf16[32,48,128]{2,1,0:T(8,128)(2,1)S(1)} %add_convert_fusion.1), channel_id=1, source_target_pairs={{0,6},{2,0},{4,2},{6,4},{1,7},{3,1},{5,3},{7,5},{8,14},{10,8},{12,... | collective-permute-start | bytes 1179656 | tf_op jit(solution)/shard_map/ppermute | solution.py:35
  74.3 2.3 %collective-permute-start = (bf16[128,448]{1,0:T(8,128)(2,1)S(1)}, bf16[128,448]{1,0:T(8,128)(2,1)S(1)}, u32[]{:S(2)}, u32[]{:S(2)}) collective-permute-start(bf16[128,448]{1,0:T(8,128)(2,1)S(1)} %select_convert_fusion), channel_id=1, source_target_pairs={{0,1},{1,0},{2,3},{3,2},{4,5},{5,4},{6,7},{7,6},{8,9},{9,8},{10,11... | collective-permute-start | bytes 344072 | tf_op jit(solution)/shard_map/ppermute | solution.py:31
  76.7 21.6 %collective-permute-start.1 = (bf16[128,448]{1,0:T(8,128)(2,1)S(1)}, bf16[128,448]{1,0:T(8,128)(2,1)S(1)}, u32[]{:S(2)}, u32[]{:S(2)}) collective-permute-start(bf16[128,448]{1,0:T(8,128)(2,1)S(1)} %add_convert_fusion.6), channel_id=1, source_target_pairs={{0,2},{2,4},{4,6},{6,0},{1,3},{3,5},{5,7},{7,1},{8,10},{10,12},{12... | collective-permute-start | bytes 344072 | tf_op jit(solution)/shard_map/ppermute | solution.py:35
  76.8 21.6 %collective-permute-start.2 = (bf16[128,448]{1,0:T(8,128)(2,1)S(1)}, bf16[128,448]{1,0:T(8,128)(2,1)S(1)}, u32[]{:S(2)}, u32[]{:S(2)}) collective-permute-start(bf16[128,448]{1,0:T(8,128)(2,1)S(1)} %add_convert_fusion.6), channel_id=1, source_target_pairs={{0,4},{2,6},{4,0},{6,2},{1,5},{3,7},{5,1},{7,3},{8,12},{10,14},{12... | collective-permute-start | bytes 344072 | tf_op jit(solution)/shard_map/ppermute | solution.py:35
  79.8 18.6 %collective-permute-start.3 = (bf16[128,448]{1,0:T(8,128)(2,1)S(1)}, bf16[128,448]{1,0:T(8,128)(2,1)S(1)}, u32[]{:S(2)}, u32[]{:S(2)}) collective-permute-start(bf16[128,448]{1,0:T(8,128)(2,1)S(1)} %add_convert_fusion.6), channel_id=1, source_target_pairs={{0,6},{2,0},{4,2},{6,4},{1,7},{3,1},{5,3},{7,5},{8,14},{10,8},{12,... | collective-permute-start | bytes 344072 | tf_op jit(solution)/shard_map/ppermute | solution.py:35
  89.9 19.1 %all-to-all-start.1 = ((bf16[32,48,128]{2,1,0:T(8,128)(2,1)}), bf16[32,48,128]{2,1,0:T(8,128)(2,1)S(1)}, u32[]{:S(2)}, u32[]{:S(2)}) async-start(bf16[32,48,128]{2,1,0:T(8,128)(2,1)} %add_convert_fusion), calls=%async_computation.1 | async-start | bytes 786432 | tf_op jit(solution)/shard_map/all_to_all | solution.py:23
  98.5 39.3 %copy-start.11 = (bf16[8,512]{1,0:T(8,128)(2,1)S(1)}, bf16[8,512]{1,0:T(8,128)(2,1)}, u32[]{:S(2)}) copy-start(bf16[8,512]{1,0:T(8,128)(2,1)} %student.1) | copy-start | bytes 24580
  98.5 2.6 %collective-permute-start.4 = (bf16[128,448]{1,0:T(8,128)(2,1)S(1)}, bf16[128,448]{1,0:T(8,128)(2,1)S(1)}, u32[]{:S(2)}, u32[]{:S(2)}) collective-permute-start(bf16[128,448]{1,0:T(8,128)(2,1)S(1)} %add_convert_fusion.5), channel_id=1, source_target_pairs={{0,1},{1,0},{2,3},{3,2},{4,5},{5,4},{6,7},{7,6},{8,9},{9,8},{10,11... | collective-permute-start | bytes 344072 | tf_op jit(solution)/shard_map/ppermute | solution.py:31
  109.1 5.5 %collective-permute-start.19 = (bf16[48,128]{1,0:T(8,128)(2,1)S(1)}, bf16[48,128]{1,0:T(8,128)(2,1)S(1)}, u32[]{:S(2)}, u32[]{:S(2)}) collective-permute-start(bf16[48,128]{1,0:T(8,128)(2,1)S(1)} %reduce_sum.21), channel_id=1, source_target_pairs={{0,2},{2,4},{4,6},{6,0},{1,3},{3,5},{5,7},{7,1},{8,10},{10,12},{12... | collective-permute-start | bytes 36872 | tf_op jit(solution)/shard_map/ppermute | solution.py:35
  112.0 4.0 %collective-permute-start.20 = (bf16[48,128]{1,0:T(8,128)(2,1)S(1)}, bf16[48,128]{1,0:T(8,128)(2,1)S(1)}, u32[]{:S(2)}, u32[]{:S(2)}) collective-permute-start(bf16[48,128]{1,0:T(8,128)(2,1)S(1)} %reduce_sum.21), channel_id=1, source_target_pairs={{0,4},{2,6},{4,0},{6,2},{1,5},{3,7},{5,1},{7,3},{8,12},{10,14},{12... | collective-permute-start | bytes 36872 | tf_op jit(solution)/shard_map/ppermute | solution.py:35
  113.9 2.5 %collective-permute-start.21 = (bf16[48,128]{1,0:T(8,128)(2,1)S(1)}, bf16[48,128]{1,0:T(8,128)(2,1)S(1)}, u32[]{:S(2)}, u32[]{:S(2)}) collective-permute-start(bf16[48,128]{1,0:T(8,128)(2,1)S(1)} %reduce_sum.21), channel_id=1, source_target_pairs={{0,6},{2,0},{4,2},{6,4},{1,7},{3,1},{5,3},{7,5},{8,14},{10,8},{12,... | collective-permute-start | bytes 36872 | tf_op jit(solution)/shard_map/ppermute | solution.py:35
  116.4 6.7 %collective-permute-start.22 = (bf16[192,128]{1,0:T(8,128)(2,1)S(1)}, bf16[192,128]{1,0:T(8,128)(2,1)S(1)}, u32[]{:S(2)}, u32[]{:S(2)}) collective-permute-start(bf16[192,128]{1,0:T(8,128)(2,1)S(1)} %pad_maximum_fusion.1), channel_id=1, source_target_pairs={{0,1},{1,0},{2,3},{3,2},{4,5},{5,4},{6,7},{7,6},{8,9},{9,8},{10,11... | collective-permute-start | bytes 147464 | tf_op jit(solution)/shard_map/ppermute | solution.py:31
  154.9 4.6 %collective-permute-start.23 = (bf16[128,224]{1,0:T(8,128)(2,1)S(1)}, bf16[128,224]{1,0:T(8,128)(2,1)S(1)}, u32[]{:S(2)}, u32[]{:S(2)}) collective-permute-start(bf16[128,224]{1,0:T(8,128)(2,1)S(1)} %select_convert_fusion.1), channel_id=1, source_target_pairs={{0,1},{1,0},{2,3},{3,2},{4,5},{5,4},{6,7},{7,6},{8,9},{9,8},{10,11... | collective-permute-start | bytes 172040 | tf_op jit(solution)/shard_map/ppermute | solution.py:31
  159.5 4.4 %collective-permute-start.24 = (bf16[128,224]{1,0:T(8,128)(2,1)S(1)}, bf16[128,224]{1,0:T(8,128)(2,1)S(1)}, u32[]{:S(2)}, u32[]{:S(2)}) collective-permute-start(bf16[128,224]{1,0:T(8,128)(2,1)S(1)} %add_convert_fusion.8), channel_id=1, source_target_pairs={{0,2},{2,4},{4,6},{6,0},{1,3},{3,5},{5,7},{7,1},{8,10},{10,12},{12... | collective-permute-start | bytes 172040 | tf_op jit(solution)/shard_map/ppermute | solution.py:35
  159.6 5.6 %collective-permute-start.25 = (bf16[128,224]{1,0:T(8,128)(2,1)S(1)}, bf16[128,224]{1,0:T(8,128)(2,1)S(1)}, u32[]{:S(2)}, u32[]{:S(2)}) collective-permute-start(bf16[128,224]{1,0:T(8,128)(2,1)S(1)} %add_convert_fusion.8), channel_id=1, source_target_pairs={{0,4},{2,6},{4,0},{6,2},{1,5},{3,7},{5,1},{7,3},{8,12},{10,14},{12... | collective-permute-start | bytes 172040 | tf_op jit(solution)/shard_map/ppermute | solution.py:35
  162.3 3.9 %collective-permute-start.26 = (bf16[128,224]{1,0:T(8,128)(2,1)S(1)}, bf16[128,224]{1,0:T(8,128)(2,1)S(1)}, u32[]{:S(2)}, u32[]{:S(2)}) collective-permute-start(bf16[128,224]{1,0:T(8,128)(2,1)S(1)} %add_convert_fusion.8), channel_id=1, source_target_pairs={{0,6},{2,0},{4,2},{6,4},{1,7},{3,1},{5,3},{7,5},{8,14},{10,8},{12,... | collective-permute-start | bytes 172040 | tf_op jit(solution)/shard_map/ppermute | solution.py:35
  166.2 2.3 %collective-permute-start.27 = (bf16[128,224]{1,0:T(8,128)(2,1)S(1)}, bf16[128,224]{1,0:T(8,128)(2,1)S(1)}, u32[]{:S(2)}, u32[]{:S(2)}) collective-permute-start(bf16[128,224]{1,0:T(8,128)(2,1)S(1)} %add_convert_fusion.7.own), channel_id=1, source_target_pairs={{0,1},{1,0},{2,3},{3,2},{4,5},{5,4},{6,7},{7,6},{8,9},{9,8},{10,11... | collective-permute-start | bytes 172040 | tf_op jit(solution)/shard_map/ppermute | solution.py:31

commit v6 on v5

--- a/solution.py
+++ b/solution.py
@@ -16,7 +16,7 @@
 BF = jnp.bfloat16
 F32 = jnp.float32
 VMEM_BYTES = 60 * 1024 * 1024
-STEPS = 4
+STEPS = 8
 
 
 def exchange(values, axes):

time: 170 us -> 172 us (1.012)
  no operation moved by 1% of the time
where the time goes in v6:
time: 172 us; the launch traced here: 171 us
  starting transfers between devices  74.8 us (43%)
  waiting for transfers between devices  36.8 us (21%)
  blocking collectives  30.4 us (18%)
  Pallas kernels  14.4 us (8%)
  local copies, waits for them, and re-layouts  6.73 us (4%)
  other arithmetic  4.72 us (3%)
  matrix products  2.14 us (1%)
    ppermute x13, starting transfers between devices, swap_cores(): return lax.ppermute(values, 'c', [(0, 1), (1, 0)])  30.5 us
    all_to_all x2, blocking collectives, exchange(): return lax.all_to_all(values, axes, 0, 0, tiled=False)  30.4 us
    ppermute x15, starting transfers between devices, along_y(): return lax.ppermute(values, 'y', [(i, (i + shift) % NY) for i in range(NY)])  24 us
    all_to_all x2, starting transfers between devices, exchange(): return lax.all_to_all(values, axes, 0, 0, tiled=False)  20.3 us
    all_to_all x2, waiting for transfers between devices, exchange(): return lax.all_to_all(values, axes, 0, 0, tiled=False)  19.6 us
    ppermute x15, waiting for transfers between devices, along_y(): return lax.ppermute(values, 'y', [(i, (i + shift) % NY) for i in range(NY)])  12.9 us
    pallas_call x1, Pallas kernels, expert_products(): pl.pallas_call(expert_kernel, out_shape=(out,) * 8, in_specs=[IN_ANY] * 8...  11.6 us
    unnamed x28, local copies, waits for them, and re-layouts  5.54 us
  transfers between devices with their start and end apart: 30, of which 16 were waited for; matrix products, arithmetic and copies ran while one was open for 7% of the time, Pallas kernels for 0%

profile of v6, /device:TPU:1, one launch (start us, length us, event | category | flops | bytes accessed | tf_op | source)
XLA Modules:
  0.0 171.0 jit_solution(1368500911550102937)
XLA Ops:
  0.6 1.7 shard_map.138
  2.3 11.9 %all-to-all-start = ((bf16[32,8,1280]{2,1,0:T(8,128)(2,1)}), bf16[32,8,1280]{2,1,0:T(8,128)(2,1)S(1)}, u32[]{:S(2)}, u32[]{:S(2)}) async-start(bf16[32,8,1280]{2,1,0:T(8,128)(2,1)} %shard_map.138), calls=%async_computation | async-start | bytes 1310720 | tf_op jit(solution)/shard_map/all_to_all | solution.py:23
  14.2 4.7 %copy.15 = bf16[1,256,6144]{1,2,0:T(8,128)(2,1)} copy(bf16[1,256,6144]{2,1,0:T(8,128)(2,1)} %param.16) | data formatting | bytes 6291456 | tf_op args[5]
  18.9 11.7 %all-to-all-done = bf16[32,8,1280]{2,1,0:T(8,128)(2,1)S(1)} async-done(((bf16[32,8,1280]{2,1,0:T(8,128)(2,1)}), bf16[32,8,1280]{2,1,0:T(8,128)(2,1)S(1)}, u32[]{:S(2)}, u32[]{:S(2)}) %all-to-all-start) | async-done | bytes 655392 | tf_op jit(solution)/shard_map/all_to_all | solution.py:23
  30.6 3.0 %collective-permute-start.10 = (bf16[256,768]{1,0:T(8,128)(2,1)S(1)}, bf16[256,768]{1,0:T(8,128)(2,1)S(1)}, u32[]{:S(2)}, u32[]{:S(2)}) collective-permute-start(bf16[256,768]{1,0:T(8,128)(2,1)S(1)} %slice.29.refs_0_), channel_id=1, source_target_pairs={{0,4},{2,6},{4,0},{6,2},{1,5},{3,7},{5,1},{7,3},{8,12},{10,14},{12... | collective-permute-start | bytes 1179656 | tf_op jit(solution)/shard_map/ppermute | solution.py:35
  33.6 0.4 collective-permute-start.6
  34.0 2.3 %collective-permute-start.8 = (bf16[256,768]{1,0:T(8,128)(2,1)S(1)}, bf16[256,768]{1,0:T(8,128)(2,1)S(1)}, u32[]{:S(2)}, u32[]{:S(2)}) collective-permute-start(bf16[256,768]{1,0:T(8,128)(2,1)S(1)} %slice.29.refs_0_), channel_id=1, source_target_pairs={{0,6},{2,0},{4,2},{6,4},{1,7},{3,1},{5,3},{7,5},{8,14},{10,8},{12,... | collective-permute-start | bytes 1179656 | tf_op jit(solution)/shard_map/ppermute | solution.py:35
  36.3 5.9 %collective-permute-start.5 = (bf16[256,768]{1,0:T(8,128)(2,1)S(1)}, bf16[256,768]{1,0:T(8,128)(2,1)S(1)}, u32[]{:S(2)}, u32[]{:S(2)}) collective-permute-start(bf16[256,768]{1,0:T(8,128)(2,1)S(1)} %slice.29.refs_0_), channel_id=1, source_target_pairs={{0,1},{1,0},{2,3},{3,2},{4,5},{5,4},{6,7},{7,6},{8,9},{9,8},{10,11... | collective-permute-start | bytes 1179656 | tf_op jit(solution)/shard_map/ppermute | solution.py:31
  42.2 5.9 %collective-permute-start.11 = (bf16[256,768]{1,0:T(8,128)(2,1)S(1)}, bf16[256,768]{1,0:T(8,128)(2,1)S(1)}, u32[]{:S(2)}, u32[]{:S(2)}) collective-permute-start(bf16[256,768]{1,0:T(8,128)(2,1)S(1)} %collective-permute-done.10.refs_6_), channel_id=1, source_target_pairs={{0,1},{1,0},{2,3},{3,2},{4,5},{5,4},{6,7},{7,6},{8,9},{9,8},{10,11... | collective-permute-start | bytes 1179656 | tf_op jit(solution)/shard_map/ppermute | solution.py:31
  48.1 0.9 collective-permute-done.6.refs_2_
  49.0 3.2 %collective-permute-start.7 = (bf16[256,768]{1,0:T(8,128)(2,1)S(1)}, bf16[256,768]{1,0:T(8,128)(2,1)}, u32[]{:S(2)}, u32[]{:S(2)}) collective-permute-start(bf16[256,768]{1,0:T(8,128)(2,1)S(1)} %collective-permute-done.6.refs_2_), channel_id=1, source_target_pairs={{0,1},{1,0},{2,3},{3,2},{4,5},{5,4},{6,7},{7,6},{8,9},{9,8},{10,11... | collective-permute-start | bytes 1179656 | tf_op jit(solution)/shard_map/ppermute | solution.py:31
  52.2 0.4 collective-permute-start.9
  52.6 0.8 copy.18.refs_11_
  53.4 0.3 collective-permute-done.7.refs_3_
  53.7 0.6 collective-permute-done.9.refs_5_
  54.3 11.6 %shard_map.139 = (bf16[32,48,128]{2,1,0:T(8,128)(2,1)}, bf16[32,48,128]{2,1,0:T(8,128)(2,1)}, bf16[32,48,128]{2,1,0:T(8,128)(2,1)}, bf16[32,48,128]{2,1,0:T(8,12...) custom-call(bf16[256,768]{1,0:T(8,128)(2,1)} %copy-done.1, ...), custom_call_target="tpu_custom_call" | custom-call | flops 2415919104 | bytes 15728640 | tf_op jit(solution)/shard_map/pallas_call | solution.py:219
  65.9 0.5 collective-permute-start.13
  66.3 0.2 fusion.17
  66.6 0.2 collective-permute-start.15
  66.8 0.3 fusion.19
  67.1 0.5 collective-permute-start.17
  67.5 0.3 collective-permute-start.12
  67.9 1.1 add_convert_fusion.3
  69.0 2.2 %collective-permute-start.14 = (bf16[32,48,128]{2,1,0:T(8,128)(2,1)S(1)}, bf16[32,48,128]{2,1,0:T(8,128)(2,1)S(1)}, u32[]{:S(2)}, u32[]{:S(2)}) collective-permute-start(bf16[32,48,128]{2,1,0:T(8,128)(2,1)S(1)} %add_convert_fusion.3), channel_id=1, source_target_pairs={{0,4},{2,6},{4,0},{6,2},{1,5},{3,7},{5,1},{7,3},{8,12},{10,14},{12... | collective-permute-start | bytes 1179656 | tf_op jit(solution)/shard_map/ppermute | solution.py:35
  71.2 1.1 add_convert_fusion.2
  72.3 0.9 collective-permute-start.16
  73.3 2.0 %collective-permute-start.18 = (bf16[32,48,128]{2,1,0:T(8,128)(2,1)S(1)}, bf16[32,48,128]{2,1,0:T(8,128)(2,1)S(1)}, u32[]{:S(2)}, u32[]{:S(2)}) collective-permute-start(bf16[32,48,128]{2,1,0:T(8,128)(2,1)S(1)} %add_convert_fusion.1), channel_id=1, source_target_pairs={{0,6},{2,0},{4,2},{6,4},{1,7},{3,1},{5,3},{7,5},{8,14},{10,8},{12,... | collective-permute-start | bytes 1179656 | tf_op jit(solution)/shard_map/ppermute | solution.py:35
  75.4 1.3 collective-permute-start
  76.7 1.0 collective-permute-done
  77.7 0.2 add_convert_fusion.6
  78.0 1.7 %collective-permute-start.2 = (bf16[128,448]{1,0:T(8,128)(2,1)S(1)}, bf16[128,448]{1,0:T(8,128)(2,1)S(1)}, u32[]{:S(2)}, u32[]{:S(2)}) collective-permute-start(bf16[128,448]{1,0:T(8,128)(2,1)S(1)} %add_convert_fusion.6), channel_id=1, source_target_pairs={{0,4},{2,6},{4,0},{6,2},{1,5},{3,7},{5,1},{7,3},{8,12},{10,14},{12... | collective-permute-start | bytes 344072 | tf_op jit(solution)/shard_map/ppermute | solution.py:35
  79.7 1.3 collective-permute-done.14
  81.0 2.5 %collective-permute-start.3 = (bf16[128,448]{1,0:T(8,128)(2,1)S(1)}, bf16[128,448]{1,0:T(8,128)(2,1)S(1)}, u32[]{:S(2)}, u32[]{:S(2)}) collective-permute-start(bf16[128,448]{1,0:T(8,128)(2,1)S(1)} %add_convert_fusion.6), channel_id=1, source_target_pairs={{0,6},{2,0},{4,2},{6,4},{1,7},{3,1},{5,3},{7,5},{8,14},{10,8},{12,... | collective-permute-start | bytes 344072 | tf_op jit(solution)/shard_map/ppermute | solution.py:35
  83.5 6.6 %collective-permute-done.16 = bf16[32,48,128]{2,1,0:T(8,128)(2,1)S(1)} collective-permute-done((bf16[32,48,128]{2,1,0:T(8,128)(2,1)S(1)}, bf16[32,48,128]{2,1,0:T(8,128)(2,1)S(1)}, u32[]{:S(2)}, u32[]{:S(2)}) %collective-permute-start.16) | collective-permute-done | bytes 393248 | tf_op jit(solution)/shard_map/ppermute | solution.py:35
  90.1 1.0 add_convert_fusion
  91.1 8.4 %all-to-all-start.1 = ((bf16[32,48,128]{2,1,0:T(8,128)(2,1)}), bf16[32,48,128]{2,1,0:T(8,128)(2,1)S(1)}, u32[]{:S(2)}, u32[]{:S(2)}) async-start(bf16[32,48,128]{2,1,0:T(8,128)(2,1)} %add_convert_fusion), calls=%async_computation.1 | async-start | bytes 786432 | tf_op jit(solution)/shard_map/all_to_all | solution.py:23
  99.6 1.5 collective-permute-start.4
  101.1 1.1 fusion.21
  102.4 7.9 %all-to-all-done.1 = bf16[32,48,128]{2,1,0:T(8,128)(2,1)S(1)} async-done(((bf16[32,48,128]{2,1,0:T(8,128)(2,1)}), bf16[32,48,128]{2,1,0:T(8,128)(2,1)S(1)}, u32[]{:S(2)}, u32[]{:S(2)}) %all-to-all-start.1) | async-done | bytes 393248 | tf_op jit(solution)/shard_map/all_to_all | solution.py:23
  110.3 2.8 %collective-permute-start.19 = (bf16[48,128]{1,0:T(8,128)(2,1)S(1)}, bf16[48,128]{1,0:T(8,128)(2,1)S(1)}, u32[]{:S(2)}, u32[]{:S(2)}) collective-permute-start(bf16[48,128]{1,0:T(8,128)(2,1)S(1)} %reduce_sum.21), channel_id=1, source_target_pairs={{0,2},{2,4},{4,6},{6,0},{1,3},{3,5},{5,7},{7,1},{8,10},{10,12},{12... | collective-permute-start | bytes 36872 | tf_op jit(solution)/shard_map/ppermute | solution.py:35
  113.1 1.9 %collective-permute-start.20 = (bf16[48,128]{1,0:T(8,128)(2,1)S(1)}, bf16[48,128]{1,0:T(8,128)(2,1)S(1)}, u32[]{:S(2)}, u32[]{:S(2)}) collective-permute-start(bf16[48,128]{1,0:T(8,128)(2,1)S(1)} %reduce_sum.21), channel_id=1, source_target_pairs={{0,4},{2,6},{4,0},{6,2},{1,5},{3,7},{5,1},{7,3},{8,12},{10,14},{12... | collective-permute-start | bytes 36872 | tf_op jit(solution)/shard_map/ppermute | solution.py:35
  115.0 0.6 collective-permute-start.21
  115.6 0.1 fusion.22
  115.8 1.4 collective-permute-done.20
  117.2 0.4 collective-permute-done.21
  117.6 5.9 %collective-permute-start.22 = (bf16[192,128]{1,0:T(8,128)(2,1)S(1)}, bf16[192,128]{1,0:T(8,128)(2,1)S(1)}, u32[]{:S(2)}, u32[]{:S(2)}) collective-permute-start(bf16[192,128]{1,0:T(8,128)(2,1)S(1)} %pad_maximum_fusion.1), channel_id=1, source_target_pairs={{0,1},{1,0},{2,3},{3,2},{4,5},{5,4},{6,7},{7,6},{8,9},{9,8},{10,11... | collective-permute-start | bytes 147464 | tf_op jit(solution)/shard_map/ppermute | solution.py:31
  123.5 0.2 fusion.23
  123.7 0.7 collective-permute-done.22
  124.4 0.2 fusion.1
  124.6 14.3 %all_to_all.20 = bf16[32,8,512]{2,1,0:T(8,128)(2,1)S(1)} all-to-all(bf16[32,8,512]{2,1,0:T(8,128)(2,1)S(1)} %fusion.1), channel_id=1, replica_groups=mesh['x'=4,'z'=8,'y'=4,'c'=2] {'x','z'}, dimensions={0} | all-to-all | bytes 524288 | tf_op jit(solution)/shard_map/all_to_all | solution.py:23
  139.0 0.6 multiply_convert_fusion.1
  139.6 16.2 %all_to_all.21 = bf16[32,8,512]{2,1,0:T(8,128)(2,1)S(1)} all-to-all(bf16[32,8,512]{2,1,0:T(8,128)(2,1)S(1)} %broadcast_in_dim.2), channel_id=1, replica_groups=mesh['x'=4,'z'=8,'y'=4,'c'=2] {'x','z'}, dimensions={0} | all-to-all | bytes 524288 | tf_op jit(solution)/shard_map/all_to_all | solution.py:23
  155.8 0.2 fusion.4
  156.0 3.7 %collective-permute-start.23 = (bf16[128,224]{1,0:T(8,128)(2,1)S(1)}, bf16[128,224]{1,0:T(8,128)(2,1)S(1)}, u32[]{:S(2)}, u32[]{:S(2)}) collective-permute-start(bf16[128,224]{1,0:T(8,128)(2,1)S(1)} %select_convert_fusion.1), channel_id=1, source_target_pairs={{0,1},{1,0},{2,3},{3,2},{4,5},{5,4},{6,7},{7,6},{8,9},{9,8},{10,11... | collective-permute-start | bytes 172040 | tf_op jit(solution)/shard_map/ppermute | solution.py:31
  159.7 0.9 collective-permute-done.23
  160.7 0.3 collective-permute-start.24
  161.0 2.7 %collective-permute-start.25 = (bf16[128,224]{1,0:T(8,128)(2,1)S(1)}, bf16[128,224]{1,0:T(8,128)(2,1)S(1)}, u32[]{:S(2)}, u32[]{:S(2)}) collective-permute-start(bf16[128,224]{1,0:T(8,128)(2,1)S(1)} %add_convert_fusion.8), channel_id=1, source_target_pairs={{0,4},{2,6},{4,0},{6,2},{1,5},{3,7},{5,1},{7,3},{8,12},{10,14},{12... | collective-permute-start | bytes 172040 | tf_op jit(solution)/shard_map/ppermute | solution.py:35
  163.6 0.7 collective-permute-start.26
  164.3 0.9 convolution_convert_fusion
  165.3 1.3 collective-permute-done.25
  166.6 1.0 collective-permute-done.26
  167.6 1.4 collective-permute-start.27
  169.0 0.9 collective-permute-done.27.other
  169.9 1.1 shard_map.140
  (57 shorter events, 0.9 us)
Async XLA Ops:
  0.6 122.8 %copy-start = (bf16[224,512]{1,0:T(8,128)(2,1)S(1)}, bf16[224,512]{1,0:T(8,128)(2,1)}, u32[]{:S(2)}) copy-start(bf16[224,512]{1,0:T(8,128)(2,1)} %param.21) | copy-start | bytes 688132
  2.3 28.3 %all-to-all-start = ((bf16[32,8,1280]{2,1,0:T(8,128)(2,1)}), bf16[32,8,1280]{2,1,0:T(8,128)(2,1)S(1)}, u32[]{:S(2)}, u32[]{:S(2)}) async-start(bf16[32,8,1280]{2,1,0:T(8,128)(2,1)} %shard_map.138), calls=%async_computation | async-start | bytes 1310720 | tf_op jit(solution)/shard_map/all_to_all | solution.py:23
  14.2 38.4 %copy-start.12 = (s32[256,2]{0,1:T(2,128)S(1)}, s32[256,2]{0,1:T(2,128)}, u32[]{:S(2)}) copy-start(s32[256,2]{0,1:T(2,128)} %param.12) | copy-start | bytes 6148
  30.6 23.6 %copy-start.1 = (bf16[256,768]{1,0:T(8,128)(2,1)}, bf16[256,768]{1,0:T(8,128)(2,1)S(1)}, u32[]{:S(2)}) copy-start(bf16[256,768]{1,0:T(8,128)(2,1)S(1)} %slice.29.refs_0_) | copy-start | bytes 1179652
  30.6 11.5 %collective-permute-start.10 = (bf16[256,768]{1,0:T(8,128)(2,1)S(1)}, bf16[256,768]{1,0:T(8,128)(2,1)S(1)}, u32[]{:S(2)}, u32[]{:S(2)}) collective-permute-start(bf16[256,768]{1,0:T(8,128)(2,1)S(1)} %slice.29.refs_0_), channel_id=1, source_target_pairs={{0,4},{2,6},{4,0},{6,2},{1,5},{3,7},{5,1},{7,3},{8,12},{10,14},{12... | collective-permute-start | bytes 1179656 | tf_op jit(solution)/shard_map/ppermute | solution.py:35
  33.6 15.3 %collective-permute-start.6 = (bf16[256,768]{1,0:T(8,128)(2,1)S(1)}, bf16[256,768]{1,0:T(8,128)(2,1)S(1)}, u32[]{:S(2)}, u32[]{:S(2)}) collective-permute-start(bf16[256,768]{1,0:T(8,128)(2,1)S(1)} %slice.29.refs_0_), channel_id=1, source_target_pairs={{0,2},{2,4},{4,6},{6,0},{1,3},{3,5},{5,7},{7,1},{8,10},{10,12},{12... | collective-permute-start | bytes 1179656 | tf_op jit(solution)/shard_map/ppermute | solution.py:35
  34.0 18.2 %collective-permute-start.8 = (bf16[256,768]{1,0:T(8,128)(2,1)S(1)}, bf16[256,768]{1,0:T(8,128)(2,1)S(1)}, u32[]{:S(2)}, u32[]{:S(2)}) collective-permute-start(bf16[256,768]{1,0:T(8,128)(2,1)S(1)} %slice.29.refs_0_), channel_id=1, source_target_pairs={{0,6},{2,0},{4,2},{6,4},{1,7},{3,1},{5,3},{7,5},{8,14},{10,8},{12,... | collective-permute-start | bytes 1179656 | tf_op jit(solution)/shard_map/ppermute | solution.py:35
  36.3 17.1 %collective-permute-start.5 = (bf16[256,768]{1,0:T(8,128)(2,1)S(1)}, bf16[256,768]{1,0:T(8,128)(2,1)S(1)}, u32[]{:S(2)}, u32[]{:S(2)}) collective-permute-start(bf16[256,768]{1,0:T(8,128)(2,1)S(1)} %slice.29.refs_0_), channel_id=1, source_target_pairs={{0,1},{1,0},{2,3},{3,2},{4,5},{5,4},{6,7},{7,6},{8,9},{9,8},{10,11... | collective-permute-start | bytes 1179656 | tf_op jit(solution)/shard_map/ppermute | solution.py:31
  42.2 12.1 %copy-start.2 = (bf16[256,768]{1,0:T(8,128)(2,1)}, bf16[256,768]{1,0:T(8,128)(2,1)S(1)}, u32[]{:S(2)}) copy-start(bf16[256,768]{1,0:T(8,128)(2,1)S(1)} %collective-permute-done.10.refs_6_) | copy-start | bytes 1179652
  42.2 11.2 %collective-permute-start.11 = (bf16[256,768]{1,0:T(8,128)(2,1)S(1)}, bf16[256,768]{1,0:T(8,128)(2,1)S(1)}, u32[]{:S(2)}, u32[]{:S(2)}) collective-permute-start(bf16[256,768]{1,0:T(8,128)(2,1)S(1)} %collective-permute-done.10.refs_6_), channel_id=1, source_target_pairs={{0,1},{1,0},{2,3},{3,2},{4,5},{5,4},{6,7},{7,6},{8,9},{9,8},{10,11... | collective-permute-start | bytes 1179656 | tf_op jit(solution)/shard_map/ppermute | solution.py:31
  49.0 5.3 %copy-start.3 = (bf16[256,768]{1,0:T(8,128)(2,1)}, bf16[256,768]{1,0:T(8,128)(2,1)S(1)}, u32[]{:S(2)}) copy-start(bf16[256,768]{1,0:T(8,128)(2,1)S(1)} %collective-permute-done.6.refs_2_) | copy-start | bytes 1179652
  49.0 4.7 %collective-permute-start.7 = (bf16[256,768]{1,0:T(8,128)(2,1)S(1)}, bf16[256,768]{1,0:T(8,128)(2,1)}, u32[]{:S(2)}, u32[]{:S(2)}) collective-permute-start(bf16[256,768]{1,0:T(8,128)(2,1)S(1)} %collective-permute-done.6.refs_2_), channel_id=1, source_target_pairs={{0,1},{1,0},{2,3},{3,2},{4,5},{5,4},{6,7},{7,6},{8,9},{9,8},{10,11... | collective-permute-start | bytes 1179656 | tf_op jit(solution)/shard_map/ppermute | solution.py:31
  52.2 2.1 %copy-start.4 = (bf16[256,768]{1,0:T(8,128)(2,1)}, bf16[256,768]{1,0:T(8,128)(2,1)S(1)}, u32[]{:S(2)}) copy-start(bf16[256,768]{1,0:T(8,128)(2,1)S(1)} %collective-permute-done.8.refs_4_) | copy-start | bytes 1179652
  52.2 2.0 %collective-permute-start.9 = (bf16[256,768]{1,0:T(8,128)(2,1)S(1)}, bf16[256,768]{1,0:T(8,128)(2,1)}, u32[]{:S(2)}, u32[]{:S(2)}) collective-permute-start(bf16[256,768]{1,0:T(8,128)(2,1)S(1)} %collective-permute-done.8.refs_4_), channel_id=1, source_target_pairs={{0,1},{1,0},{2,3},{3,2},{4,5},{5,4},{6,7},{7,6},{8,9},{9,8},{10,11... | collective-permute-start | bytes 1179656 | tf_op jit(solution)/shard_map/ppermute | solution.py:31
  53.4 0.9 copy-start.5
  53.4 0.9 copy-start.6
  54.3 12.1 %copy-start.9 = (bf16[512,224]{0,1:T(8,128)(2,1)S(1)}, bf16[512,224]{0,1:T(8,128)(2,1)}, u32[]{:S(2)}) copy-start(bf16[512,224]{0,1:T(8,128)(2,1)} %param.20) | copy-start | bytes 688132
  54.3 12.5 %copy-start.10 = (bf16[512,224]{0,1:T(8,128)(2,1)S(1)}, bf16[512,224]{0,1:T(8,128)(2,1)}, u32[]{:S(2)}) copy-start(bf16[512,224]{0,1:T(8,128)(2,1)} %param.19) | copy-start | bytes 688132
  65.9 7.4 %copy-start.8 = (bf16[32,48,128]{2,1,0:T(8,128)(2,1)S(1)}, bf16[32,48,128]{2,1,0:T(8,128)(2,1)}, u32[]{:S(2)}) copy-start(bf16[32,48,128]{2,1,0:T(8,128)(2,1)} %get-tuple-element.34) | copy-start | bytes 1179652
  65.9 24.2 %copy-start.7 = (bf16[32,48,128]{2,1,0:T(8,128)(2,1)S(1)}, bf16[32,48,128]{2,1,0:T(8,128)(2,1)}, u32[]{:S(2)}) copy-start(bf16[32,48,128]{2,1,0:T(8,128)(2,1)} %get-tuple-element.28) | copy-start | bytes 1179652
  65.9 2.0 %collective-permute-start.13 = (bf16[32,48,128]{2,1,0:T(8,128)(2,1)}, bf16[32,48,128]{2,1,0:T(8,128)(2,1)S(1)}, u32[]{:S(2)}, u32[]{:S(2)}) collective-permute-start(bf16[32,48,128]{2,1,0:T(8,128)(2,1)} %get-tuple-element.31), channel_id=1, source_target_pairs={{0,1},{1,0},{2,3},{3,2},{4,5},{5,4},{6,7},{7,6},{8,9},{9,8},{10,11... | collective-permute-start | bytes 1179656 | tf_op jit(solution)/shard_map/ppermute | solution.py:31
  66.6 4.6 %collective-permute-start.15 = (bf16[32,48,128]{2,1,0:T(8,128)(2,1)}, bf16[32,48,128]{2,1,0:T(8,128)(2,1)S(1)}, u32[]{:S(2)}, u32[]{:S(2)}) collective-permute-start(bf16[32,48,128]{2,1,0:T(8,128)(2,1)} %get-tuple-element.33), channel_id=1, source_target_pairs={{0,1},{1,0},{2,3},{3,2},{4,5},{5,4},{6,7},{7,6},{8,9},{9,8},{10,11... | collective-permute-start | bytes 1179656 | tf_op jit(solution)/shard_map/ppermute | solution.py:31
  67.1 6.1 %collective-permute-start.17 = (bf16[32,48,128]{2,1,0:T(8,128)(2,1)}, bf16[32,48,128]{2,1,0:T(8,128)(2,1)S(1)}, u32[]{:S(2)}, u32[]{:S(2)}) collective-permute-start(bf16[32,48,128]{2,1,0:T(8,128)(2,1)} %get-tuple-element.35), channel_id=1, source_target_pairs={{0,1},{1,0},{2,3},{3,2},{4,5},{5,4},{6,7},{7,6},{8,9},{9,8},{10,11... | collective-permute-start | bytes 1179656 | tf_op jit(solution)/shard_map/ppermute | solution.py:31
  67.5 10.4 %collective-permute-start.12 = (bf16[32,48,128]{2,1,0:T(8,128)(2,1)}, bf16[32,48,128]{2,1,0:T(8,128)(2,1)S(1)}, u32[]{:S(2)}, u32[]{:S(2)}) collective-permute-start(bf16[32,48,128]{2,1,0:T(8,128)(2,1)} %get-tuple-element.29), channel_id=1, source_target_pairs={{0,1},{1,0},{2,3},{3,2},{4,5},{5,4},{6,7},{7,6},{8,9},{9,8},{10,11... | collective-permute-start | bytes 1179656 | tf_op jit(solution)/shard_map/ppermute | solution.py:31
  69.0 12.0 %collective-permute-start.14 = (bf16[32,48,128]{2,1,0:T(8,128)(2,1)S(1)}, bf16[32,48,128]{2,1,0:T(8,128)(2,1)S(1)}, u32[]{:S(2)}, u32[]{:S(2)}) collective-permute-start(bf16[32,48,128]{2,1,0:T(8,128)(2,1)S(1)} %add_convert_fusion.3), channel_id=1, source_target_pairs={{0,4},{2,6},{4,0},{6,2},{1,5},{3,7},{5,1},{7,3},{8,12},{10,14},{12... | collective-permute-start | bytes 1179656 | tf_op jit(solution)/shard_map/ppermute | solution.py:35
  72.3 17.7 %collective-permute-start.16 = (bf16[32,48,128]{2,1,0:T(8,128)(2,1)S(1)}, bf16[32,48,128]{2,1,0:T(8,128)(2,1)S(1)}, u32[]{:S(2)}, u32[]{:S(2)}) collective-permute-start(bf16[32,48,128]{2,1,0:T(8,128)(2,1)S(1)} %add_convert_fusion.2), channel_id=1, source_target_pairs={{0,2},{2,4},{4,6},{6,0},{1,3},{3,5},{5,7},{7,1},{8,10},{10,12},{12... | collective-permute-start | bytes 1179656 | tf_op jit(solution)/shard_map/ppermute | solution.py:35
  73.3 16.7 %collective-permute-start.18 = (bf16[32,48,128]{2,1,0:T(8,128)(2,1)S(1)}, bf16[32,48,128]{2,1,0:T(8,128)(2,1)S(1)}, u32[]{:S(2)}, u32[]{:S(2)}) collective-permute-start(bf16[32,48,128]{2,1,0:T(8,128)(2,1)S(1)} %add_convert_fusion.1), channel_id=1, source_target_pairs={{0,6},{2,0},{4,2},{6,4},{1,7},{3,1},{5,3},{7,5},{8,14},{10,8},{12,... | collective-permute-start | bytes 1179656 | tf_op jit(solution)/shard_map/ppermute | solution.py:35
  75.4 2.3 %collective-permute-start = (bf16[128,448]{1,0:T(8,128)(2,1)S(1)}, bf16[128,448]{1,0:T(8,128)(2,1)S(1)}, u32[]{:S(2)}, u32[]{:S(2)}) collective-permute-start(bf16[128,448]{1,0:T(8,128)(2,1)S(1)} %select_convert_fusion), channel_id=1, source_target_pairs={{0,1},{1,0},{2,3},{3,2},{4,5},{5,4},{6,7},{7,6},{8,9},{9,8},{10,11... | collective-permute-start | bytes 344072 | tf_op jit(solution)/shard_map/ppermute | solution.py:31
  77.9 21.6 %collective-permute-start.1 = (bf16[128,448]{1,0:T(8,128)(2,1)S(1)}, bf16[128,448]{1,0:T(8,128)(2,1)S(1)}, u32[]{:S(2)}, u32[]{:S(2)}) collective-permute-start(bf16[128,448]{1,0:T(8,128)(2,1)S(1)} %add_convert_fusion.6), channel_id=1, source_target_pairs={{0,2},{2,4},{4,6},{6,0},{1,3},{3,5},{5,7},{7,1},{8,10},{10,12},{12... | collective-permute-start | bytes 344072 | tf_op jit(solution)/shard_map/ppermute | solution.py:35
  78.0 21.5 %collective-permute-start.2 = (bf16[128,448]{1,0:T(8,128)(2,1)S(1)}, bf16[128,448]{1,0:T(8,128)(2,1)S(1)}, u32[]{:S(2)}, u32[]{:S(2)}) collective-permute-start(bf16[128,448]{1,0:T(8,128)(2,1)S(1)} %add_convert_fusion.6), channel_id=1, source_target_pairs={{0,4},{2,6},{4,0},{6,2},{1,5},{3,7},{5,1},{7,3},{8,12},{10,14},{12... | collective-permute-start | bytes 344072 | tf_op jit(solution)/shard_map/ppermute | solution.py:35
  81.0 18.6 %collective-permute-start.3 = (bf16[128,448]{1,0:T(8,128)(2,1)S(1)}, bf16[128,448]{1,0:T(8,128)(2,1)S(1)}, u32[]{:S(2)}, u32[]{:S(2)}) collective-permute-start(bf16[128,448]{1,0:T(8,128)(2,1)S(1)} %add_convert_fusion.6), channel_id=1, source_target_pairs={{0,6},{2,0},{4,2},{6,4},{1,7},{3,1},{5,3},{7,5},{8,14},{10,8},{12,... | collective-permute-start | bytes 344072 | tf_op jit(solution)/shard_map/ppermute | solution.py:35
  91.1 19.2 %all-to-all-start.1 = ((bf16[32,48,128]{2,1,0:T(8,128)(2,1)}), bf16[32,48,128]{2,1,0:T(8,128)(2,1)S(1)}, u32[]{:S(2)}, u32[]{:S(2)}) async-start(bf16[32,48,128]{2,1,0:T(8,128)(2,1)} %add_convert_fusion), calls=%async_computation.1 | async-start | bytes 786432 | tf_op jit(solution)/shard_map/all_to_all | solution.py:23
  99.6 39.3 %copy-start.11 = (bf16[8,512]{1,0:T(8,128)(2,1)S(1)}, bf16[8,512]{1,0:T(8,128)(2,1)}, u32[]{:S(2)}) copy-start(bf16[8,512]{1,0:T(8,128)(2,1)} %student.1) | copy-start | bytes 24580
  99.6 2.6 %collective-permute-start.4 = (bf16[128,448]{1,0:T(8,128)(2,1)S(1)}, bf16[128,448]{1,0:T(8,128)(2,1)S(1)}, u32[]{:S(2)}, u32[]{:S(2)}) collective-permute-start(bf16[128,448]{1,0:T(8,128)(2,1)S(1)} %add_convert_fusion.5), channel_id=1, source_target_pairs={{0,1},{1,0},{2,3},{3,2},{4,5},{5,4},{6,7},{7,6},{8,9},{9,8},{10,11... | collective-permute-start | bytes 344072 | tf_op jit(solution)/shard_map/ppermute | solution.py:31
  110.3 5.5 %collective-permute-start.19 = (bf16[48,128]{1,0:T(8,128)(2,1)S(1)}, bf16[48,128]{1,0:T(8,128)(2,1)S(1)}, u32[]{:S(2)}, u32[]{:S(2)}) collective-permute-start(bf16[48,128]{1,0:T(8,128)(2,1)S(1)} %reduce_sum.21), channel_id=1, source_target_pairs={{0,2},{2,4},{4,6},{6,0},{1,3},{3,5},{5,7},{7,1},{8,10},{10,12},{12... | collective-permute-start | bytes 36872 | tf_op jit(solution)/shard_map/ppermute | solution.py:35
  113.1 4.0 %collective-permute-start.20 = (bf16[48,128]{1,0:T(8,128)(2,1)S(1)}, bf16[48,128]{1,0:T(8,128)(2,1)S(1)}, u32[]{:S(2)}, u32[]{:S(2)}) collective-permute-start(bf16[48,128]{1,0:T(8,128)(2,1)S(1)} %reduce_sum.21), channel_id=1, source_target_pairs={{0,4},{2,6},{4,0},{6,2},{1,5},{3,7},{5,1},{7,3},{8,12},{10,14},{12... | collective-permute-start | bytes 36872 | tf_op jit(solution)/shard_map/ppermute | solution.py:35
  115.0 2.5 %collective-permute-start.21 = (bf16[48,128]{1,0:T(8,128)(2,1)S(1)}, bf16[48,128]{1,0:T(8,128)(2,1)S(1)}, u32[]{:S(2)}, u32[]{:S(2)}) collective-permute-start(bf16[48,128]{1,0:T(8,128)(2,1)S(1)} %reduce_sum.21), channel_id=1, source_target_pairs={{0,6},{2,0},{4,2},{6,4},{1,7},{3,1},{5,3},{7,5},{8,14},{10,8},{12,... | collective-permute-start | bytes 36872 | tf_op jit(solution)/shard_map/ppermute | solution.py:35
  117.6 6.7 %collective-permute-start.22 = (bf16[192,128]{1,0:T(8,128)(2,1)S(1)}, bf16[192,128]{1,0:T(8,128)(2,1)S(1)}, u32[]{:S(2)}, u32[]{:S(2)}) collective-permute-start(bf16[192,128]{1,0:T(8,128)(2,1)S(1)} %pad_maximum_fusion.1), channel_id=1, source_target_pairs={{0,1},{1,0},{2,3},{3,2},{4,5},{5,4},{6,7},{7,6},{8,9},{9,8},{10,11... | collective-permute-start | bytes 147464 | tf_op jit(solution)/shard_map/ppermute | solution.py:31
  156.0 4.6 %collective-permute-start.23 = (bf16[128,224]{1,0:T(8,128)(2,1)S(1)}, bf16[128,224]{1,0:T(8,128)(2,1)S(1)}, u32[]{:S(2)}, u32[]{:S(2)}) collective-permute-start(bf16[128,224]{1,0:T(8,128)(2,1)S(1)} %select_convert_fusion.1), channel_id=1, source_target_pairs={{0,1},{1,0},{2,3},{3,2},{4,5},{5,4},{6,7},{7,6},{8,9},{9,8},{10,11... | collective-permute-start | bytes 172040 | tf_op jit(solution)/shard_map/ppermute | solution.py:31
  160.7 4.6 %collective-permute-start.24 = (bf16[128,224]{1,0:T(8,128)(2,1)S(1)}, bf16[128,224]{1,0:T(8,128)(2,1)S(1)}, u32[]{:S(2)}, u32[]{:S(2)}) collective-permute-start(bf16[128,224]{1,0:T(8,128)(2,1)S(1)} %add_convert_fusion.8), channel_id=1, source_target_pairs={{0,2},{2,4},{4,6},{6,0},{1,3},{3,5},{5,7},{7,1},{8,10},{10,12},{12... | collective-permute-start | bytes 172040 | tf_op jit(solution)/shard_map/ppermute | solution.py:35
  161.0 5.6 %collective-permute-start.25 = (bf16[128,224]{1,0:T(8,128)(2,1)S(1)}, bf16[128,224]{1,0:T(8,128)(2,1)S(1)}, u32[]{:S(2)}, u32[]{:S(2)}) collective-permute-start(bf16[128,224]{1,0:T(8,128)(2,1)S(1)} %add_convert_fusion.8), channel_id=1, source_target_pairs={{0,4},{2,6},{4,0},{6,2},{1,5},{3,7},{5,1},{7,3},{8,12},{10,14},{12... | collective-permute-start | bytes 172040 | tf_op jit(solution)/shard_map/ppermute | solution.py:35
  163.6 3.9 %collective-permute-start.26 = (bf16[128,224]{1,0:T(8,128)(2,1)S(1)}, bf16[128,224]{1,0:T(8,128)(2,1)S(1)}, u32[]{:S(2)}, u32[]{:S(2)}) collective-permute-start(bf16[128,224]{1,0:T(8,128)(2,1)S(1)} %add_convert_fusion.8), channel_id=1, source_target_pairs={{0,6},{2,0},{4,2},{6,4},{1,7},{3,1},{5,3},{7,5},{8,14},{10,8},{12,... | collective-permute-start | bytes 172040 | tf_op jit(solution)/shard_map/ppermute | solution.py:35
  167.6 2.3 %collective-permute-start.27 = (bf16[128,224]{1,0:T(8,128)(2,1)S(1)}, bf16[128,224]{1,0:T(8,128)(2,1)S(1)}, u32[]{:S(2)}, u32[]{:S(2)}) collective-permute-start(bf16[128,224]{1,0:T(8,128)(2,1)S(1)} %add_convert_fusion.7.own), channel_id=1, source_target_pairs={{0,1},{1,0},{2,3},{3,2},{4,5},{5,4},{6,7},{7,6},{8,9},{9,8},{10,11... | collective-permute-start | bytes 172040 | tf_op jit(solution)/shard_map/ppermute | solution.py:31
